TPU v7x, 256 devices: a whole 4x4x8 slice. The times are simulated.
256 devices in a mesh: sens: 32 (over x_lo, z, core), cand: 8 (over x_hi, y).
Axes of the slice: x: 4 (x_hi: 2, x_lo: 2; x = x_hi * 2 + x_lo), y: 4, z: 8, core: 2. Of those that a mesh axis runs over, the one named last changes fastest.
Arguments:
- jacobian: bfloat16 [8192, 131072], P('sens', 'cand'), may hold values from -0.015625 to 0.015625
- weights: float32 [2, 8192], P(None, 'sens'), may hold values from 1 to 10
- blocks: float32 [2, 16, 131072], P(None, None, 'cand'), may hold values from -6 to 6
Outputs:
- curvature: float32 [2, 16, 131072], P(None, None, 'cand')
All inputs are finite; a program needn't handle non-finite values.
Results may differ from a plain program's by a relative error of at most 0.004.
Values sent between devices are 32-bit elements; how exact they have to be, the bound alone decides.
No kernel may reach another device: no remote copies, remote signals or barrier semaphores. Data moves between devices by JAX's collectives and lax.ppermute only.
A program may use at most 64 MiB of HBM per device.

v0:
```python
import jax
import jax.numpy as jnp
from jax import lax
from jax.sharding import PartitionSpec as P


def column_sum(partial_terms):
    return lax.psum(partial_terms, "sens")


def curvature_pass(directions, row_weights, jacobian):
    predicted = jnp.einsum("pkc,rc->pkr", directions, jacobian, preferred_element_type=jnp.float32)
    predicted = lax.psum(predicted, "cand")
    weighted = (row_weights[:, None, :] * predicted).astype(jnp.bfloat16)
    partial_terms = jnp.einsum(
        "pkr,rc->pkc", weighted, jacobian, preferred_element_type=jnp.float32
    )
    return column_sum(partial_terms)


def local(jacobian, weights, blocks):
    directions = blocks.astype(jnp.bfloat16)
    return curvature_pass(directions, weights, jacobian)


def solution(mesh):
    return jax.shard_map(
        local,
        mesh=mesh,
        in_specs=(P("sens", "cand"), P(None, "sens"), P(None, None, "cand")),
        out_specs=P(None, None, "cand"),
        check_vma=False,
    )
```

profile of v0, /device:TPU:1, one launch (start us, length us, event | category | flops | bytes accessed | tf_op | source)
XLA Modules:
  0.0 298.8 jit_solution(4202867976009979084)
XLA Ops:
  6.5 0.0 copy-start
  6.5 0.0 all-reduce.2.cloned.1.call-start
  6.5 6.6 %fusion.2 = f32[2,16,256]{2,1,0:T(8,128)S(1)} fusion(bf16[256,16384]{1,0:T(8,128)(2,1)} %param.3, f32[2,16,16384]{2,1,0:T(8,128)} %param.5), kind=kOutput, calls=%fused_computation.2 | convolution fusion | flops 268959744 | bytes 10518528 | tf_op jit(solution)/shard_map/pkc,rc->pkr/dot_general | solution.py:12
  13.2 35.6 %psum.14 = f32[2,16,256]{2,1,0:T(8,128)S(1)} all-reduce(f32[2,16,256]{2,1,0:T(8,128)S(1)} %fusion.2), channel_id=1, replica_groups=mesh['sens'=32,'cand'=8] {'cand'}, use_global_device_ids=true, to_apply=%region_0.0 | all-reduce | flops 8192 | bytes 65536 | tf_op jit(solution)/shard_map/psum | solution.py:13
  48.8 0.0 copy-done
  48.8 6.2 %fusion = f32[2,16,16384]{2,1,0:T(8,128)} fusion(bf16[256,16384]{1,0:T(8,128)(2,1)} %param.3, f32[2,16,256]{2,1,0:T(8,128)S(1)} %psum.14, f32[2,256]{1,0:T(2,128)S(1)} %copy-done), kind=kOutput, calls=%fused_computation | convolution fusion | flops 268451840 | bytes 10520576 | tf_op jit(solution)/shard_map/pkr,rc->pkc/dot_general | solution.py:15
  55.1 0.0 all-reduce.2.cloned.1.call-update
  55.1 233.8 %all-reduce.2.cloned.1.call-done = f32[2,16,16384]{2,1,0:T(8,128)} async-done(((f32[2,16,16384]{2,1,0:T(8,128)}), f32[2,16,16384]{2,1,0:T(8,128)}) %all-reduce.2.cloned.1.call-update) | async-done | bytes 2097168 | tf_op jit(solution)/shard_map/psum | solution.py:8
  288.9 3.0 %copy.5 = f32[2,16,16384]{2,1,0:T(8,128)} copy(f32[2,16,16384]{2,1,0:T(8,128)} %all-reduce.2.cloned.1.call-done) | data formatting | bytes 4194304
Async XLA Ops:
  6.5 42.3 %copy-start = (f32[2,256]{1,0:T(2,128)S(1)}, f32[2,256]{1,0:T(2,128)}, u32[]{:S(2)}) copy-start(f32[2,256]{1,0:T(2,128)} %param.4) | copy-start | bytes 6148
  6.5 282.3 %all-reduce.2.cloned.1.call-start = ((), (), s32[]{:S(2)}) async-start(), calls=%async_computation | async-start | bytes 4194304 | tf_op jit(solution)/shard_map/psum | solution.py:8
Sparse Core Ops, SparseCore 0:
  55.2 233.6 all-reduce.1
where the time goes:
time: 299 us
  waiting for transfers between devices  234 us (78%)
  blocking collectives  35.6 us (12%)
  between operations  13.4 us (4%)
  matrix products  12.9 us (4%)
  local copies, waits for them, and re-layouts  3.05 us (1%)
    psum x1, waiting for transfers between devices, column_sum(): return lax.psum(partial_terms, 'sens')  234 us
    psum x1, blocking collectives, curvature_pass(): predicted = lax.psum(predicted, 'cand')  35.6 us
    dot_general x1, matrix products, curvature_pass(): jnp.einsum('pkc,rc->pkr', directions, jacobian, preferred_element_type=jn...  6.64 us
    dot_general x1, matrix products, curvature_pass(): jnp.einsum('pkr,rc->pkc', weighted, jacobian, preferred_element_type=jnp....  6.25 us
  transfers between devices with their start and end apart: 1, of which 1 were waited for; matrix products, arithmetic and copies ran while one was open for 0% of the time, Pallas kernels for 0%

commit v1 on v0

v1 whole, which is shorter than its diff:
```python
import functools

import jax
import jax.numpy as jnp
from jax import lax
from jax.experimental import pallas as pl
from jax.experimental.pallas import tpu as pltpu
from jax.sharding import PartitionSpec as P

N_XL, N_Z, N_CORE = 2, 8, 2
N_SENS = N_XL * N_Z * N_CORE
N_XH, N_Y = 2, 4
N_CAND = N_XH * N_Y
PIECES = 2
MIB = 1 << 20


def sens_id(xl, z, core):
    return (xl * N_Z + z) * N_CORE + core


def sens_perm(move):
    pairs = []
    for xl in range(N_XL):
        for z in range(N_Z):
            for core in range(N_CORE):
                pairs.append((sens_id(xl, z, core), sens_id(*move(xl, z, core))))
    return pairs


CORE_SWAP = sens_perm(lambda xl, z, core: (xl, z, 1 - core))
X_SWAP = sens_perm(lambda xl, z, core: (1 - xl, z, core))
Z_SHIFT = [sens_perm(lambda xl, z, core, k=k: (xl, (z + k) % N_Z, core)) for k in range(N_Z)]
CAND_SHIFT = [
    [
        (xh * N_Y + y, ((xh + a) % N_XH) * N_Y + (y + b) % N_Y)
        for xh in range(N_XH)
        for y in range(N_Y)
    ]
    for a in range(N_XH)
    for b in range(N_Y)
]


def predict_kernel(blocks_ref, jac_ref, out_ref):
    @pl.when(pl.program_id(0) == 0)
    def _():
        out_ref[...] = jnp.zeros_like(out_ref)

    directions = blocks_ref[...].astype(jnp.bfloat16)
    out_ref[...] += lax.dot_general(
        directions, jac_ref[...], (((1,), (1,)), ((), ())), preferred_element_type=jnp.float32
    )


def predict(blocks, jacobian):
    k, ncols = blocks.shape
    rows = jacobian.shape[0]
    width = 2048
    return pl.pallas_call(
        predict_kernel,
        grid=(ncols // width,),
        in_specs=[
            pl.BlockSpec((k, width), lambda i: (0, i)),
            pl.BlockSpec((rows, width), lambda i: (0, i)),
        ],
        out_specs=pl.BlockSpec((k, rows), lambda i: (0, 0)),
        out_shape=jax.ShapeDtypeStruct((k, rows), jnp.float32),
        compiler_params=pltpu.CompilerParams(vmem_limit_bytes=16 * MIB),
        cost_estimate=pl.CostEstimate(
            flops=2 * k * ncols * rows, bytes_accessed=2 * rows * ncols, transcendentals=0
        ),
    )(blocks, jacobian)


def weigh_kernel(weights_ref, *refs):
    parts, out_ref = refs[:-1], refs[-1]
    total = parts[0][...]
    for part in parts[1:]:
        total = total + part[...]
    half = total.shape[0] // 2
    for p in range(2):
        rows = pl.ds(p * half, half)
        out_ref[rows, :] = (
            weights_ref[p : p + 1, :] * total[p * half : (p + 1) * half]
        ).astype(jnp.bfloat16)


def weigh(weights, parts):
    return pl.pallas_call(
        weigh_kernel,
        out_shape=jax.ShapeDtypeStruct(parts[0].shape, jnp.bfloat16),
        compiler_params=pltpu.CompilerParams(vmem_limit_bytes=4 * MIB),
    )(weights, *parts)


def product_kernel(where_ref, weighted_ref, jac_ref, sibling_ref, across_ref, mine_ref):
    step = pl.program_id(0)
    z = where_ref[2]
    chunk = mine_ref.shape[-1]

    def fill(dst):
        for zz in range(N_Z):
            dst[lax.rem(zz + N_Z - z, N_Z)] = jnp.dot(
                weighted_ref[...],
                jac_ref[:, zz * chunk : (zz + 1) * chunk],
                preferred_element_type=jnp.float32,
            )

    @pl.when(step < 2)
    def _():
        fill(sibling_ref.at[step])

    @pl.when(step == 2)
    def _():
        fill(across_ref)

    @pl.when(step == 3)
    def _():
        fill(mine_ref)


def product(where, weighted, jacobian, piece):
    k, rows = weighted.shape
    ncols = jacobian.shape[1]
    chunk = ncols // (PIECES * N_SENS)

    def jac_map(i, where_ref):
        core, xl = where_ref[0], where_ref[1]
        core = jnp.where(i < 2, 1 - core, core)
        xl = jnp.where((i == 0) | (i == 3), xl, 1 - xl)
        return 0, piece * 4 + core * 2 + xl

    vmem = pl.BlockSpec(memory_space=pltpu.VMEM)
    f32 = jnp.float32
    return pl.pallas_call(
        product_kernel,
        grid_spec=pltpu.PrefetchScalarGridSpec(
            num_scalar_prefetch=1,
            grid=(4,),
            in_specs=[vmem, pl.BlockSpec((rows, N_Z * chunk), jac_map)],
            out_specs=[vmem, vmem, vmem],
        ),
        out_shape=[
            jax.ShapeDtypeStruct((2, N_Z, k, chunk), f32),
            jax.ShapeDtypeStruct((N_Z, k, chunk), f32),
            jax.ShapeDtypeStruct((N_Z, k, chunk), f32),
        ],
        compiler_params=pltpu.CompilerParams(vmem_limit_bytes=16 * MIB),
        cost_estimate=pl.CostEstimate(
            flops=2 * k * ncols * rows // PIECES,
            bytes_accessed=2 * rows * ncols // PIECES,
            transcendentals=0,
        ),
    )(where, weighted, jacobian)


def assemble_kernel(where_ref, *refs):
    out_ref = refs[-1]
    core, xl, z = where_ref[0], where_ref[1], where_ref[2]
    chunk = refs[0].shape[-1]
    for piece in range(PIECES):
        own_mine, own_across, sib = refs[3 * piece : 3 * piece + 3]
        for j in range(N_Z):
            zz = lax.rem(z + N_Z - j, N_Z)
            for c, x, value in (
                (core, xl, own_mine[j]),
                (core, 1 - xl, own_across[j]),
                (1 - core, xl, sib[0, j]),
                (1 - core, 1 - xl, sib[1, j]),
            ):
                at = ((piece * 4 + c * 2 + x) * N_Z + zz) * chunk
                out_ref[:, pl.ds(pl.multiple_of(at, chunk), chunk)] = value


def assemble(where, parts, ncols):
    k = parts[0].shape[1]
    vmem = pl.BlockSpec(memory_space=pltpu.VMEM)
    return pl.pallas_call(
        assemble_kernel,
        in_specs=[pl.BlockSpec(memory_space=pltpu.SMEM)] + [vmem] * len(parts),
        out_specs=vmem,
        out_shape=jax.ShapeDtypeStruct((k, ncols), jnp.float32),
        compiler_params=pltpu.CompilerParams(vmem_limit_bytes=16 * MIB),
    )(where, *parts)


def local(jacobian, weights, blocks):
    p, k, ncols = blocks.shape
    me = lax.axis_index("sens")
    where = jnp.stack([me % N_CORE, me // (N_CORE * N_Z), (me // N_CORE) % N_Z]).astype(jnp.int32)

    predicted = predict(blocks.reshape(p * k, ncols), jacobian)
    parts = [predicted] + [lax.ppermute(predicted, "cand", perm) for perm in CAND_SHIFT[1:]]
    weighted = weigh(weights, parts)

    gathered = []
    for piece in range(PIECES):
        to_sibling, to_across, mine = product(where, weighted, jacobian, piece)
        from_sibling = lax.ppermute(to_sibling, "sens", CORE_SWAP)
        from_across = lax.ppermute(to_across + from_sibling[1], "sens", X_SWAP)
        own = mine + from_sibling[0] + from_across
        total = own[0]
        for shift in range(1, N_Z):
            total = total + lax.ppermute(own[shift], "sens", Z_SHIFT[shift])
        column = jnp.stack(
            [total] + [lax.ppermute(total, "sens", Z_SHIFT[shift]) for shift in range(1, N_Z)]
        )
        across = lax.ppermute(column, "sens", X_SWAP)
        sibling = lax.ppermute(jnp.stack([column, across]), "sens", CORE_SWAP)
        gathered += [column, across, sibling]
    return assemble(where, gathered, ncols).reshape(p, k, ncols)


def solution(mesh):
    return jax.shard_map(
        local,
        mesh=mesh,
        in_specs=(P("sens", "cand"), P(None, "sens"), P(None, None, "cand")),
        out_specs=P(None, None, "cand"),
        check_vma=False,
    )
```

time: 299 us -> 135 us (0.45)
  waiting for transfers between devices: 234 us -> 27 us
  starting transfers between devices: 0.01 us -> 89 us
  blocking collectives: 35.6 us -> 0 us
  between operations: 13.4 us -> 0.21 us
  matrix products: 12.9 us -> 0 us
  Pallas kernels: 0 us -> 10.3 us
  local copies, waits for them, and re-layouts: 3.05 us -> 8.44 us
    psum x1 -> x0, waiting for transfers between devices: 234 us -> none  [column_sum(): return lax.psum(partial_terms, 'sens')]
    ppermute x0 -> x43, starting transfers between devices: none -> 89 us  [the longest x14 28.1 us: local(): total = total + lax.ppermute(own[shift], 'sens', Z_SHIFT[shift])]
    psum x1 -> x0, blocking collectives: 35.6 us -> none  [curvature_pass(): predicted = lax.psum(predicted, 'cand')]
    ppermute x0 -> x43, waiting for transfers between devices: none -> 27 us  [the longest x14 15 us: local(): lax.ppermute(total, 'sens', Z_SHIFT[shift])]
    dot_general x2 -> x0, matrix products: 12.9 us -> none  [the longest x1 6.64 us: curvature_pass(): jnp.einsum('pkc,rc->pkr', directions, jacobian, preferred_element_type=jn...]
    pallas_call x0 -> x5, Pallas kernels: none -> 10.3 us  [the longest x1 4.12 us: predict(): pl.pallas_call(predict_kernel, grid=(ncols // width,), in_specs=[pl.Block...]
    unnamed x3 -> x20, local copies, waits for them, and re-layouts: 3.05 us -> 8.4 us
  transfers between devices with their start and end apart: 1 -> 43, of which waited for: 1 -> 12; matrix products, arithmetic and copies ran while one was open for 0% -> 0% of each run, Pallas kernels for 0% -> 1%
where the time goes in v1:
time: 135 us
  starting transfers between devices  89 us (66%)
  waiting for transfers between devices  27 us (20%)
  Pallas kernels  10.3 us (8%)
  local copies, waits for them, and re-layouts  8.44 us (6%)
    ppermute x14, starting transfers between devices, local(): total = total + lax.ppermute(own[shift], 'sens', Z_SHIFT[shift])  28.1 us
    ppermute x14, starting transfers between devices, local(): lax.ppermute(total, 'sens', Z_SHIFT[shift])  22.1 us
    ppermute x2, starting transfers between devices, local(): sibling = lax.ppermute(jnp.stack([column, across]), 'sens', CORE_SWAP)  16.7 us
    ppermute x14, waiting for transfers between devices, local(): lax.ppermute(total, 'sens', Z_SHIFT[shift])  15 us
    ppermute x7, starting transfers between devices, local(): lax.ppermute(predicted, 'cand', perm)  13.2 us
    unnamed x20, local copies, waits for them, and re-layouts  8.4 us
    ppermute x2, waiting for transfers between devices, local(): from_across = lax.ppermute(to_across + from_sibling[1], 'sens', X_SWAP)  4.3 us
    pallas_call x1, Pallas kernels, predict(): pl.pallas_call(predict_kernel, grid=(ncols // width,), in_specs=[pl.Block...  4.12 us
  transfers between devices with their start and end apart: 43, of which 12 were waited for; matrix products, arithmetic and copies ran while one was open for 0% of the time, Pallas kernels for 1%

profile of v1, /device:TPU:1, one launch (start us, length us, event | category | flops | bytes accessed | tf_op | source)
XLA Modules:
  0.0 135.2 jit_solution(10146751111845330889)
XLA Ops:
  0.0 3.4 %copy-done = bf16[256,16384]{1,0:T(8,128)(2,1)S(1)} copy-done((bf16[256,16384]{1,0:T(8,128)(2,1)S(1)}, bf16[256,16384]{1,0:T(8,128)(2,1)}, u32[]{:S(2)}) %copy-start) | copy-done | bytes 8388632
  5.0 4.1 %shard_map.37.refs_0_ = f32[32,256]{1,0:T(8,128)S(1)} custom-call(f32[32,16384]{1,0:T(8,128)S(1)} %bitcast.123, bf16[256,16384]{1,0:T(8,128)(2,1)S(1)} %copy-done), custom_call_target="tpu_custom_call" | custom-call | flops 268435456 | bytes 8388608 | tf_op jit(solution)/shard_map/pallas_call | solution.py:60
  9.1 6.1 %collective-permute-start.6 = (f32[32,256]{1,0:T(8,128)S(1)}, f32[32,256]{1,0:T(8,128)S(1)}, u32[]{:S(2)}, u32[]{:S(2)}) collective-permute-start(f32[32,256]{1,0:T(8,128)S(1)} %shard_map.37.refs_0_), channel_id=1, source_target_pairs={{0,7},{1,4},{2,5},{3,6},{4,3},{5,0},{6,1},{7,2},{8,15},{9,12},{10,... | collective-permute-start | bytes 98312 | tf_op jit(solution)/shard_map/ppermute | solution.py:194
  15.5 3.1 %collective-permute-start.4 = (f32[32,256]{1,0:T(8,128)S(1)}, f32[32,256]{1,0:T(8,128)S(1)}, u32[]{:S(2)}, u32[]{:S(2)}) collective-permute-start(f32[32,256]{1,0:T(8,128)S(1)} %shard_map.37.refs_0_), channel_id=1, source_target_pairs={{0,5},{1,6},{2,7},{3,4},{4,1},{5,2},{6,3},{7,0},{8,13},{9,14},{10,... | collective-permute-start | bytes 98312 | tf_op jit(solution)/shard_map/ppermute | solution.py:194
  26.3 3.4 %copy-done.1 = bf16[256,16384]{1,0:T(8,128)(2,1)S(1)} copy-done((bf16[256,16384]{1,0:T(8,128)(2,1)S(1)}, bf16[256,16384]{1,0:T(8,128)(2,1)}, u32[]{:S(2)}) %copy-start.1) | copy-done | bytes 8388632
  31.7 3.6 %collective-permute-start.25 = (f32[2,8,32,256]{3,2,1,0:T(8,128)S(1)}, f32[2,8,32,256]{3,2,1,0:T(8,128)S(1)}, u32[]{:S(2)}, u32[]{:S(2)}) collective-permute-start(f32[2,8,32,256]{3,2,1,0:T(8,128)S(1)} %get-tuple-element.15), channel_id=1, source_target_pairs={{0,8},{8,0},{16,24},{24,16},{32,40},{40,32},{48,56},{56,48},{64,72... | collective-permute-start | bytes 1572872 | tf_op jit(solution)/shard_map/ppermute | solution.py:200
  40.7 4.3 %collective-permute-done.26 = f32[8,32,256]{2,1,0:T(8,128)S(1)} collective-permute-done((f32[8,32,256]{2,1,0:T(8,128)S(1)}, f32[8,32,256]{2,1,0:T(8,128)S(1)}, u32[]{:S(2)}, u32[]{:S(2)}) %collective-permute-start.26) | collective-permute-done | bytes 262176 | tf_op jit(solution)/shard_map/ppermute | solution.py:201
  46.7 4.0 %collective-permute-start.33 = (f32[32,256]{1,0:T(8,128)S(1)}, f32[32,256]{1,0:T(8,128)S(1)}, u32[]{:S(2)}, u32[]{:S(2)}) collective-permute-start(f32[32,256]{1,0:T(8,128)S(1)} %get-tuple-element.22), channel_id=1, source_target_pairs={{0,112},{8,120},{16,0},{24,8},{32,16},{40,24},{48,32},{56,40},{64,... | collective-permute-start | bytes 98312 | tf_op jit(solution)/shard_map/ppermute | solution.py:205
  54.7 2.8 %collective-permute-start.30 = (f32[32,256]{1,0:T(8,128)S(1)}, f32[32,256]{1,0:T(8,128)S(1)}, u32[]{:S(2)}, u32[]{:S(2)}) collective-permute-start(f32[32,256]{1,0:T(8,128)S(1)} %get-tuple-element.25), channel_id=1, source_target_pairs={{0,64},{8,72},{16,80},{24,88},{32,96},{40,104},{48,112},{56,120},{... | collective-permute-start | bytes 98312 | tf_op jit(solution)/shard_map/ppermute | solution.py:205
  59.3 2.4 %collective-permute-start.28 = (f32[32,256]{1,0:T(8,128)S(1)}, f32[32,256]{1,0:T(8,128)S(1)}, u32[]{:S(2)}, u32[]{:S(2)}) collective-permute-start(f32[32,256]{1,0:T(8,128)S(1)} %get-tuple-element.27), channel_id=1, source_target_pairs={{0,32},{8,40},{16,48},{24,56},{32,64},{40,72},{48,80},{56,88},{64,... | collective-permute-start | bytes 98312 | tf_op jit(solution)/shard_map/ppermute | solution.py:205
  61.7 2.7 %collective-permute-start.15 = (f32[32,256]{1,0:T(8,128)S(1)}, f32[32,256]{1,0:T(8,128)S(1)}, u32[]{:S(2)}, u32[]{:S(2)}) collective-permute-start(f32[32,256]{1,0:T(8,128)S(1)} %get-tuple-element.29), channel_id=1, source_target_pairs={{0,112},{8,120},{16,0},{24,8},{32,16},{40,24},{48,32},{56,40},{64,... | collective-permute-start | bytes 98312 | tf_op jit(solution)/shard_map/ppermute | solution.py:205
  64.4 2.8 %collective-permute-start.13 = (f32[32,256]{1,0:T(8,128)S(1)}, f32[32,256]{1,0:T(8,128)S(1)}, u32[]{:S(2)}, u32[]{:S(2)}) collective-permute-start(f32[32,256]{1,0:T(8,128)S(1)} %get-tuple-element.31), channel_id=1, source_target_pairs={{0,80},{8,88},{16,96},{24,104},{32,112},{40,120},{48,0},{56,8},{64... | collective-permute-start | bytes 98312 | tf_op jit(solution)/shard_map/ppermute | solution.py:205
  67.2 2.6 %collective-permute-start.12 = (f32[32,256]{1,0:T(8,128)S(1)}, f32[32,256]{1,0:T(8,128)S(1)}, u32[]{:S(2)}, u32[]{:S(2)}) collective-permute-start(f32[32,256]{1,0:T(8,128)S(1)} %get-tuple-element.32), channel_id=1, source_target_pairs={{0,64},{8,72},{16,80},{24,88},{32,96},{40,104},{48,112},{56,120},{... | collective-permute-start | bytes 98312 | tf_op jit(solution)/shard_map/ppermute | solution.py:205
  70.3 3.0 %collective-permute-start.10 = (f32[32,256]{1,0:T(8,128)S(1)}, f32[32,256]{1,0:T(8,128)S(1)}, u32[]{:S(2)}, u32[]{:S(2)}) collective-permute-start(f32[32,256]{1,0:T(8,128)S(1)} %get-tuple-element.34), channel_id=1, source_target_pairs={{0,32},{8,40},{16,48},{24,56},{32,64},{40,72},{48,80},{56,88},{64,... | collective-permute-start | bytes 98312 | tf_op jit(solution)/shard_map/ppermute | solution.py:205
  74.7 3.4 %collective-permute-start.38 = (f32[32,256]{1,0:T(8,128)S(1)}, f32[32,256]{1,0:T(8,128)S(1)}, u32[]{:S(2)}, u32[]{:S(2)}) collective-permute-start(f32[32,256]{1,0:T(8,128)S(1)} %get-tuple-element.18), channel_id=1, source_target_pairs={{0,80},{8,88},{16,96},{24,104},{32,112},{40,120},{48,0},{56,8},{64... | collective-permute-start | bytes 98312 | tf_op jit(solution)/shard_map/ppermute | solution.py:207
  78.0 2.7 %collective-permute-start.37 = (f32[32,256]{1,0:T(8,128)S(1)}, f32[32,256]{1,0:T(8,128)S(1)}, u32[]{:S(2)}, u32[]{:S(2)}) collective-permute-start(f32[32,256]{1,0:T(8,128)S(1)} %get-tuple-element.18), channel_id=1, source_target_pairs={{0,64},{8,72},{16,80},{24,88},{32,96},{40,104},{48,112},{56,120},{... | collective-permute-start | bytes 98312 | tf_op jit(solution)/shard_map/ppermute | solution.py:207
  80.8 2.9 %collective-permute-start.34 = (f32[32,256]{1,0:T(8,128)S(1)}, f32[32,256]{1,0:T(8,128)S(1)}, u32[]{:S(2)}, u32[]{:S(2)}) collective-permute-start(f32[32,256]{1,0:T(8,128)S(1)} %get-tuple-element.18), channel_id=1, source_target_pairs={{0,16},{8,24},{16,32},{24,40},{32,48},{40,56},{48,64},{56,72},{64,... | collective-permute-start | bytes 98312 | tf_op jit(solution)/shard_map/ppermute | solution.py:207
  87.2 3.2 %collective-permute-done.35 = f32[32,256]{1,0:T(8,128)S(1)} collective-permute-done((f32[32,256]{1,0:T(8,128)S(1)}, f32[32,256]{1,0:T(8,128)S(1)}, u32[]{:S(2)}, u32[]{:S(2)}) %collective-permute-start.35) | collective-permute-done | bytes 32800 | tf_op jit(solution)/shard_map/ppermute | solution.py:207
  90.4 3.4 %collective-permute-start.21 = (f32[32,256]{1,0:T(8,128)S(1)}, f32[32,256]{1,0:T(8,128)S(1)}, u32[]{:S(2)}, u32[]{:S(2)}) collective-permute-start(f32[32,256]{1,0:T(8,128)S(1)} %get-tuple-element.20), channel_id=1, source_target_pairs={{0,96},{8,104},{16,112},{24,120},{32,0},{40,8},{48,16},{56,24},{64... | collective-permute-start | bytes 98312 | tf_op jit(solution)/shard_map/ppermute | solution.py:207
  97.1 3.0 %collective-permute-start.18 = (f32[32,256]{1,0:T(8,128)S(1)}, f32[32,256]{1,0:T(8,128)S(1)}, u32[]{:S(2)}, u32[]{:S(2)}) collective-permute-start(f32[32,256]{1,0:T(8,128)S(1)} %get-tuple-element.20), channel_id=1, source_target_pairs={{0,48},{8,56},{16,64},{24,72},{32,80},{40,88},{48,96},{56,104},{64... | collective-permute-start | bytes 98312 | tf_op jit(solution)/shard_map/ppermute | solution.py:207
  100.4 3.8 %collective-permute-done.16 = f32[32,256]{1,0:T(8,128)S(1)} collective-permute-done((f32[32,256]{1,0:T(8,128)S(1)}, f32[32,256]{1,0:T(8,128)S(1)}, u32[]{:S(2)}, u32[]{:S(2)}) %collective-permute-start.16) | collective-permute-done | bytes 32800 | tf_op jit(solution)/shard_map/ppermute | solution.py:207
  104.2 5.0 %collective-permute-done.17 = f32[32,256]{1,0:T(8,128)S(1)} collective-permute-done((f32[32,256]{1,0:T(8,128)S(1)}, f32[32,256]{1,0:T(8,128)S(1)}, u32[]{:S(2)}, u32[]{:S(2)}) %collective-permute-start.17) | collective-permute-done | bytes 32800 | tf_op jit(solution)/shard_map/ppermute | solution.py:207
  114.8 13.0 %collective-permute-start.42 = (f32[2,8,32,256]{3,2,1,0:T(8,128)S(1)}, f32[2,8,32,256]{3,2,1,0:T(8,128)S(1)}, u32[]{:S(2)}, u32[]{:S(2)}) collective-permute-start(f32[2,8,32,256]{3,2,1,0:T(8,128)S(1)} %pad_maximum_fusion.1), channel_id=1, source_target_pairs={{0,8},{8,0},{16,24},{24,16},{32,40},{40,32},{48,56},{56,48},{64,72... | collective-permute-start | bytes 1572872 | tf_op jit(solution)/shard_map/ppermute | solution.py:210
  127.9 3.8 %collective-permute-start.24 = (f32[2,8,32,256]{3,2,1,0:T(8,128)S(1)}, f32[2,8,32,256]{3,2,1,0:T(8,128)S(1)}, u32[]{:S(2)}, u32[]{:S(2)}) collective-permute-start(f32[2,8,32,256]{3,2,1,0:T(8,128)S(1)} %pad_maximum_fusion), channel_id=1, source_target_pairs={{0,8},{8,0},{16,24},{24,16},{32,40},{40,32},{48,56},{56,48},{64,72... | collective-permute-start | bytes 1572872 | tf_op jit(solution)/shard_map/ppermute | solution.py:210
  (100 shorter events, 42.5 us)
Async XLA Ops:
  9.1 11.8 %collective-permute-start.6 = (f32[32,256]{1,0:T(8,128)S(1)}, f32[32,256]{1,0:T(8,128)S(1)}, u32[]{:S(2)}, u32[]{:S(2)}) collective-permute-start(f32[32,256]{1,0:T(8,128)S(1)} %shard_map.37.refs_0_), channel_id=1, source_target_pairs={{0,7},{1,4},{2,5},{3,6},{4,3},{5,0},{6,1},{7,2},{8,15},{9,12},{10,... | collective-permute-start | bytes 98312 | tf_op jit(solution)/shard_map/ppermute | solution.py:194
  39.4 15.3 %collective-permute-start.8 = (f32[8,32,256]{2,1,0:T(8,128)S(1)}, f32[8,32,256]{2,1,0:T(8,128)S(1)}, u32[]{:S(2)}, u32[]{:S(2)}) collective-permute-start(f32[8,32,256]{2,1,0:T(8,128)S(1)} %fusion.3), channel_id=1, source_target_pairs={{0,128},{8,136},{16,144},{24,152},{32,160},{40,168},{48,176},{56,1... | collective-permute-start | bytes 786440 | tf_op jit(solution)/shard_map/ppermute | solution.py:201
  45.0 12.6 %collective-permute-start.27 = (f32[32,256]{1,0:T(8,128)S(1)}, f32[32,256]{1,0:T(8,128)S(1)}, u32[]{:S(2)}, u32[]{:S(2)}) collective-permute-start(f32[32,256]{1,0:T(8,128)S(1)} %get-tuple-element.21), channel_id=1, source_target_pairs={{0,16},{8,24},{16,32},{24,40},{32,48},{40,56},{48,64},{56,72},{64,... | collective-permute-start | bytes 98312 | tf_op jit(solution)/shard_map/ppermute | solution.py:205
  46.7 12.6 %collective-permute-start.33 = (f32[32,256]{1,0:T(8,128)S(1)}, f32[32,256]{1,0:T(8,128)S(1)}, u32[]{:S(2)}, u32[]{:S(2)}) collective-permute-start(f32[32,256]{1,0:T(8,128)S(1)} %get-tuple-element.22), channel_id=1, source_target_pairs={{0,112},{8,120},{16,0},{24,8},{32,16},{40,24},{48,32},{56,40},{64,... | collective-permute-start | bytes 98312 | tf_op jit(solution)/shard_map/ppermute | solution.py:205
  50.8 10.9 %collective-permute-start.32 = (f32[32,256]{1,0:T(8,128)S(1)}, f32[32,256]{1,0:T(8,128)S(1)}, u32[]{:S(2)}, u32[]{:S(2)}) collective-permute-start(f32[32,256]{1,0:T(8,128)S(1)} %get-tuple-element.23), channel_id=1, source_target_pairs={{0,96},{8,104},{16,112},{24,120},{32,0},{40,8},{48,16},{56,24},{64... | collective-permute-start | bytes 98312 | tf_op jit(solution)/shard_map/ppermute | solution.py:205
  52.6 9.1 %collective-permute-start.31 = (f32[32,256]{1,0:T(8,128)S(1)}, f32[32,256]{1,0:T(8,128)S(1)}, u32[]{:S(2)}, u32[]{:S(2)}) collective-permute-start(f32[32,256]{1,0:T(8,128)S(1)} %get-tuple-element.24), channel_id=1, source_target_pairs={{0,80},{8,88},{16,96},{24,104},{32,112},{40,120},{48,0},{56,8},{64... | collective-permute-start | bytes 98312 | tf_op jit(solution)/shard_map/ppermute | solution.py:205
  54.7 9.7 %collective-permute-start.30 = (f32[32,256]{1,0:T(8,128)S(1)}, f32[32,256]{1,0:T(8,128)S(1)}, u32[]{:S(2)}, u32[]{:S(2)}) collective-permute-start(f32[32,256]{1,0:T(8,128)S(1)} %get-tuple-element.25), channel_id=1, source_target_pairs={{0,64},{8,72},{16,80},{24,88},{32,96},{40,104},{48,112},{56,120},{... | collective-permute-start | bytes 98312 | tf_op jit(solution)/shard_map/ppermute | solution.py:205
  61.7 8.6 %collective-permute-start.15 = (f32[32,256]{1,0:T(8,128)S(1)}, f32[32,256]{1,0:T(8,128)S(1)}, u32[]{:S(2)}, u32[]{:S(2)}) collective-permute-start(f32[32,256]{1,0:T(8,128)S(1)} %get-tuple-element.29), channel_id=1, source_target_pairs={{0,112},{8,120},{16,0},{24,8},{32,16},{40,24},{48,32},{56,40},{64,... | collective-permute-start | bytes 98312 | tf_op jit(solution)/shard_map/ppermute | solution.py:205
  64.4 8.9 %collective-permute-start.14 = (f32[32,256]{1,0:T(8,128)S(1)}, f32[32,256]{1,0:T(8,128)S(1)}, u32[]{:S(2)}, u32[]{:S(2)}) collective-permute-start(f32[32,256]{1,0:T(8,128)S(1)} %get-tuple-element.30), channel_id=1, source_target_pairs={{0,96},{8,104},{16,112},{24,120},{32,0},{40,8},{48,16},{56,24},{64... | collective-permute-start | bytes 98312 | tf_op jit(solution)/shard_map/ppermute | solution.py:205
  64.4 10.3 %collective-permute-start.13 = (f32[32,256]{1,0:T(8,128)S(1)}, f32[32,256]{1,0:T(8,128)S(1)}, u32[]{:S(2)}, u32[]{:S(2)}) collective-permute-start(f32[32,256]{1,0:T(8,128)S(1)} %get-tuple-element.31), channel_id=1, source_target_pairs={{0,80},{8,88},{16,96},{24,104},{32,112},{40,120},{48,0},{56,8},{64... | collective-permute-start | bytes 98312 | tf_op jit(solution)/shard_map/ppermute | solution.py:205
  67.2 10.8 %collective-permute-start.12 = (f32[32,256]{1,0:T(8,128)S(1)}, f32[32,256]{1,0:T(8,128)S(1)}, u32[]{:S(2)}, u32[]{:S(2)}) collective-permute-start(f32[32,256]{1,0:T(8,128)S(1)} %get-tuple-element.32), channel_id=1, source_target_pairs={{0,64},{8,72},{16,80},{24,88},{32,96},{40,104},{48,112},{56,120},{... | collective-permute-start | bytes 98312 | tf_op jit(solution)/shard_map/ppermute | solution.py:205
  69.9 10.9 %collective-permute-start.11 = (f32[32,256]{1,0:T(8,128)S(1)}, f32[32,256]{1,0:T(8,128)S(1)}, u32[]{:S(2)}, u32[]{:S(2)}) collective-permute-start(f32[32,256]{1,0:T(8,128)S(1)} %get-tuple-element.33), channel_id=1, source_target_pairs={{0,48},{8,56},{16,64},{24,72},{32,80},{40,88},{48,96},{56,104},{64... | collective-permute-start | bytes 98312 | tf_op jit(solution)/shard_map/ppermute | solution.py:205
  70.3 10.5 %collective-permute-start.10 = (f32[32,256]{1,0:T(8,128)S(1)}, f32[32,256]{1,0:T(8,128)S(1)}, u32[]{:S(2)}, u32[]{:S(2)}) collective-permute-start(f32[32,256]{1,0:T(8,128)S(1)} %get-tuple-element.34), channel_id=1, source_target_pairs={{0,32},{8,40},{16,48},{24,56},{32,64},{40,72},{48,80},{56,88},{64,... | collective-permute-start | bytes 98312 | tf_op jit(solution)/shard_map/ppermute | solution.py:205
  73.3 23.7 %collective-permute-start.39 = (f32[32,256]{1,0:T(8,128)S(1)}, f32[32,256]{1,0:T(8,128)S(1)}, u32[]{:S(2)}, u32[]{:S(2)}) collective-permute-start(f32[32,256]{1,0:T(8,128)S(1)} %get-tuple-element.18), channel_id=1, source_target_pairs={{0,96},{8,104},{16,112},{24,120},{32,0},{40,8},{48,16},{56,24},{64... | collective-permute-start | bytes 98312 | tf_op jit(solution)/shard_map/ppermute | solution.py:207
  74.7 20.1 %collective-permute-start.38 = (f32[32,256]{1,0:T(8,128)S(1)}, f32[32,256]{1,0:T(8,128)S(1)}, u32[]{:S(2)}, u32[]{:S(2)}) collective-permute-start(f32[32,256]{1,0:T(8,128)S(1)} %get-tuple-element.18), channel_id=1, source_target_pairs={{0,80},{8,88},{16,96},{24,104},{32,112},{40,120},{48,0},{56,8},{64... | collective-permute-start | bytes 98312 | tf_op jit(solution)/shard_map/ppermute | solution.py:207
  78.0 15.7 %collective-permute-start.37 = (f32[32,256]{1,0:T(8,128)S(1)}, f32[32,256]{1,0:T(8,128)S(1)}, u32[]{:S(2)}, u32[]{:S(2)}) collective-permute-start(f32[32,256]{1,0:T(8,128)S(1)} %get-tuple-element.18), channel_id=1, source_target_pairs={{0,64},{8,72},{16,80},{24,88},{32,96},{40,104},{48,112},{56,120},{... | collective-permute-start | bytes 98312 | tf_op jit(solution)/shard_map/ppermute | solution.py:207
  80.8 9.6 %collective-permute-start.36 = (f32[32,256]{1,0:T(8,128)S(1)}, f32[32,256]{1,0:T(8,128)S(1)}, u32[]{:S(2)}, u32[]{:S(2)}) collective-permute-start(f32[32,256]{1,0:T(8,128)S(1)} %get-tuple-element.18), channel_id=1, source_target_pairs={{0,48},{8,56},{16,64},{24,72},{32,80},{40,88},{48,96},{56,104},{64... | collective-permute-start | bytes 98312 | tf_op jit(solution)/shard_map/ppermute | solution.py:207
  90.3 9.7 %collective-permute-start.40 = (f32[32,256]{1,0:T(8,128)S(1)}, f32[32,256]{1,0:T(8,128)S(1)}, u32[]{:S(2)}, u32[]{:S(2)}) collective-permute-start(f32[32,256]{1,0:T(8,128)S(1)} %get-tuple-element.18), channel_id=1, source_target_pairs={{0,112},{8,120},{16,0},{24,8},{32,16},{40,24},{48,32},{56,40},{64,... | collective-permute-start | bytes 98312 | tf_op jit(solution)/shard_map/ppermute | solution.py:207
  90.4 20.2 %collective-permute-start.21 = (f32[32,256]{1,0:T(8,128)S(1)}, f32[32,256]{1,0:T(8,128)S(1)}, u32[]{:S(2)}, u32[]{:S(2)}) collective-permute-start(f32[32,256]{1,0:T(8,128)S(1)} %get-tuple-element.20), channel_id=1, source_target_pairs={{0,96},{8,104},{16,112},{24,120},{32,0},{40,8},{48,16},{56,24},{64... | collective-permute-start | bytes 98312 | tf_op jit(solution)/shard_map/ppermute | solution.py:207
  93.8 16.8 %collective-permute-start.20 = (f32[32,256]{1,0:T(8,128)S(1)}, f32[32,256]{1,0:T(8,128)S(1)}, u32[]{:S(2)}, u32[]{:S(2)}) collective-permute-start(f32[32,256]{1,0:T(8,128)S(1)} %get-tuple-element.20), channel_id=1, source_target_pairs={{0,80},{8,88},{16,96},{24,104},{32,112},{40,120},{48,0},{56,8},{64... | collective-permute-start | bytes 98312 | tf_op jit(solution)/shard_map/ppermute | solution.py:207
  94.7 15.8 %collective-permute-start.19 = (f32[32,256]{1,0:T(8,128)S(1)}, f32[32,256]{1,0:T(8,128)S(1)}, u32[]{:S(2)}, u32[]{:S(2)}) collective-permute-start(f32[32,256]{1,0:T(8,128)S(1)} %get-tuple-element.20), channel_id=1, source_target_pairs={{0,64},{8,72},{16,80},{24,88},{32,96},{40,104},{48,112},{56,120},{... | collective-permute-start | bytes 98312 | tf_op jit(solution)/shard_map/ppermute | solution.py:207
  97.1 12.1 %collective-permute-start.18 = (f32[32,256]{1,0:T(8,128)S(1)}, f32[32,256]{1,0:T(8,128)S(1)}, u32[]{:S(2)}, u32[]{:S(2)}) collective-permute-start(f32[32,256]{1,0:T(8,128)S(1)} %get-tuple-element.20), channel_id=1, source_target_pairs={{0,48},{8,56},{16,64},{24,72},{32,80},{40,88},{48,96},{56,104},{64... | collective-permute-start | bytes 98312 | tf_op jit(solution)/shard_map/ppermute | solution.py:207
  112.0 15.9 %collective-permute-start.23 = (f32[8,32,256]{2,1,0:T(8,128)S(1)}, f32[8,32,256]{2,1,0:T(8,128)S(1)}, u32[]{:S(2)}, u32[]{:S(2)}) collective-permute-start(f32[8,32,256]{2,1,0:T(8,128)S(1)} %constant_dynamic-update-slice_fusion.refs_0_), channel_id=1, source_target_pairs={{0,128},{8,136},{16,144},{24,152},{32,160},{40,168},{48,176},{56,1... | collective-permute-start | bytes 786440 | tf_op jit(solution)/shard_map/ppermute | solution.py:209
  114.8 16.8 %collective-permute-start.42 = (f32[2,8,32,256]{3,2,1,0:T(8,128)S(1)}, f32[2,8,32,256]{3,2,1,0:T(8,128)S(1)}, u32[]{:S(2)}, u32[]{:S(2)}) collective-permute-start(f32[2,8,32,256]{3,2,1,0:T(8,128)S(1)} %pad_maximum_fusion.1), channel_id=1, source_target_pairs={{0,8},{8,0},{16,24},{24,16},{32,40},{40,32},{48,56},{56,48},{64,72... | collective-permute-start | bytes 1572872 | tf_op jit(solution)/shard_map/ppermute | solution.py:210
  (23 other events, 131.2 us)

commit v2 on v0

v2 whole, which is shorter than its diff:
```python
import jax
import jax.numpy as jnp
from jax import lax
from jax.experimental import pallas as pl
from jax.experimental.pallas import tpu as pltpu
from jax.sharding import PartitionSpec as P

N_CORE = 2
N_Z = 8
N_SENS = 32
N_CAND = 8
SLOTS = 4
STREAMS = 1
STEPS = 8
MIB = 1 << 20

STEP_OF_EVEN = (1, -1, 3)


def z_pairs(stage):
    pairs = []
    for s in range(N_SENS):
        core, z, xl = s % N_CORE, (s // N_CORE) % N_Z, s // (N_CORE * N_Z)
        sign = 1 if (z - core) % 2 == 0 else -1
        to = (z + sign * STEP_OF_EVEN[stage]) % N_Z
        pairs.append((s, (xl * N_Z + to) * N_CORE + core))
    return pairs


NEAR, NEXT, FAR = z_pairs(0), z_pairs(1), z_pairs(2)
CORE_SWAP = [(s, s ^ 1) for s in range(N_SENS)]
X_SWAP = [(s, s ^ 16) for s in range(N_SENS)]
CAND_STAGES = [[(c, c ^ flip) for c in range(N_CAND)] for flip in (1, 3, 4)]
PAIR_OF_SLOT = (0, 2, -1, 1)

VMEM = pl.BlockSpec(memory_space=pltpu.VMEM)
SMEM = pl.BlockSpec(memory_space=pltpu.SMEM)
HBM = pl.BlockSpec(memory_space=pltpu.HBM)


def slot_columns(me, core, slot, stream, width):
    place = lax.rem(lax.div(me, N_CORE) + N_Z - core, N_Z)
    odd = lax.rem(place, 2)
    pair = lax.div(place + odd * (2 * N_Z - 3), 2)
    pair = lax.rem(pair + 2 * N_Z + (1 - 2 * odd) * PAIR_OF_SLOT[slot], SLOTS)
    block = (core * STREAMS + stream) * SLOTS + pair
    return pl.ds(pl.multiple_of(block * width, width), width)


def predict_kernel(me_ref, blocks_ref, jac_ref, out_ref):
    width = jac_ref.shape[1] // STEPS
    total = jnp.zeros(out_ref.shape, jnp.float32)
    for step in range(STEPS):
        cols = slice(step * width, (step + 1) * width)
        total += lax.dot_general(
            blocks_ref[:, cols].astype(jnp.bfloat16),
            jac_ref[:, cols],
            (((1,), (1,)), ((), ())),
            preferred_element_type=jnp.float32,
        )
    out_ref[...] = total


def predict(me, blocks, jacobian):
    k, ncols = blocks.shape
    rows = jacobian.shape[0]
    return pl.pallas_call(
        predict_kernel,
        in_specs=[SMEM, VMEM, VMEM],
        out_specs=VMEM,
        out_shape=jax.ShapeDtypeStruct((k, rows), jnp.float32),
        compiler_params=pltpu.CompilerParams(vmem_limit_bytes=24 * MIB),
        cost_estimate=pl.CostEstimate(
            flops=2 * k * ncols * rows, bytes_accessed=2 * rows * ncols, transcendentals=0
        ),
    )(me, blocks, jacobian)


def product(me, weighted, held, other_core, slots, stream):
    k, rows = weighted.shape
    width = held.shape[1] // (N_CORE * SLOTS * STREAMS)

    def kernel(me_ref, weighted_ref, held_ref, out_ref):
        core = lax.rem(me_ref[0], N_CORE)
        core = 1 - core if other_core else core
        for i, slot in enumerate(slots):
            out_ref[i] = jnp.dot(
                weighted_ref[...],
                held_ref[:, slot_columns(me_ref[0], core, slot, stream, width)],
                preferred_element_type=jnp.float32,
            )

    return pl.pallas_call(
        kernel,
        in_specs=[SMEM, VMEM, VMEM],
        out_specs=VMEM,
        out_shape=jax.ShapeDtypeStruct((len(slots), k, width), jnp.float32),
        compiler_params=pltpu.CompilerParams(vmem_limit_bytes=24 * MIB),
        cost_estimate=pl.CostEstimate(
            flops=2 * k * len(slots) * width * rows,
            bytes_accessed=2 * rows * len(slots) * width,
            transcendentals=0,
        ),
    )(me, weighted, held)


def assemble(me, streams, ncols):
    k, width = streams[0][0].shape[-2:]
    per_stream = len(streams[0])

    def kernel(me_ref, *refs):
        out_ref = refs[-1]
        core = lax.rem(me_ref[0], N_CORE)
        for stream in range(STREAMS):
            parts = refs[stream * per_stream : (stream + 1) * per_stream]
            for owner, (low, high) in ((core, parts[:2]), (1 - core, parts[2:])):
                for slot in range(SLOTS):
                    ref = low if slot < 2 else high
                    cols = slot_columns(me_ref[0], owner, slot, stream, width)
                    out_ref[:, cols] = ref[slot % 2]

    operands = [part for parts in streams for part in parts]
    return pl.pallas_call(
        kernel,
        in_specs=[SMEM] + [VMEM] * len(operands),
        out_specs=VMEM,
        out_shape=jax.ShapeDtypeStruct((k, ncols), jnp.float32),
        compiler_params=pltpu.CompilerParams(vmem_limit_bytes=16 * MIB),
    )(me, *operands)


def local(jacobian, weights, blocks):
    p, k, ncols = blocks.shape
    me = lax.axis_index("sens").astype(jnp.int32).reshape(1)

    def swap(value, pairs):
        return lax.ppermute(value, "sens", pairs)

    predicted = predict(me, blocks.reshape(p * k, ncols), jacobian)
    held = jacobian
    for pairs in CAND_STAGES:
        predicted = predicted + lax.ppermute(predicted, "cand", pairs)
    weighted = weights[:, None, :] * predicted.reshape(p, k, -1)
    weighted = weighted.reshape(p * k, -1).astype(jnp.bfloat16)

    streams = []
    for stream in range(STREAMS):
        high = swap(product(me, weighted, held, True, (2, 3), stream), CORE_SWAP)
        high = high + product(me, weighted, held, False, (2, 3), stream)
        near = swap(high, NEAR)
        low = swap(product(me, weighted, held, True, (0, 1), stream), CORE_SWAP)
        low = low + product(me, weighted, held, False, (0, 1), stream)
        total = low[0] + near[0] + swap(low[1] + near[1], NEXT)
        total = total + swap(total, FAR)
        total = total + swap(total, X_SWAP)
        low = jnp.stack([total, swap(total, NEXT)])
        high = swap(low, NEAR)
        streams.append((low, high, swap(low, CORE_SWAP), swap(high, CORE_SWAP)))
    return assemble(me, streams, ncols).reshape(p, k, ncols)


def solution(mesh):
    return jax.shard_map(
        local,
        mesh=mesh,
        in_specs=(P("sens", "cand"), P(None, "sens"), P(None, None, "cand")),
        out_specs=P(None, None, "cand"),
        check_vma=False,
    )
```

time: 299 us -> 86.7 us (0.29)
  waiting for transfers between devices: 234 us -> 46.8 us
  blocking collectives: 35.6 us -> 0 us
  starting transfers between devices: 0.01 us -> 28.5 us
  between operations: 13.4 us -> 0.08 us
  matrix products: 12.9 us -> 0 us
  Pallas kernels: 0 us -> 5.9 us
    psum x1 -> x0, waiting for transfers between devices: 234 us -> none  [column_sum(): return lax.psum(partial_terms, 'sens')]
    ppermute x0 -> x13, waiting for transfers between devices: none -> 46.8 us  [the longest x10 42.7 us: swap(): return lax.ppermute(value, 'sens', pairs)]
    psum x1 -> x0, blocking collectives: 35.6 us -> none  [curvature_pass(): predicted = lax.psum(predicted, 'cand')]
    ppermute x0 -> x13, starting transfers between devices: none -> 28.5 us  [the longest x10 20.7 us: swap(): return lax.ppermute(value, 'sens', pairs)]
    dot_general x2 -> x0, matrix products: 12.9 us -> none  [the longest x1 6.64 us: curvature_pass(): jnp.einsum('pkc,rc->pkr', directions, jacobian, preferred_element_type=jn...]
    pallas_call x0 -> x6, Pallas kernels: none -> 5.9 us  [the longest x1 2.56 us: predict(): pl.pallas_call(predict_kernel, in_specs=[SMEM, VMEM, VMEM], out_specs=VME...]
  transfers between devices with their start and end apart: 1 -> 13, of which waited for: 1 -> 11; matrix products, arithmetic and copies ran while one was open for 0% -> 0% of each run, Pallas kernels for 0% -> 2%
where the time goes in v2:
time: 86.7 us; the launch traced here: 86.6 us
  waiting for transfers between devices  46.8 us (54%)
  starting transfers between devices  28.5 us (33%)
  Pallas kernels  5.9 us (7%)
  local copies, waits for them, and re-layouts  4.98 us (6%)
    ppermute x10, waiting for transfers between devices, swap(): return lax.ppermute(value, 'sens', pairs)  42.7 us
    ppermute x10, starting transfers between devices, swap(): return lax.ppermute(value, 'sens', pairs)  20.7 us
    ppermute x3, starting transfers between devices, local(): predicted = predicted + lax.ppermute(predicted, 'cand', pairs)  7.84 us
    unnamed x8, local copies, waits for them, and re-layouts  4.98 us
    ppermute x3, waiting for transfers between devices, local(): predicted = predicted + lax.ppermute(predicted, 'cand', pairs)  4.13 us
    pallas_call x1, Pallas kernels, predict(): pl.pallas_call(predict_kernel, in_specs=[SMEM, VMEM, VMEM], out_specs=VME...  2.56 us
    pallas_call x4, Pallas kernels, product(): pl.pallas_call(kernel, in_specs=[SMEM, VMEM, VMEM], out_specs=VMEM, out_s...  1.86 us
  transfers between devices with their start and end apart: 13, of which 11 were waited for; matrix products, arithmetic and copies ran while one was open for 0% of the time, Pallas kernels for 2%

profile of v2, /device:TPU:1, one launch (start us, length us, event | category | flops | bytes accessed | tf_op | source)
XLA Modules:
  0.0 86.6 jit_solution(14385647031572378176)
XLA Ops:
  0.0 3.4 %copy-done = bf16[256,16384]{1,0:T(8,128)(2,1)S(1)} copy-done((bf16[256,16384]{1,0:T(8,128)(2,1)S(1)}, bf16[256,16384]{1,0:T(8,128)(2,1)}, u32[]{:S(2)}) %copy-start) | copy-done | bytes 8388632
  3.4 1.6 %copy-done.2 = f32[2,16,16384]{2,1,0:T(8,128)S(1)} copy-done((f32[2,16,16384]{2,1,0:T(8,128)S(1)}, f32[2,16,16384]{2,1,0:T(8,128)}, u32[]{:S(2)}) %copy-start.2) | copy-done | bytes 2097176
  5.0 2.6 %shard_map.37 = f32[32,256]{1,0:T(8,128)S(1)} custom-call(s32[1]{0:T(128)} %bitcast.me_ref, f32[32,16384]{1,0:T(8,128)S(1)} %bitcast.15, bf16[256,16384]{1,0:T(8,128)(2,1)S(1)} %copy-done), custom_call_target="tpu_custom_call" | custom-call | flops 268435456 | bytes 8388608 | tf_op jit(solution)/shard_map/pallas_call | solution.py:67
  7.5 2.2 %collective-permute-start = (f32[32,256]{1,0:T(8,128)S(1)}, f32[32,256]{1,0:T(8,128)S(1)}, u32[]{:S(2)}, u32[]{:S(2)}) collective-permute-start(f32[32,256]{1,0:T(8,128)S(1)} %shard_map.37), channel_id=1, source_target_pairs={{0,1},{1,0},{2,3},{3,2},{4,5},{5,4},{6,7},{7,6},{8,9},{9,8},{10,11... | collective-permute-start | bytes 98312 | tf_op jit(solution)/shard_map/ppermute | solution.py:142
  9.7 1.3 %collective-permute-done = f32[32,256]{1,0:T(8,128)S(1)} collective-permute-done((f32[32,256]{1,0:T(8,128)S(1)}, f32[32,256]{1,0:T(8,128)S(1)}, u32[]{:S(2)}, u32[]{:S(2)}) %collective-permute-start) | collective-permute-done | bytes 32800 | tf_op jit(solution)/shard_map/ppermute | solution.py:142
  11.1 2.9 %collective-permute-start.1 = (f32[32,256]{1,0:T(8,128)S(1)}, f32[32,256]{1,0:T(8,128)S(1)}, u32[]{:S(2)}, u32[]{:S(2)}) collective-permute-start(f32[32,256]{1,0:T(8,128)S(1)} %add.36), channel_id=1, source_target_pairs={{0,3},{1,2},{2,1},{3,0},{4,7},{5,6},{6,5},{7,4},{8,11},{9,10},{10,... | collective-permute-start | bytes 98312 | tf_op jit(solution)/shard_map/ppermute | solution.py:142
  14.0 1.3 %collective-permute-done.1 = f32[32,256]{1,0:T(8,128)S(1)} collective-permute-done((f32[32,256]{1,0:T(8,128)S(1)}, f32[32,256]{1,0:T(8,128)S(1)}, u32[]{:S(2)}, u32[]{:S(2)}) %collective-permute-start.1) | collective-permute-done | bytes 32800 | tf_op jit(solution)/shard_map/ppermute | solution.py:142
  15.3 2.7 %collective-permute-start.2 = (f32[32,256]{1,0:T(8,128)S(1)}, f32[32,256]{1,0:T(8,128)S(1)}, u32[]{:S(2)}, u32[]{:S(2)}) collective-permute-start(f32[32,256]{1,0:T(8,128)S(1)} %add.37), channel_id=1, source_target_pairs={{0,4},{1,5},{2,6},{3,7},{4,0},{5,1},{6,2},{7,3},{8,12},{9,13},{10,... | collective-permute-start | bytes 98312 | tf_op jit(solution)/shard_map/ppermute | solution.py:142
  18.0 1.5 %collective-permute-done.2 = f32[32,256]{1,0:T(8,128)S(1)} collective-permute-done((f32[32,256]{1,0:T(8,128)S(1)}, f32[32,256]{1,0:T(8,128)S(1)}, u32[]{:S(2)}, u32[]{:S(2)}) %collective-permute-start.2) | collective-permute-done | bytes 32800 | tf_op jit(solution)/shard_map/ppermute | solution.py:142
  20.0 5.9 %collective-permute-start.4 = (f32[2,32,2048]{2,1,0:T(8,128)S(1)}, f32[2,32,2048]{2,1,0:T(8,128)S(1)}, u32[]{:S(2)}, u32[]{:S(2)}) collective-permute-start(f32[2,32,2048]{2,1,0:T(8,128)S(1)} %shard_map.40), channel_id=1, source_target_pairs={{0,8},{8,0},{16,24},{24,16},{32,40},{40,32},{48,56},{56,48},{64,72... | collective-permute-start | bytes 1572872 | tf_op jit(solution)/shard_map/ppermute | solution.py:137
  27.5 3.9 %collective-permute-start.5 = (f32[2,32,2048]{2,1,0:T(8,128)S(1)}, f32[2,32,2048]{2,1,0:T(8,128)S(1)}, u32[]{:S(2)}, u32[]{:S(2)}) collective-permute-start(f32[2,32,2048]{2,1,0:T(8,128)S(1)} %add.40), channel_id=1, source_target_pairs={{0,16},{8,120},{16,0},{24,40},{32,48},{40,24},{48,32},{56,72},{64,... | collective-permute-start | bytes 1572872 | tf_op jit(solution)/shard_map/ppermute | solution.py:137
  32.0 6.0 %collective-permute-done.5 = f32[2,32,2048]{2,1,0:T(8,128)S(1)} collective-permute-done((f32[2,32,2048]{2,1,0:T(8,128)S(1)}, f32[2,32,2048]{2,1,0:T(8,128)S(1)}, u32[]{:S(2)}, u32[]{:S(2)}) %collective-permute-start.5) | collective-permute-done | bytes 524320 | tf_op jit(solution)/shard_map/ppermute | solution.py:137
  38.1 5.5 %collective-permute-done.6 = f32[32,2048]{1,0:T(8,128)S(1)} collective-permute-done((f32[32,2048]{1,0:T(8,128)S(1)}, f32[32,2048]{1,0:T(8,128)S(1)}, u32[]{:S(2)}, u32[]{:S(2)}) %collective-permute-start.6) | collective-permute-done | bytes 262176 | tf_op jit(solution)/shard_map/ppermute | solution.py:137
  43.7 2.9 %collective-permute-start.7 = (f32[32,2048]{1,0:T(8,128)S(1)}, f32[32,2048]{1,0:T(8,128)S(1)}, u32[]{:S(2)}, u32[]{:S(2)}) collective-permute-start(f32[32,2048]{1,0:T(8,128)S(1)} %fusion.2), channel_id=1, source_target_pairs={{0,48},{8,88},{16,96},{24,72},{32,80},{40,120},{48,0},{56,104},{64... | collective-permute-start | bytes 786440 | tf_op jit(solution)/shard_map/ppermute | solution.py:137
  46.6 11.1 %collective-permute-done.7 = f32[32,2048]{1,0:T(8,128)S(1)} collective-permute-done((f32[32,2048]{1,0:T(8,128)S(1)}, f32[32,2048]{1,0:T(8,128)S(1)}, u32[]{:S(2)}, u32[]{:S(2)}) %collective-permute-start.7) | collective-permute-done | bytes 262176 | tf_op jit(solution)/shard_map/ppermute | solution.py:137
  57.7 1.3 %collective-permute-start.8 = (f32[32,2048]{1,0:T(8,128)S(1)}, f32[32,2048]{1,0:T(8,128)S(1)}, u32[]{:S(2)}, u32[]{:S(2)}) collective-permute-start(f32[32,2048]{1,0:T(8,128)S(1)} %add.46), channel_id=1, source_target_pairs={{0,128},{8,136},{16,144},{24,152},{32,160},{40,168},{48,176},{56,1... | collective-permute-start | bytes 786440 | tf_op jit(solution)/shard_map/ppermute | solution.py:137
  59.0 6.5 %collective-permute-done.8 = f32[32,2048]{1,0:T(8,128)S(1)} collective-permute-done((f32[32,2048]{1,0:T(8,128)S(1)}, f32[32,2048]{1,0:T(8,128)S(1)}, u32[]{:S(2)}, u32[]{:S(2)}) %collective-permute-start.8) | collective-permute-done | bytes 262176 | tf_op jit(solution)/shard_map/ppermute | solution.py:137
  65.6 5.5 %collective-permute-done.9 = f32[32,2048]{1,0:T(8,128)S(1)} collective-permute-done((f32[32,2048]{1,0:T(8,128)S(1)}, f32[32,2048]{1,0:T(8,128)S(1)}, u32[]{:S(2)}, u32[]{:S(2)}) %collective-permute-start.9) | collective-permute-done | bytes 262176 | tf_op jit(solution)/shard_map/ppermute | solution.py:137
  71.2 0.8 collective-permute-start.10
  72.0 2.5 %collective-permute-start.11 = (f32[2,32,2048]{2,1,0:T(8,128)S(1)}, f32[2,32,2048]{2,1,0:T(8,128)S(1)}, u32[]{:S(2)}, u32[]{:S(2)}) collective-permute-start(f32[2,32,2048]{2,1,0:T(8,128)S(1)} %pad_maximum_fusion.refs_0_), channel_id=1, source_target_pairs={{0,8},{8,0},{16,24},{24,16},{32,40},{40,32},{48,56},{56,48},{64,72... | collective-permute-start | bytes 1572872 | tf_op jit(solution)/shard_map/ppermute | solution.py:137
  74.5 6.0 %collective-permute-done.10.refs_1_ = f32[2,32,2048]{2,1,0:T(8,128)S(1)} collective-permute-done((f32[2,32,2048]{2,1,0:T(8,128)S(1)}, f32[2,32,2048]{2,1,0:T(8,128)S(1)}, u32[]{:S(2)}, u32[]{:S(2)}) %collective-permute-start.10) | collective-permute-done | bytes 524320 | tf_op jit(solution)/shard_map/ppermute | solution.py:137
  80.5 3.1 %collective-permute-start.12 = (f32[2,32,2048]{2,1,0:T(8,128)S(1)}, f32[2,32,2048]{2,1,0:T(8,128)S(1)}, u32[]{:S(2)}, u32[]{:S(2)}) collective-permute-start(f32[2,32,2048]{2,1,0:T(8,128)S(1)} %collective-permute-done.10.refs_1_), channel_id=1, source_target_pairs={{0,8},{8,0},{16,24},{24,16},{32,40},{40,32},{48,56},{56,48},{64,72... | collective-permute-start | bytes 1572872 | tf_op jit(solution)/shard_map/ppermute | solution.py:137
  83.6 1.5 %collective-permute-done.12.refs_3_ = f32[2,32,2048]{2,1,0:T(8,128)S(1)} collective-permute-done((f32[2,32,2048]{2,1,0:T(8,128)S(1)}, f32[2,32,2048]{2,1,0:T(8,128)S(1)}, u32[]{:S(2)}, u32[]{:S(2)}) %collective-permute-start.12) | collective-permute-done | bytes 524320 | tf_op jit(solution)/shard_map/ppermute | solution.py:137
  85.1 1.5 %shard_map.42 = f32[32,16384]{1,0:T(8,128)} custom-call(s32[1]{0:T(128)} %bitcast.me_ref, f32[2,32,2048]{2,1,0:T(8,128)S(1)} %pad_maximum_fusion.refs_0_, f32[2,32,2048]{2,1,0:T(8,128)S(1)} %collective-permute-done.10.refs_1_, f32[2,32,2048]{2,1,0:T(8,128)S(1)} %collective-permute-done.11.refs_2_, f32[2,32,2048]{2,1,0:T(8,128)S(1)} %collective-permute-done.12.refs_3_), custom_call_target="tpu_custom_call" | custom-call | tf_op jit(solution)/shard_map/pallas_call | solution.py:123
  (26 shorter events, 3.0 us)
Async XLA Ops:
  0.0 3.4 %copy-start = (bf16[256,16384]{1,0:T(8,128)(2,1)S(1)}, bf16[256,16384]{1,0:T(8,128)(2,1)}, u32[]{:S(2)}) copy-start(bf16[256,16384]{1,0:T(8,128)(2,1)} %held_ref.7) | copy-start | bytes 25165828
  3.4 1.6 %copy-start.2 = (f32[2,16,16384]{2,1,0:T(8,128)S(1)}, f32[2,16,16384]{2,1,0:T(8,128)}, u32[]{:S(2)}) copy-start(f32[2,16,16384]{2,1,0:T(8,128)} %param.5) | copy-start | bytes 6291460
  5.0 14.6 %copy-start.3 = (f32[2,256]{1,0:T(2,128)S(1)}, f32[2,256]{1,0:T(2,128)}, u32[]{:S(2)}) copy-start(f32[2,256]{1,0:T(2,128)} %param.4) | copy-start | bytes 6148
  5.0 14.6 %copy-start.1 = (bf16[256,16384]{1,0:T(8,128)(2,1)S(1)}, bf16[256,16384]{1,0:T(8,128)(2,1)}, u32[]{:S(2)}) copy-start(bf16[256,16384]{1,0:T(8,128)(2,1)} %held_ref.7) | copy-start | bytes 25165828
  7.5 3.5 %collective-permute-start = (f32[32,256]{1,0:T(8,128)S(1)}, f32[32,256]{1,0:T(8,128)S(1)}, u32[]{:S(2)}, u32[]{:S(2)}) collective-permute-start(f32[32,256]{1,0:T(8,128)S(1)} %shard_map.37), channel_id=1, source_target_pairs={{0,1},{1,0},{2,3},{3,2},{4,5},{5,4},{6,7},{7,6},{8,9},{9,8},{10,11... | collective-permute-start | bytes 98312 | tf_op jit(solution)/shard_map/ppermute | solution.py:142
  11.1 4.2 %collective-permute-start.1 = (f32[32,256]{1,0:T(8,128)S(1)}, f32[32,256]{1,0:T(8,128)S(1)}, u32[]{:S(2)}, u32[]{:S(2)}) collective-permute-start(f32[32,256]{1,0:T(8,128)S(1)} %add.36), channel_id=1, source_target_pairs={{0,3},{1,2},{2,1},{3,0},{4,7},{5,6},{6,5},{7,4},{8,11},{9,10},{10,... | collective-permute-start | bytes 98312 | tf_op jit(solution)/shard_map/ppermute | solution.py:142
  15.3 4.3 %collective-permute-start.2 = (f32[32,256]{1,0:T(8,128)S(1)}, f32[32,256]{1,0:T(8,128)S(1)}, u32[]{:S(2)}, u32[]{:S(2)}) collective-permute-start(f32[32,256]{1,0:T(8,128)S(1)} %add.37), channel_id=1, source_target_pairs={{0,4},{1,5},{2,6},{3,7},{4,0},{5,1},{6,2},{7,3},{8,12},{9,13},{10,... | collective-permute-start | bytes 98312 | tf_op jit(solution)/shard_map/ppermute | solution.py:142
  20.0 7.4 %collective-permute-start.4 = (f32[2,32,2048]{2,1,0:T(8,128)S(1)}, f32[2,32,2048]{2,1,0:T(8,128)S(1)}, u32[]{:S(2)}, u32[]{:S(2)}) collective-permute-start(f32[2,32,2048]{2,1,0:T(8,128)S(1)} %shard_map.40), channel_id=1, source_target_pairs={{0,8},{8,0},{16,24},{24,16},{32,40},{40,32},{48,56},{56,48},{64,72... | collective-permute-start | bytes 1572872 | tf_op jit(solution)/shard_map/ppermute | solution.py:137
  26.4 5.5 %collective-permute-start.3 = (f32[2,32,2048]{2,1,0:T(8,128)S(1)}, f32[2,32,2048]{2,1,0:T(8,128)S(1)}, u32[]{:S(2)}, u32[]{:S(2)}) collective-permute-start(f32[2,32,2048]{2,1,0:T(8,128)S(1)} %shard_map.38), channel_id=1, source_target_pairs={{0,8},{8,0},{16,24},{24,16},{32,40},{40,32},{48,56},{56,48},{64,72... | collective-permute-start | bytes 1572872 | tf_op jit(solution)/shard_map/ppermute | solution.py:137
  27.5 10.5 %collective-permute-start.5 = (f32[2,32,2048]{2,1,0:T(8,128)S(1)}, f32[2,32,2048]{2,1,0:T(8,128)S(1)}, u32[]{:S(2)}, u32[]{:S(2)}) collective-permute-start(f32[2,32,2048]{2,1,0:T(8,128)S(1)} %add.40), channel_id=1, source_target_pairs={{0,16},{8,120},{16,0},{24,40},{32,48},{40,24},{48,32},{56,72},{64,... | collective-permute-start | bytes 1572872 | tf_op jit(solution)/shard_map/ppermute | solution.py:137
  38.0 5.6 %collective-permute-start.6 = (f32[32,2048]{1,0:T(8,128)S(1)}, f32[32,2048]{1,0:T(8,128)S(1)}, u32[]{:S(2)}, u32[]{:S(2)}) collective-permute-start(f32[32,2048]{1,0:T(8,128)S(1)} %fusion), channel_id=1, source_target_pairs={{0,112},{8,24},{16,32},{24,8},{32,16},{40,56},{48,64},{56,40},{64,... | collective-permute-start | bytes 786440 | tf_op jit(solution)/shard_map/ppermute | solution.py:137
  43.7 14.0 %collective-permute-start.7 = (f32[32,2048]{1,0:T(8,128)S(1)}, f32[32,2048]{1,0:T(8,128)S(1)}, u32[]{:S(2)}, u32[]{:S(2)}) collective-permute-start(f32[32,2048]{1,0:T(8,128)S(1)} %fusion.2), channel_id=1, source_target_pairs={{0,48},{8,88},{16,96},{24,72},{32,80},{40,120},{48,0},{56,104},{64... | collective-permute-start | bytes 786440 | tf_op jit(solution)/shard_map/ppermute | solution.py:137
  57.7 7.7 %collective-permute-start.8 = (f32[32,2048]{1,0:T(8,128)S(1)}, f32[32,2048]{1,0:T(8,128)S(1)}, u32[]{:S(2)}, u32[]{:S(2)}) collective-permute-start(f32[32,2048]{1,0:T(8,128)S(1)} %add.46), channel_id=1, source_target_pairs={{0,128},{8,136},{16,144},{24,152},{32,160},{40,168},{48,176},{56,1... | collective-permute-start | bytes 786440 | tf_op jit(solution)/shard_map/ppermute | solution.py:137
  65.5 5.6 %collective-permute-start.9 = (f32[32,2048]{1,0:T(8,128)S(1)}, f32[32,2048]{1,0:T(8,128)S(1)}, u32[]{:S(2)}, u32[]{:S(2)}) collective-permute-start(f32[32,2048]{1,0:T(8,128)S(1)} %add.47), channel_id=1, source_target_pairs={{0,112},{8,24},{16,32},{24,8},{32,16},{40,56},{48,64},{56,40},{64,... | collective-permute-start | bytes 786440 | tf_op jit(solution)/shard_map/ppermute | solution.py:137
  71.2 9.3 %collective-permute-start.10 = (f32[2,32,2048]{2,1,0:T(8,128)S(1)}, f32[2,32,2048]{2,1,0:T(8,128)S(1)}, u32[]{:S(2)}, u32[]{:S(2)}) collective-permute-start(f32[2,32,2048]{2,1,0:T(8,128)S(1)} %pad_maximum_fusion.refs_0_), channel_id=1, source_target_pairs={{0,16},{8,120},{16,0},{24,40},{32,48},{40,24},{48,32},{56,72},{64,... | collective-permute-start | bytes 1572872 | tf_op jit(solution)/shard_map/ppermute | solution.py:137
  72.0 11.6 %collective-permute-start.11 = (f32[2,32,2048]{2,1,0:T(8,128)S(1)}, f32[2,32,2048]{2,1,0:T(8,128)S(1)}, u32[]{:S(2)}, u32[]{:S(2)}) collective-permute-start(f32[2,32,2048]{2,1,0:T(8,128)S(1)} %pad_maximum_fusion.refs_0_), channel_id=1, source_target_pairs={{0,8},{8,0},{16,24},{24,16},{32,40},{40,32},{48,56},{56,48},{64,72... | collective-permute-start | bytes 1572872 | tf_op jit(solution)/shard_map/ppermute | solution.py:137
  80.5 4.6 %collective-permute-start.12 = (f32[2,32,2048]{2,1,0:T(8,128)S(1)}, f32[2,32,2048]{2,1,0:T(8,128)S(1)}, u32[]{:S(2)}, u32[]{:S(2)}) collective-permute-start(f32[2,32,2048]{2,1,0:T(8,128)S(1)} %collective-permute-done.10.refs_1_), channel_id=1, source_target_pairs={{0,8},{8,0},{16,24},{24,16},{32,40},{40,32},{48,56},{56,48},{64,72... | collective-permute-start | bytes 1572872 | tf_op jit(solution)/shard_map/ppermute | solution.py:137

commit v3 on v2

--- a/solution.py
+++ b/solution.py
@@ -10,7 +10,7 @@
 N_SENS = 32
 N_CAND = 8
 SLOTS = 4
-STREAMS = 1
+STREAMS = 2
 STEPS = 8
 MIB = 1 << 20
 
@@ -31,7 +31,8 @@
 CORE_SWAP = [(s, s ^ 1) for s in range(N_SENS)]
 X_SWAP = [(s, s ^ 16) for s in range(N_SENS)]
 CAND_STAGES = [[(c, c ^ flip) for c in range(N_CAND)] for flip in (1, 3, 4)]
-PAIR_OF_SLOT = (0, 2, -1, 1)
+X_FIRST = (False, False)
+SUMS = ((FAR, NEXT), (NEXT, FAR))
 
 VMEM = pl.BlockSpec(memory_space=pltpu.VMEM)
 SMEM = pl.BlockSpec(memory_space=pltpu.SMEM)
@@ -40,10 +41,14 @@
 
 def slot_columns(me, core, slot, stream, width):
     place = lax.rem(lax.div(me, N_CORE) + N_Z - core, N_Z)
-    odd = lax.rem(place, 2)
-    pair = lax.div(place + odd * (2 * N_Z - 3), 2)
-    pair = lax.rem(pair + 2 * N_Z + (1 - 2 * odd) * PAIR_OF_SLOT[slot], SLOTS)
-    block = (core * STREAMS + stream) * SLOTS + pair
+    half = lax.rem(lax.div(place + 1, 2), 2)
+    xl = lax.div(me, N_CORE * N_Z)
+    first, second = slot // 2, slot % 2
+    if X_FIRST[stream]:
+        first, second = second, first
+    half = 1 - half if first else half
+    xl = 1 - xl if second else xl
+    block = (core * STREAMS + stream) * SLOTS + 2 * half + xl
     return pl.ds(pl.multiple_of(block * width, width), width)
 
 
@@ -138,23 +143,27 @@
 
     predicted = predict(me, blocks.reshape(p * k, ncols), jacobian)
     held = jacobian
-    for pairs in CAND_STAGES:
-        predicted = predicted + lax.ppermute(predicted, "cand", pairs)
+    def flip(value, bits):
+        return lax.ppermute(value, "cand", [(c, c ^ bits) for c in range(N_CAND)])
+
+    predicted = predicted + flip(predicted, 1) + (flip(predicted, 3) + flip(predicted, 2))
+    predicted = predicted + flip(predicted, 4)
     weighted = weights[:, None, :] * predicted.reshape(p, k, -1)
     weighted = weighted.reshape(p * k, -1).astype(jnp.bfloat16)
 
     streams = []
     for stream in range(STREAMS):
+        first, second = (X_SWAP, NEAR) if X_FIRST[stream] else (NEAR, X_SWAP)
         high = swap(product(me, weighted, held, True, (2, 3), stream), CORE_SWAP)
         high = high + product(me, weighted, held, False, (2, 3), stream)
-        near = swap(high, NEAR)
+        high = swap(high, first)
         low = swap(product(me, weighted, held, True, (0, 1), stream), CORE_SWAP)
         low = low + product(me, weighted, held, False, (0, 1), stream)
-        total = low[0] + near[0] + swap(low[1] + near[1], NEXT)
-        total = total + swap(total, FAR)
-        total = total + swap(total, X_SWAP)
-        low = jnp.stack([total, swap(total, NEXT)])
-        high = swap(low, NEAR)
+        total = low[0] + high[0] + swap(low[1] + high[1], second)
+        for pairs in SUMS[stream]:
+            total = total + swap(total, pairs)
+        low = jnp.stack([total, swap(total, second)])
+        high = swap(low, first)
         streams.append((low, high, swap(low, CORE_SWAP), swap(high, CORE_SWAP)))
     return assemble(me, streams, ncols).reshape(p, k, ncols)
 

time: 86.7 us -> 74.9 us (0.86)
  waiting for transfers between devices: 46.8 us -> 19.8 us
  starting transfers between devices: 28.5 us -> 43.2 us
    ppermute x10 -> x20, waiting for transfers between devices: 42.7 us -> 14.5 us  [swap(): return lax.ppermute(value, 'sens', pairs)]
    ppermute x10 -> x20, starting transfers between devices: 20.7 us -> 36.1 us  [swap(): return lax.ppermute(value, 'sens', pairs)]
    ppermute x3 -> x4, waiting for transfers between devices: 4.13 us -> 5.34 us  [flip(): return lax.ppermute(value, 'cand', [(c, c ^ bits) for c in range(N_CAND)])]
    ppermute x3 -> x4, starting transfers between devices: 7.84 us -> 7.12 us  [flip(): return lax.ppermute(value, 'cand', [(c, c ^ bits) for c in range(N_CAND)])]
    pallas_call x4 -> x8, Pallas kernels: 1.86 us -> 2.29 us  [product(): pl.pallas_call(kernel, in_specs=[SMEM, VMEM, VMEM], out_specs=VMEM, out_s...]
  transfers between devices with their start and end apart: 13 -> 24, of which waited for: 11 -> 12; matrix products, arithmetic and copies ran while one was open for 0% -> 0% of each run, Pallas kernels for 2% -> 3%
where the time goes in v3:
time: 74.9 us; the launch traced here: 74.8 us
  starting transfers between devices  43.2 us (58%)
  waiting for transfers between devices  19.8 us (26%)
  Pallas kernels  6.32 us (8%)
  local copies, waits for them, and re-layouts  4.98 us (7%)
    ppermute x20, starting transfers between devices, swap(): return lax.ppermute(value, 'sens', pairs)  36.1 us
    ppermute x20, waiting for transfers between devices, swap(): return lax.ppermute(value, 'sens', pairs)  14.5 us
    ppermute x4, starting transfers between devices, flip(): return lax.ppermute(value, 'cand', [(c, c ^ bits) for c in range(N_CAND)])  7.12 us
    ppermute x4, waiting for transfers between devices, flip(): return lax.ppermute(value, 'cand', [(c, c ^ bits) for c in range(N_CAND)])  5.34 us
    unnamed x8, local copies, waits for them, and re-layouts  4.98 us
    pallas_call x1, Pallas kernels, predict(): pl.pallas_call(predict_kernel, in_specs=[SMEM, VMEM, VMEM], out_specs=VME...  2.56 us
    pallas_call x8, Pallas kernels, product(): pl.pallas_call(kernel, in_specs=[SMEM, VMEM, VMEM], out_specs=VMEM, out_s...  2.29 us
  transfers between devices with their start and end apart: 24, of which 12 were waited for; matrix products, arithmetic and copies ran while one was open for 0% of the time, Pallas kernels for 3%

profile of v3, /device:TPU:1, one launch (start us, length us, event | category | flops | bytes accessed | tf_op | source)
XLA Modules:
  0.0 74.8 jit_solution(7103036025143564076)
XLA Ops:
  0.0 3.4 %copy-done = bf16[256,16384]{1,0:T(8,128)(2,1)S(1)} copy-done((bf16[256,16384]{1,0:T(8,128)(2,1)S(1)}, bf16[256,16384]{1,0:T(8,128)(2,1)}, u32[]{:S(2)}) %copy-start) | copy-done | bytes 8388632
  3.4 1.6 %copy-done.2 = f32[2,16,16384]{2,1,0:T(8,128)S(1)} copy-done((f32[2,16,16384]{2,1,0:T(8,128)S(1)}, f32[2,16,16384]{2,1,0:T(8,128)}, u32[]{:S(2)}) %copy-start.2) | copy-done | bytes 2097176
  5.0 2.6 %shard_map.37 = f32[32,256]{1,0:T(8,128)S(1)} custom-call(s32[1]{0:T(128)} %bitcast.me_ref, f32[32,16384]{1,0:T(8,128)S(1)} %bitcast.23, bf16[256,16384]{1,0:T(8,128)(2,1)S(1)} %copy-done), custom_call_target="tpu_custom_call" | custom-call | flops 268435456 | bytes 8388608 | tf_op jit(solution)/shard_map/pallas_call | solution.py:72
  7.5 3.8 %collective-permute-start.2 = (f32[32,256]{1,0:T(8,128)S(1)}, f32[32,256]{1,0:T(8,128)S(1)}, u32[]{:S(2)}, u32[]{:S(2)}) collective-permute-start(f32[32,256]{1,0:T(8,128)S(1)} %shard_map.37), channel_id=1, source_target_pairs={{0,2},{1,3},{2,0},{3,1},{4,6},{5,7},{6,4},{7,5},{8,10},{9,11},{10,... | collective-permute-start | bytes 98312 | tf_op jit(solution)/shard_map/ppermute | solution.py:147
  12.7 3.0 %collective-permute-done.1 = f32[32,256]{1,0:T(8,128)S(1)} collective-permute-done((f32[32,256]{1,0:T(8,128)S(1)}, f32[32,256]{1,0:T(8,128)S(1)}, u32[]{:S(2)}, u32[]{:S(2)}) %collective-permute-start.1) | collective-permute-done | bytes 32800 | tf_op jit(solution)/shard_map/ppermute | solution.py:147
  15.7 2.5 %collective-permute-start.3 = (f32[32,256]{1,0:T(8,128)S(1)}, f32[32,256]{1,0:T(8,128)S(1)}, u32[]{:S(2)}, u32[]{:S(2)}) collective-permute-start(f32[32,256]{1,0:T(8,128)S(1)} %add_add_fusion), channel_id=1, source_target_pairs={{0,4},{1,5},{2,6},{3,7},{4,0},{5,1},{6,2},{7,3},{8,12},{9,13},{10,... | collective-permute-start | bytes 98312 | tf_op jit(solution)/shard_map/ppermute | solution.py:147
  18.2 1.8 %collective-permute-done.3 = f32[32,256]{1,0:T(8,128)S(1)} collective-permute-done((f32[32,256]{1,0:T(8,128)S(1)}, f32[32,256]{1,0:T(8,128)S(1)}, u32[]{:S(2)}, u32[]{:S(2)}) %collective-permute-start.3) | collective-permute-done | bytes 32800 | tf_op jit(solution)/shard_map/ppermute | solution.py:147
  20.3 3.0 %collective-permute-start.5 = (f32[2,32,1024]{2,1,0:T(8,128)S(1)}, f32[2,32,1024]{2,1,0:T(8,128)S(1)}, u32[]{:S(2)}, u32[]{:S(2)}) collective-permute-start(f32[2,32,1024]{2,1,0:T(8,128)S(1)} %shard_map.40), channel_id=1, source_target_pairs={{0,8},{8,0},{16,24},{24,16},{32,40},{40,32},{48,56},{56,48},{64,72... | collective-permute-start | bytes 786440 | tf_op jit(solution)/shard_map/ppermute | solution.py:142
  25.3 5.7 %collective-permute-start.6 = (f32[2,32,1024]{2,1,0:T(8,128)S(1)}, f32[2,32,1024]{2,1,0:T(8,128)S(1)}, u32[]{:S(2)}, u32[]{:S(2)}) collective-permute-start(f32[2,32,1024]{2,1,0:T(8,128)S(1)} %add.71), channel_id=1, source_target_pairs={{0,16},{8,120},{16,0},{24,40},{32,48},{40,24},{48,32},{56,72},{64,... | collective-permute-start | bytes 786440 | tf_op jit(solution)/shard_map/ppermute | solution.py:142
  32.0 2.6 %collective-permute-done.6 = f32[2,32,1024]{2,1,0:T(8,128)S(1)} collective-permute-done((f32[2,32,1024]{2,1,0:T(8,128)S(1)}, f32[2,32,1024]{2,1,0:T(8,128)S(1)}, u32[]{:S(2)}, u32[]{:S(2)}) %collective-permute-start.6) | collective-permute-done | bytes 262176 | tf_op jit(solution)/shard_map/ppermute | solution.py:142
  34.7 1.3 %collective-permute-start.7 = (f32[32,1024]{1,0:T(8,128)S(1)}, f32[32,1024]{1,0:T(8,128)S(1)}, u32[]{:S(2)}, u32[]{:S(2)}) collective-permute-start(f32[32,1024]{1,0:T(8,128)S(1)} %fusion.3), channel_id=1, source_target_pairs={{0,128},{8,136},{16,144},{24,152},{32,160},{40,168},{48,176},{56,1... | collective-permute-start | bytes 393224 | tf_op jit(solution)/shard_map/ppermute | solution.py:142
  36.0 1.8 %collective-permute-done.16 = f32[2,32,1024]{2,1,0:T(8,128)S(1)} collective-permute-done((f32[2,32,1024]{2,1,0:T(8,128)S(1)}, f32[2,32,1024]{2,1,0:T(8,128)S(1)}, u32[]{:S(2)}, u32[]{:S(2)}) %collective-permute-start.16) | collective-permute-done | bytes 262176 | tf_op jit(solution)/shard_map/ppermute | solution.py:142
  37.8 1.3 %collective-permute-start.17 = (f32[32,1024]{1,0:T(8,128)S(1)}, f32[32,1024]{1,0:T(8,128)S(1)}, u32[]{:S(2)}, u32[]{:S(2)}) collective-permute-start(f32[32,1024]{1,0:T(8,128)S(1)} %fusion), channel_id=1, source_target_pairs={{0,128},{8,136},{16,144},{24,152},{32,160},{40,168},{48,176},{56,1... | collective-permute-start | bytes 393224 | tf_op jit(solution)/shard_map/ppermute | solution.py:142
  39.7 1.9 %collective-permute-start.8 = (f32[32,1024]{1,0:T(8,128)S(1)}, f32[32,1024]{1,0:T(8,128)S(1)}, u32[]{:S(2)}, u32[]{:S(2)}) collective-permute-start(f32[32,1024]{1,0:T(8,128)S(1)} %fusion.5), channel_id=1, source_target_pairs={{0,48},{8,88},{16,96},{24,72},{32,80},{40,120},{48,0},{56,104},{64... | collective-permute-start | bytes 393224 | tf_op jit(solution)/shard_map/ppermute | solution.py:142
  41.7 2.3 %collective-permute-start.18 = (f32[32,1024]{1,0:T(8,128)S(1)}, f32[32,1024]{1,0:T(8,128)S(1)}, u32[]{:S(2)}, u32[]{:S(2)}) collective-permute-start(f32[32,1024]{1,0:T(8,128)S(1)} %fusion.2), channel_id=1, source_target_pairs={{0,112},{8,24},{16,32},{24,8},{32,16},{40,56},{48,64},{56,40},{64,... | collective-permute-start | bytes 393224 | tf_op jit(solution)/shard_map/ppermute | solution.py:142
  44.1 4.2 %collective-permute-done.8 = f32[32,1024]{1,0:T(8,128)S(1)} collective-permute-done((f32[32,1024]{1,0:T(8,128)S(1)}, f32[32,1024]{1,0:T(8,128)S(1)}, u32[]{:S(2)}, u32[]{:S(2)}) %collective-permute-start.8) | collective-permute-done | bytes 131104 | tf_op jit(solution)/shard_map/ppermute | solution.py:142
  48.6 4.0 %collective-permute-start.19 = (f32[32,1024]{1,0:T(8,128)S(1)}, f32[32,1024]{1,0:T(8,128)S(1)}, u32[]{:S(2)}, u32[]{:S(2)}) collective-permute-start(f32[32,1024]{1,0:T(8,128)S(1)} %add.86), channel_id=1, source_target_pairs={{0,48},{8,88},{16,96},{24,72},{32,80},{40,120},{48,0},{56,104},{64... | collective-permute-start | bytes 393224 | tf_op jit(solution)/shard_map/ppermute | solution.py:142
  52.7 1.4 %collective-permute-start.10 = (f32[32,1024]{1,0:T(8,128)S(1)}, f32[32,1024]{1,0:T(8,128)S(1)}, u32[]{:S(2)}, u32[]{:S(2)}) collective-permute-start(f32[32,1024]{1,0:T(8,128)S(1)} %add.78), channel_id=1, source_target_pairs={{0,128},{8,136},{16,144},{24,152},{32,160},{40,168},{48,176},{56,1... | collective-permute-start | bytes 393224 | tf_op jit(solution)/shard_map/ppermute | solution.py:142
  54.1 2.5 %collective-permute-done.19 = f32[32,1024]{1,0:T(8,128)S(1)} collective-permute-done((f32[32,1024]{1,0:T(8,128)S(1)}, f32[32,1024]{1,0:T(8,128)S(1)}, u32[]{:S(2)}, u32[]{:S(2)}) %collective-permute-start.19) | collective-permute-done | bytes 131104 | tf_op jit(solution)/shard_map/ppermute | solution.py:142
  57.6 4.7 %collective-permute-start.11 = (f32[2,32,1024]{2,1,0:T(8,128)S(1)}, f32[2,32,1024]{2,1,0:T(8,128)S(1)}, u32[]{:S(2)}, u32[]{:S(2)}) collective-permute-start(f32[2,32,1024]{2,1,0:T(8,128)S(1)} %pad_maximum_fusion.refs_0_), channel_id=1, source_target_pairs={{0,16},{8,120},{16,0},{24,40},{32,48},{40,24},{48,32},{56,72},{64,... | collective-permute-start | bytes 786440 | tf_op jit(solution)/shard_map/ppermute | solution.py:142
  62.4 4.2 %collective-permute-start.21 = (f32[2,32,1024]{2,1,0:T(8,128)S(1)}, f32[2,32,1024]{2,1,0:T(8,128)S(1)}, u32[]{:S(2)}, u32[]{:S(2)}) collective-permute-start(f32[2,32,1024]{2,1,0:T(8,128)S(1)} %pad_maximum_fusion.1.refs_4_), channel_id=1, source_target_pairs={{0,16},{8,120},{16,0},{24,40},{32,48},{40,24},{48,32},{56,72},{64,... | collective-permute-start | bytes 786440 | tf_op jit(solution)/shard_map/ppermute | solution.py:142
  67.8 1.3 %collective-permute-start.13 = (f32[2,32,1024]{2,1,0:T(8,128)S(1)}, f32[2,32,1024]{2,1,0:T(8,128)S(1)}, u32[]{:S(2)}, u32[]{:S(2)}) collective-permute-start(f32[2,32,1024]{2,1,0:T(8,128)S(1)} %collective-permute-done.11.refs_1_), channel_id=1, source_target_pairs={{0,8},{8,0},{16,24},{24,16},{32,40},{40,32},{48,56},{56,48},{64,72... | collective-permute-start | bytes 786440 | tf_op jit(solution)/shard_map/ppermute | solution.py:142
  70.4 1.8 %collective-permute-start.23 = (f32[2,32,1024]{2,1,0:T(8,128)S(1)}, f32[2,32,1024]{2,1,0:T(8,128)S(1)}, u32[]{:S(2)}, u32[]{:S(2)}) collective-permute-start(f32[2,32,1024]{2,1,0:T(8,128)S(1)} %collective-permute-done.21.refs_5_), channel_id=1, source_target_pairs={{0,8},{8,0},{16,24},{24,16},{32,40},{40,32},{48,56},{56,48},{64,72... | collective-permute-start | bytes 786440 | tf_op jit(solution)/shard_map/ppermute | solution.py:142
  73.3 1.5 %shard_map.46 = f32[32,16384]{1,0:T(8,128)} custom-call(s32[1]{0:T(128)} %bitcast.me_ref, f32[2,32,1024]{2,1,0:T(8,128)S(1)} %pad_maximum_fusion.refs_0_, f32[2,32,1024]{2,1,0:T(8,128)S(1)} %collective-permute-done.11.refs_1_, f32[2,32,1024]{2,1,0:T(8,128)S(1)} %collective-permute-done.12.refs_2_, f32[2,32,1024]{2,1,0:T(8,128)S(1)} %collective-permute-done.13.refs_3_, ...), custom_call_target="tpu_custom_call" | custom-call | tf_op jit(solution)/shard_map/pallas_call | solution.py:128
  (58 shorter events, 10.4 us)
Async XLA Ops:
  7.5 5.1 %collective-permute-start.2 = (f32[32,256]{1,0:T(8,128)S(1)}, f32[32,256]{1,0:T(8,128)S(1)}, u32[]{:S(2)}, u32[]{:S(2)}) collective-permute-start(f32[32,256]{1,0:T(8,128)S(1)} %shard_map.37), channel_id=1, source_target_pairs={{0,2},{1,3},{2,0},{3,1},{4,6},{5,7},{6,4},{7,5},{8,10},{9,11},{10,... | collective-permute-start | bytes 98312 | tf_op jit(solution)/shard_map/ppermute | solution.py:147
  11.4 4.3 %collective-permute-start.1 = (f32[32,256]{1,0:T(8,128)S(1)}, f32[32,256]{1,0:T(8,128)S(1)}, u32[]{:S(2)}, u32[]{:S(2)}) collective-permute-start(f32[32,256]{1,0:T(8,128)S(1)} %shard_map.37), channel_id=1, source_target_pairs={{0,3},{1,2},{2,1},{3,0},{4,7},{5,6},{6,5},{7,4},{8,11},{9,10},{10,... | collective-permute-start | bytes 98312 | tf_op jit(solution)/shard_map/ppermute | solution.py:147
  12.1 3.5 %collective-permute-start = (f32[32,256]{1,0:T(8,128)S(1)}, f32[32,256]{1,0:T(8,128)S(1)}, u32[]{:S(2)}, u32[]{:S(2)}) collective-permute-start(f32[32,256]{1,0:T(8,128)S(1)} %shard_map.37), channel_id=1, source_target_pairs={{0,1},{1,0},{2,3},{3,2},{4,5},{5,4},{6,7},{7,6},{8,9},{9,8},{10,11... | collective-permute-start | bytes 98312 | tf_op jit(solution)/shard_map/ppermute | solution.py:147
  15.7 4.4 %collective-permute-start.3 = (f32[32,256]{1,0:T(8,128)S(1)}, f32[32,256]{1,0:T(8,128)S(1)}, u32[]{:S(2)}, u32[]{:S(2)}) collective-permute-start(f32[32,256]{1,0:T(8,128)S(1)} %add_add_fusion), channel_id=1, source_target_pairs={{0,4},{1,5},{2,6},{3,7},{4,0},{5,1},{6,2},{7,3},{8,12},{9,13},{10,... | collective-permute-start | bytes 98312 | tf_op jit(solution)/shard_map/ppermute | solution.py:147
  20.3 4.9 %collective-permute-start.5 = (f32[2,32,1024]{2,1,0:T(8,128)S(1)}, f32[2,32,1024]{2,1,0:T(8,128)S(1)}, u32[]{:S(2)}, u32[]{:S(2)}) collective-permute-start(f32[2,32,1024]{2,1,0:T(8,128)S(1)} %shard_map.40), channel_id=1, source_target_pairs={{0,8},{8,0},{16,24},{24,16},{32,40},{40,32},{48,56},{56,48},{64,72... | collective-permute-start | bytes 786440 | tf_op jit(solution)/shard_map/ppermute | solution.py:142
  23.6 7.6 %collective-permute-start.15 = (f32[2,32,1024]{2,1,0:T(8,128)S(1)}, f32[2,32,1024]{2,1,0:T(8,128)S(1)}, u32[]{:S(2)}, u32[]{:S(2)}) collective-permute-start(f32[2,32,1024]{2,1,0:T(8,128)S(1)} %shard_map.44), channel_id=1, source_target_pairs={{0,8},{8,0},{16,24},{24,16},{32,40},{40,32},{48,56},{56,48},{64,72... | collective-permute-start | bytes 786440 | tf_op jit(solution)/shard_map/ppermute | solution.py:142
  24.6 7.4 %collective-permute-start.4 = (f32[2,32,1024]{2,1,0:T(8,128)S(1)}, f32[2,32,1024]{2,1,0:T(8,128)S(1)}, u32[]{:S(2)}, u32[]{:S(2)}) collective-permute-start(f32[2,32,1024]{2,1,0:T(8,128)S(1)} %shard_map.38), channel_id=1, source_target_pairs={{0,8},{8,0},{16,24},{24,16},{32,40},{40,32},{48,56},{56,48},{64,72... | collective-permute-start | bytes 786440 | tf_op jit(solution)/shard_map/ppermute | solution.py:142
  25.1 6.9 %collective-permute-start.14 = (f32[2,32,1024]{2,1,0:T(8,128)S(1)}, f32[2,32,1024]{2,1,0:T(8,128)S(1)}, u32[]{:S(2)}, u32[]{:S(2)}) collective-permute-start(f32[2,32,1024]{2,1,0:T(8,128)S(1)} %shard_map.42), channel_id=1, source_target_pairs={{0,8},{8,0},{16,24},{24,16},{32,40},{40,32},{48,56},{56,48},{64,72... | collective-permute-start | bytes 786440 | tf_op jit(solution)/shard_map/ppermute | solution.py:142
  25.3 9.4 %collective-permute-start.6 = (f32[2,32,1024]{2,1,0:T(8,128)S(1)}, f32[2,32,1024]{2,1,0:T(8,128)S(1)}, u32[]{:S(2)}, u32[]{:S(2)}) collective-permute-start(f32[2,32,1024]{2,1,0:T(8,128)S(1)} %add.71), channel_id=1, source_target_pairs={{0,16},{8,120},{16,0},{24,40},{32,48},{40,24},{48,32},{56,72},{64,... | collective-permute-start | bytes 786440 | tf_op jit(solution)/shard_map/ppermute | solution.py:142
  31.3 6.5 %collective-permute-start.16 = (f32[2,32,1024]{2,1,0:T(8,128)S(1)}, f32[2,32,1024]{2,1,0:T(8,128)S(1)}, u32[]{:S(2)}, u32[]{:S(2)}) collective-permute-start(f32[2,32,1024]{2,1,0:T(8,128)S(1)} %add.80), channel_id=1, source_target_pairs={{0,16},{8,120},{16,0},{24,40},{32,48},{40,24},{48,32},{56,72},{64,... | collective-permute-start | bytes 786440 | tf_op jit(solution)/shard_map/ppermute | solution.py:142
  34.7 4.9 %collective-permute-start.7 = (f32[32,1024]{1,0:T(8,128)S(1)}, f32[32,1024]{1,0:T(8,128)S(1)}, u32[]{:S(2)}, u32[]{:S(2)}) collective-permute-start(f32[32,1024]{1,0:T(8,128)S(1)} %fusion.3), channel_id=1, source_target_pairs={{0,128},{8,136},{16,144},{24,152},{32,160},{40,168},{48,176},{56,1... | collective-permute-start | bytes 393224 | tf_op jit(solution)/shard_map/ppermute | solution.py:142
  37.8 3.9 %collective-permute-start.17 = (f32[32,1024]{1,0:T(8,128)S(1)}, f32[32,1024]{1,0:T(8,128)S(1)}, u32[]{:S(2)}, u32[]{:S(2)}) collective-permute-start(f32[32,1024]{1,0:T(8,128)S(1)} %fusion), channel_id=1, source_target_pairs={{0,128},{8,136},{16,144},{24,152},{32,160},{40,168},{48,176},{56,1... | collective-permute-start | bytes 393224 | tf_op jit(solution)/shard_map/ppermute | solution.py:142
  39.7 8.6 %collective-permute-start.8 = (f32[32,1024]{1,0:T(8,128)S(1)}, f32[32,1024]{1,0:T(8,128)S(1)}, u32[]{:S(2)}, u32[]{:S(2)}) collective-permute-start(f32[32,1024]{1,0:T(8,128)S(1)} %fusion.5), channel_id=1, source_target_pairs={{0,48},{8,88},{16,96},{24,72},{32,80},{40,120},{48,0},{56,104},{64... | collective-permute-start | bytes 393224 | tf_op jit(solution)/shard_map/ppermute | solution.py:142
  41.7 6.9 %collective-permute-start.18 = (f32[32,1024]{1,0:T(8,128)S(1)}, f32[32,1024]{1,0:T(8,128)S(1)}, u32[]{:S(2)}, u32[]{:S(2)}) collective-permute-start(f32[32,1024]{1,0:T(8,128)S(1)} %fusion.2), channel_id=1, source_target_pairs={{0,112},{8,24},{16,32},{24,8},{32,16},{40,56},{48,64},{56,40},{64,... | collective-permute-start | bytes 393224 | tf_op jit(solution)/shard_map/ppermute | solution.py:142
  48.3 4.4 %collective-permute-start.9 = (f32[32,1024]{1,0:T(8,128)S(1)}, f32[32,1024]{1,0:T(8,128)S(1)}, u32[]{:S(2)}, u32[]{:S(2)}) collective-permute-start(f32[32,1024]{1,0:T(8,128)S(1)} %add.77), channel_id=1, source_target_pairs={{0,112},{8,24},{16,32},{24,8},{32,16},{40,56},{48,64},{56,40},{64,... | collective-permute-start | bytes 393224 | tf_op jit(solution)/shard_map/ppermute | solution.py:142
  48.6 7.9 %collective-permute-start.19 = (f32[32,1024]{1,0:T(8,128)S(1)}, f32[32,1024]{1,0:T(8,128)S(1)}, u32[]{:S(2)}, u32[]{:S(2)}) collective-permute-start(f32[32,1024]{1,0:T(8,128)S(1)} %add.86), channel_id=1, source_target_pairs={{0,48},{8,88},{16,96},{24,72},{32,80},{40,120},{48,0},{56,104},{64... | collective-permute-start | bytes 393224 | tf_op jit(solution)/shard_map/ppermute | solution.py:142
  52.7 4.9 %collective-permute-start.10 = (f32[32,1024]{1,0:T(8,128)S(1)}, f32[32,1024]{1,0:T(8,128)S(1)}, u32[]{:S(2)}, u32[]{:S(2)}) collective-permute-start(f32[32,1024]{1,0:T(8,128)S(1)} %add.78), channel_id=1, source_target_pairs={{0,128},{8,136},{16,144},{24,152},{32,160},{40,168},{48,176},{56,1... | collective-permute-start | bytes 393224 | tf_op jit(solution)/shard_map/ppermute | solution.py:142
  56.6 5.8 %collective-permute-start.20 = (f32[32,1024]{1,0:T(8,128)S(1)}, f32[32,1024]{1,0:T(8,128)S(1)}, u32[]{:S(2)}, u32[]{:S(2)}) collective-permute-start(f32[32,1024]{1,0:T(8,128)S(1)} %add.87), channel_id=1, source_target_pairs={{0,128},{8,136},{16,144},{24,152},{32,160},{40,168},{48,176},{56,1... | collective-permute-start | bytes 393224 | tf_op jit(solution)/shard_map/ppermute | solution.py:142
  57.6 10.1 %collective-permute-start.11 = (f32[2,32,1024]{2,1,0:T(8,128)S(1)}, f32[2,32,1024]{2,1,0:T(8,128)S(1)}, u32[]{:S(2)}, u32[]{:S(2)}) collective-permute-start(f32[2,32,1024]{2,1,0:T(8,128)S(1)} %pad_maximum_fusion.refs_0_), channel_id=1, source_target_pairs={{0,16},{8,120},{16,0},{24,40},{32,48},{40,24},{48,32},{56,72},{64,... | collective-permute-start | bytes 786440 | tf_op jit(solution)/shard_map/ppermute | solution.py:142
  62.4 8.0 %collective-permute-start.21 = (f32[2,32,1024]{2,1,0:T(8,128)S(1)}, f32[2,32,1024]{2,1,0:T(8,128)S(1)}, u32[]{:S(2)}, u32[]{:S(2)}) collective-permute-start(f32[2,32,1024]{2,1,0:T(8,128)S(1)} %pad_maximum_fusion.1.refs_4_), channel_id=1, source_target_pairs={{0,16},{8,120},{16,0},{24,40},{32,48},{40,24},{48,32},{56,72},{64,... | collective-permute-start | bytes 786440 | tf_op jit(solution)/shard_map/ppermute | solution.py:142
  66.6 5.5 %collective-permute-start.12 = (f32[2,32,1024]{2,1,0:T(8,128)S(1)}, f32[2,32,1024]{2,1,0:T(8,128)S(1)}, u32[]{:S(2)}, u32[]{:S(2)}) collective-permute-start(f32[2,32,1024]{2,1,0:T(8,128)S(1)} %pad_maximum_fusion.refs_0_), channel_id=1, source_target_pairs={{0,8},{8,0},{16,24},{24,16},{32,40},{40,32},{48,56},{56,48},{64,72... | collective-permute-start | bytes 786440 | tf_op jit(solution)/shard_map/ppermute | solution.py:142
  67.8 4.4 %collective-permute-start.22 = (f32[2,32,1024]{2,1,0:T(8,128)S(1)}, f32[2,32,1024]{2,1,0:T(8,128)S(1)}, u32[]{:S(2)}, u32[]{:S(2)}) collective-permute-start(f32[2,32,1024]{2,1,0:T(8,128)S(1)} %pad_maximum_fusion.1.refs_4_), channel_id=1, source_target_pairs={{0,8},{8,0},{16,24},{24,16},{32,40},{40,32},{48,56},{56,48},{64,72... | collective-permute-start | bytes 786440 | tf_op jit(solution)/shard_map/ppermute | solution.py:142
  67.8 4.4 %collective-permute-start.13 = (f32[2,32,1024]{2,1,0:T(8,128)S(1)}, f32[2,32,1024]{2,1,0:T(8,128)S(1)}, u32[]{:S(2)}, u32[]{:S(2)}) collective-permute-start(f32[2,32,1024]{2,1,0:T(8,128)S(1)} %collective-permute-done.11.refs_1_), channel_id=1, source_target_pairs={{0,8},{8,0},{16,24},{24,16},{32,40},{40,32},{48,56},{56,48},{64,72... | collective-permute-start | bytes 786440 | tf_op jit(solution)/shard_map/ppermute | solution.py:142
  70.4 2.9 %collective-permute-start.23 = (f32[2,32,1024]{2,1,0:T(8,128)S(1)}, f32[2,32,1024]{2,1,0:T(8,128)S(1)}, u32[]{:S(2)}, u32[]{:S(2)}) collective-permute-start(f32[2,32,1024]{2,1,0:T(8,128)S(1)} %collective-permute-done.21.refs_5_), channel_id=1, source_target_pairs={{0,8},{8,0},{16,24},{24,16},{32,40},{40,32},{48,56},{56,48},{64,72... | collective-permute-start | bytes 786440 | tf_op jit(solution)/shard_map/ppermute | solution.py:142
  (4 other events, 35.1 us)

commit v4 on v3

--- a/solution.py
+++ b/solution.py
@@ -52,18 +52,39 @@
     return pl.ds(pl.multiple_of(block * width, width), width)
 
 
-def predict_kernel(me_ref, blocks_ref, jac_ref, out_ref):
+def predict_kernel(
+    me_ref, blocks_ref, jac_ref, out_ref, held_ref, blocks_buf, blocks_sem, jac_sem
+):
     width = jac_ref.shape[1] // STEPS
-    total = jnp.zeros(out_ref.shape, jnp.float32)
+
+    def columns(step):
+        return pl.ds(pl.multiple_of(step * width, width), width)
+
+    def copies(step):
+        cols = columns(step)
+        return (
+            pltpu.make_async_copy(
+                blocks_ref.at[:, cols], blocks_buf.at[:, cols], blocks_sem.at[step]
+            ),
+            pltpu.make_async_copy(jac_ref.at[:, cols], held_ref.at[:, cols], jac_sem.at[step]),
+        )
+
     for step in range(STEPS):
-        cols = slice(step * width, (step + 1) * width)
-        total += lax.dot_general(
-            blocks_ref[:, cols].astype(jnp.bfloat16),
-            jac_ref[:, cols],
+        for copy in copies(step):
+            copy.start()
+
+    def add(step, total):
+        for copy in copies(step):
+            copy.wait()
+        cols = columns(step)
+        return total + lax.dot_general(
+            blocks_buf[:, cols].astype(jnp.bfloat16),
+            held_ref[:, cols],
             (((1,), (1,)), ((), ())),
             preferred_element_type=jnp.float32,
         )
-    out_ref[...] = total
+
+    out_ref[...] = lax.fori_loop(0, STEPS, add, jnp.zeros(out_ref.shape, jnp.float32))
 
 
 def predict(me, blocks, jacobian):
@@ -71,10 +92,18 @@
     rows = jacobian.shape[0]
     return pl.pallas_call(
         predict_kernel,
-        in_specs=[SMEM, VMEM, VMEM],
-        out_specs=VMEM,
-        out_shape=jax.ShapeDtypeStruct((k, rows), jnp.float32),
-        compiler_params=pltpu.CompilerParams(vmem_limit_bytes=24 * MIB),
+        in_specs=[SMEM, HBM, HBM],
+        out_specs=[VMEM, VMEM],
+        out_shape=[
+            pltpu.VMEM((k, rows), jnp.float32),
+            pltpu.VMEM(jacobian.shape, jacobian.dtype),
+        ],
+        scratch_shapes=[
+            pltpu.VMEM((k, ncols), jnp.float32),
+            pltpu.SemaphoreType.DMA((STEPS,)),
+            pltpu.SemaphoreType.DMA((STEPS,)),
+        ],
+        compiler_params=pltpu.CompilerParams(vmem_limit_bytes=48 * MIB),
         cost_estimate=pl.CostEstimate(
             flops=2 * k * ncols * rows, bytes_accessed=2 * rows * ncols, transcendentals=0
         ),
@@ -141,8 +170,7 @@
     def swap(value, pairs):
         return lax.ppermute(value, "sens", pairs)
 
-    predicted = predict(me, blocks.reshape(p * k, ncols), jacobian)
-    held = jacobian
+    predicted, held = predict(me, blocks.reshape(p * k, ncols), jacobian)
     def flip(value, bits):
         return lax.ppermute(value, "cand", [(c, c ^ bits) for c in range(N_CAND)])
 
@@ -162,8 +190,10 @@
         total = low[0] + high[0] + swap(low[1] + high[1], second)
         for pairs in SUMS[stream]:
             total = total + swap(total, pairs)
-        low = jnp.stack([total, swap(total, second)])
-        high = swap(low, first)
+        own = swap(total, first)
+        other = swap(total, second)
+        low = jnp.stack([total, other])
+        high = jnp.stack([own, swap(other, first)])
         streams.append((low, high, swap(low, CORE_SWAP), swap(high, CORE_SWAP)))
     return assemble(me, streams, ncols).reshape(p, k, ncols)
 

time: 74.9 us -> 72 us (0.961)
  local copies, waits for them, and re-layouts: 4.98 us -> 0.01 us
  starting transfers between devices: 43.2 us -> 39.4 us
  waiting for transfers between devices: 19.8 us -> 23.3 us
  Pallas kernels: 6.32 us -> 8.64 us
    unnamed x8 -> x2, local copies, waits for them, and re-layouts: 4.98 us -> 0.01 us
    ppermute x20 -> x22, starting transfers between devices: 36.1 us -> 31.8 us  [swap(): return lax.ppermute(value, 'sens', pairs)]
    ppermute x20 -> x22, waiting for transfers between devices: 14.5 us -> 18.2 us  [swap(): return lax.ppermute(value, 'sens', pairs)]
    pallas_call x1, Pallas kernels: 2.56 us -> 4.87 us  [predict(): pl.pallas_call(predict_kernel, in_specs=[SMEM, HBM, HBM], out_specs=[VMEM...]
  transfers between devices with their start and end apart: 24 -> 26, of which waited for: 12 -> 12; matrix products, arithmetic and copies ran while one was open for 0% -> 0% of each run, Pallas kernels for 3% -> 3%
where the time goes in v4:
time: 72 us; the launch traced here: 71.9 us
  starting transfers between devices  39.4 us (55%)
  waiting for transfers between devices  23.3 us (32%)
  Pallas kernels  8.64 us (12%)
    ppermute x22, starting transfers between devices, swap(): return lax.ppermute(value, 'sens', pairs)  31.8 us
    ppermute x22, waiting for transfers between devices, swap(): return lax.ppermute(value, 'sens', pairs)  18.2 us
    ppermute x4, starting transfers between devices, flip(): return lax.ppermute(value, 'cand', [(c, c ^ bits) for c in range(N_CAND)])  7.67 us
    ppermute x4, waiting for transfers between devices, flip(): return lax.ppermute(value, 'cand', [(c, c ^ bits) for c in range(N_CAND)])  5.07 us
    pallas_call x1, Pallas kernels, predict(): pl.pallas_call(predict_kernel, in_specs=[SMEM, HBM, HBM], out_specs=[VMEM...  4.87 us
    pallas_call x8, Pallas kernels, product(): pl.pallas_call(kernel, in_specs=[SMEM, VMEM, VMEM], out_specs=VMEM, out_s...  2.3 us
    pallas_call x1, Pallas kernels, assemble(): pl.pallas_call(kernel, in_specs=[SMEM] + [VMEM] * len(operands), out_spec...  1.47 us
  transfers between devices with their start and end apart: 26, of which 12 were waited for; matrix products, arithmetic and copies ran while one was open for 0% of the time, Pallas kernels for 3%

profile of v4, /device:TPU:1, one launch (start us, length us, event | category | flops | bytes accessed | tf_op | source)
XLA Modules:
  0.0 71.9 jit_solution(1295772746622087331)
XLA Ops:
  0.0 4.9 %shard_map.37 = (f32[32,256]{1,0:T(8,128)S(1)}, bf16[256,16384]{1,0:T(8,128)(2,1)S(1)}) custom-call(s32[1]{0:T(128)} %bitcast.me_ref, f32[32,16384]{1,0:T(8,128)} %bitcast.27, bf16[256,16384]{1,0:T(8,128)(2,1)} %jac_ref.1), custom_call_target="tpu_custom_call" | custom-call | flops 268435456 | bytes 8388608 | tf_op jit(solution)/shard_map/pallas_call | solution.py:93
  4.9 2.2 %collective-permute-start = (f32[32,256]{1,0:T(8,128)S(1)}, f32[32,256]{1,0:T(8,128)S(1)}, u32[]{:S(2)}, u32[]{:S(2)}) collective-permute-start(f32[32,256]{1,0:T(8,128)S(1)} %get-tuple-element.7), channel_id=1, source_target_pairs={{0,1},{1,0},{2,3},{3,2},{4,5},{5,4},{6,7},{7,6},{8,9},{9,8},{10,11... | collective-permute-start | bytes 98312 | tf_op jit(solution)/shard_map/ppermute | solution.py:175
  7.1 1.9 %collective-permute-start.1 = (f32[32,256]{1,0:T(8,128)S(1)}, f32[32,256]{1,0:T(8,128)S(1)}, u32[]{:S(2)}, u32[]{:S(2)}) collective-permute-start(f32[32,256]{1,0:T(8,128)S(1)} %get-tuple-element.7), channel_id=1, source_target_pairs={{0,3},{1,2},{2,1},{3,0},{4,7},{5,6},{6,5},{7,4},{8,11},{9,10},{10,... | collective-permute-start | bytes 98312 | tf_op jit(solution)/shard_map/ppermute | solution.py:175
  9.7 1.3 %collective-permute-done.1 = f32[32,256]{1,0:T(8,128)S(1)} collective-permute-done((f32[32,256]{1,0:T(8,128)S(1)}, f32[32,256]{1,0:T(8,128)S(1)}, u32[]{:S(2)}, u32[]{:S(2)}) %collective-permute-start.1) | collective-permute-done | bytes 32800 | tf_op jit(solution)/shard_map/ppermute | solution.py:175
  11.1 2.2 %collective-permute-done.2 = f32[32,256]{1,0:T(8,128)S(1)} collective-permute-done((f32[32,256]{1,0:T(8,128)S(1)}, f32[32,256]{1,0:T(8,128)S(1)}, u32[]{:S(2)}, u32[]{:S(2)}) %collective-permute-start.2) | collective-permute-done | bytes 32800 | tf_op jit(solution)/shard_map/ppermute | solution.py:175
  13.3 2.8 %collective-permute-start.3 = (f32[32,256]{1,0:T(8,128)S(1)}, f32[32,256]{1,0:T(8,128)S(1)}, u32[]{:S(2)}, u32[]{:S(2)}) collective-permute-start(f32[32,256]{1,0:T(8,128)S(1)} %add_add_fusion), channel_id=1, source_target_pairs={{0,4},{1,5},{2,6},{3,7},{4,0},{5,1},{6,2},{7,3},{8,12},{9,13},{10,... | collective-permute-start | bytes 98312 | tf_op jit(solution)/shard_map/ppermute | solution.py:175
  16.1 1.5 %collective-permute-done.3 = f32[32,256]{1,0:T(8,128)S(1)} collective-permute-done((f32[32,256]{1,0:T(8,128)S(1)}, f32[32,256]{1,0:T(8,128)S(1)}, u32[]{:S(2)}, u32[]{:S(2)}) %collective-permute-start.3) | collective-permute-done | bytes 32800 | tf_op jit(solution)/shard_map/ppermute | solution.py:175
  18.0 3.6 %collective-permute-start.16 = (f32[2,32,1024]{2,1,0:T(8,128)S(1)}, f32[2,32,1024]{2,1,0:T(8,128)S(1)}, u32[]{:S(2)}, u32[]{:S(2)}) collective-permute-start(f32[2,32,1024]{2,1,0:T(8,128)S(1)} %shard_map.44), channel_id=1, source_target_pairs={{0,8},{8,0},{16,24},{24,16},{32,40},{40,32},{48,56},{56,48},{64,72... | collective-permute-start | bytes 786440 | tf_op jit(solution)/shard_map/ppermute | solution.py:171
  23.5 5.7 %collective-permute-start.17 = (f32[2,32,1024]{2,1,0:T(8,128)S(1)}, f32[2,32,1024]{2,1,0:T(8,128)S(1)}, u32[]{:S(2)}, u32[]{:S(2)}) collective-permute-start(f32[2,32,1024]{2,1,0:T(8,128)S(1)} %add.80), channel_id=1, source_target_pairs={{0,16},{8,120},{16,0},{24,40},{32,48},{40,24},{48,32},{56,72},{64,... | collective-permute-start | bytes 786440 | tf_op jit(solution)/shard_map/ppermute | solution.py:171
  30.2 2.6 %collective-permute-done.17 = f32[2,32,1024]{2,1,0:T(8,128)S(1)} collective-permute-done((f32[2,32,1024]{2,1,0:T(8,128)S(1)}, f32[2,32,1024]{2,1,0:T(8,128)S(1)}, u32[]{:S(2)}, u32[]{:S(2)}) %collective-permute-start.17) | collective-permute-done | bytes 262176 | tf_op jit(solution)/shard_map/ppermute | solution.py:171
  34.2 1.8 %collective-permute-done.6 = f32[2,32,1024]{2,1,0:T(8,128)S(1)} collective-permute-done((f32[2,32,1024]{2,1,0:T(8,128)S(1)}, f32[2,32,1024]{2,1,0:T(8,128)S(1)}, u32[]{:S(2)}, u32[]{:S(2)}) %collective-permute-start.6) | collective-permute-done | bytes 262176 | tf_op jit(solution)/shard_map/ppermute | solution.py:171
  38.0 1.9 %collective-permute-done.7 = f32[32,1024]{1,0:T(8,128)S(1)} collective-permute-done((f32[32,1024]{1,0:T(8,128)S(1)}, f32[32,1024]{1,0:T(8,128)S(1)}, u32[]{:S(2)}, u32[]{:S(2)}) %collective-permute-start.7) | collective-permute-done | bytes 131104 | tf_op jit(solution)/shard_map/ppermute | solution.py:171
  39.9 2.8 %collective-permute-start.8 = (f32[32,1024]{1,0:T(8,128)S(1)}, f32[32,1024]{1,0:T(8,128)S(1)}, u32[]{:S(2)}, u32[]{:S(2)}) collective-permute-start(f32[32,1024]{1,0:T(8,128)S(1)} %fusion.5), channel_id=1, source_target_pairs={{0,48},{8,88},{16,96},{24,72},{32,80},{40,120},{48,0},{56,104},{64... | collective-permute-start | bytes 393224 | tf_op jit(solution)/shard_map/ppermute | solution.py:171
  42.7 1.9 %collective-permute-start.20 = (f32[32,1024]{1,0:T(8,128)S(1)}, f32[32,1024]{1,0:T(8,128)S(1)}, u32[]{:S(2)}, u32[]{:S(2)}) collective-permute-start(f32[32,1024]{1,0:T(8,128)S(1)} %add.86), channel_id=1, source_target_pairs={{0,48},{8,88},{16,96},{24,72},{32,80},{40,120},{48,0},{56,104},{64... | collective-permute-start | bytes 393224 | tf_op jit(solution)/shard_map/ppermute | solution.py:171
  44.6 2.8 %collective-permute-done.8 = f32[32,1024]{1,0:T(8,128)S(1)} collective-permute-done((f32[32,1024]{1,0:T(8,128)S(1)}, f32[32,1024]{1,0:T(8,128)S(1)}, u32[]{:S(2)}, u32[]{:S(2)}) %collective-permute-start.8) | collective-permute-done | bytes 131104 | tf_op jit(solution)/shard_map/ppermute | solution.py:171
  47.5 2.5 %collective-permute-start.9 = (f32[32,1024]{1,0:T(8,128)S(1)}, f32[32,1024]{1,0:T(8,128)S(1)}, u32[]{:S(2)}, u32[]{:S(2)}) collective-permute-start(f32[32,1024]{1,0:T(8,128)S(1)} %add.77), channel_id=1, source_target_pairs={{0,112},{8,24},{16,32},{24,8},{32,16},{40,56},{48,64},{56,40},{64,... | collective-permute-start | bytes 393224 | tf_op jit(solution)/shard_map/ppermute | solution.py:171
  50.0 3.4 %collective-permute-done.20 = f32[32,1024]{1,0:T(8,128)S(1)} collective-permute-done((f32[32,1024]{1,0:T(8,128)S(1)}, f32[32,1024]{1,0:T(8,128)S(1)}, u32[]{:S(2)}, u32[]{:S(2)}) %collective-permute-start.20) | collective-permute-done | bytes 131104 | tf_op jit(solution)/shard_map/ppermute | solution.py:171
  53.4 1.3 %collective-permute-start.21 = (f32[32,1024]{1,0:T(8,128)S(1)}, f32[32,1024]{1,0:T(8,128)S(1)}, u32[]{:S(2)}, u32[]{:S(2)}) collective-permute-start(f32[32,1024]{1,0:T(8,128)S(1)} %add.87), channel_id=1, source_target_pairs={{0,128},{8,136},{16,144},{24,152},{32,160},{40,168},{48,176},{56,1... | collective-permute-start | bytes 393224 | tf_op jit(solution)/shard_map/ppermute | solution.py:171
  54.7 2.0 %collective-permute-done.9 = f32[32,1024]{1,0:T(8,128)S(1)} collective-permute-done((f32[32,1024]{1,0:T(8,128)S(1)}, f32[32,1024]{1,0:T(8,128)S(1)}, u32[]{:S(2)}, u32[]{:S(2)}) %collective-permute-start.9) | collective-permute-done | bytes 131104 | tf_op jit(solution)/shard_map/ppermute | solution.py:171
  58.5 2.1 %collective-permute-start.11 = (f32[32,1024]{1,0:T(8,128)S(1)}, f32[32,1024]{1,0:T(8,128)S(1)}, u32[]{:S(2)}, u32[]{:S(2)}) collective-permute-start(f32[32,1024]{1,0:T(8,128)S(1)} %add.78), channel_id=1, source_target_pairs={{0,16},{8,120},{16,0},{24,40},{32,48},{40,24},{48,32},{56,72},{64,... | collective-permute-start | bytes 393224 | tf_op jit(solution)/shard_map/ppermute | solution.py:171
  62.4 4.1 %collective-permute-start.12 = (f32[32,1024]{1,0:T(8,128)S(1)}, f32[32,1024]{1,0:T(8,128)S(1)}, u32[]{:S(2)}, u32[]{:S(2)}) collective-permute-start(f32[32,1024]{1,0:T(8,128)S(1)} %collective-permute-done.10), channel_id=1, source_target_pairs={{0,16},{8,120},{16,0},{24,40},{32,48},{40,24},{48,32},{56,72},{64,... | collective-permute-start | bytes 393224 | tf_op jit(solution)/shard_map/ppermute | solution.py:171
  67.2 1.6 %collective-permute-done.12 = f32[32,1024]{1,0:T(8,128)S(1)} collective-permute-done((f32[32,1024]{1,0:T(8,128)S(1)}, f32[32,1024]{1,0:T(8,128)S(1)}, u32[]{:S(2)}, u32[]{:S(2)}) %collective-permute-start.12) | collective-permute-done | bytes 131104 | tf_op jit(solution)/shard_map/ppermute | solution.py:171
  69.0 1.5 %collective-permute-done.14.refs_3_ = f32[2,32,1024]{2,1,0:T(8,128)S(1)} collective-permute-done((f32[2,32,1024]{2,1,0:T(8,128)S(1)}, f32[2,32,1024]{2,1,0:T(8,128)S(1)}, u32[]{:S(2)}, u32[]{:S(2)}) %collective-permute-start.14) | collective-permute-done | bytes 262176 | tf_op jit(solution)/shard_map/ppermute | solution.py:171
  70.5 1.5 %shard_map.46 = f32[32,16384]{1,0:T(8,128)} custom-call(s32[1]{0:T(128)} %bitcast.me_ref, f32[2,32,1024]{2,1,0:T(8,128)S(1)} %pad_maximum_fusion.refs_0_, f32[2,32,1024]{2,1,0:T(8,128)S(1)} %pad_maximum_fusion.1.refs_1_, f32[2,32,1024]{2,1,0:T(8,128)S(1)} %collective-permute-done.13.refs_2_, f32[2,32,1024]{2,1,0:T(8,128)S(1)} %collective-permute-done.14.refs_3_, ...), custom_call_target="tpu_custom_call" | custom-call | tf_op jit(solution)/shard_map/pallas_call | solution.py:157
  (58 shorter events, 11.8 us)
Async XLA Ops:
  4.9 4.8 %collective-permute-start = (f32[32,256]{1,0:T(8,128)S(1)}, f32[32,256]{1,0:T(8,128)S(1)}, u32[]{:S(2)}, u32[]{:S(2)}) collective-permute-start(f32[32,256]{1,0:T(8,128)S(1)} %get-tuple-element.7), channel_id=1, source_target_pairs={{0,1},{1,0},{2,3},{3,2},{4,5},{5,4},{6,7},{7,6},{8,9},{9,8},{10,11... | collective-permute-start | bytes 98312 | tf_op jit(solution)/shard_map/ppermute | solution.py:175
  7.1 4.0 %collective-permute-start.1 = (f32[32,256]{1,0:T(8,128)S(1)}, f32[32,256]{1,0:T(8,128)S(1)}, u32[]{:S(2)}, u32[]{:S(2)}) collective-permute-start(f32[32,256]{1,0:T(8,128)S(1)} %get-tuple-element.7), channel_id=1, source_target_pairs={{0,3},{1,2},{2,1},{3,0},{4,7},{5,6},{6,5},{7,4},{8,11},{9,10},{10,... | collective-permute-start | bytes 98312 | tf_op jit(solution)/shard_map/ppermute | solution.py:175
  9.0 4.3 %collective-permute-start.2 = (f32[32,256]{1,0:T(8,128)S(1)}, f32[32,256]{1,0:T(8,128)S(1)}, u32[]{:S(2)}, u32[]{:S(2)}) collective-permute-start(f32[32,256]{1,0:T(8,128)S(1)} %get-tuple-element.7), channel_id=1, source_target_pairs={{0,2},{1,3},{2,0},{3,1},{4,6},{5,7},{6,4},{7,5},{8,10},{9,11},{10,... | collective-permute-start | bytes 98312 | tf_op jit(solution)/shard_map/ppermute | solution.py:175
  13.3 4.4 %collective-permute-start.3 = (f32[32,256]{1,0:T(8,128)S(1)}, f32[32,256]{1,0:T(8,128)S(1)}, u32[]{:S(2)}, u32[]{:S(2)}) collective-permute-start(f32[32,256]{1,0:T(8,128)S(1)} %add_add_fusion), channel_id=1, source_target_pairs={{0,4},{1,5},{2,6},{3,7},{4,0},{5,1},{6,2},{7,3},{8,12},{9,13},{10,... | collective-permute-start | bytes 98312 | tf_op jit(solution)/shard_map/ppermute | solution.py:175
  18.0 5.5 %collective-permute-start.16 = (f32[2,32,1024]{2,1,0:T(8,128)S(1)}, f32[2,32,1024]{2,1,0:T(8,128)S(1)}, u32[]{:S(2)}, u32[]{:S(2)}) collective-permute-start(f32[2,32,1024]{2,1,0:T(8,128)S(1)} %shard_map.44), channel_id=1, source_target_pairs={{0,8},{8,0},{16,24},{24,16},{32,40},{40,32},{48,56},{56,48},{64,72... | collective-permute-start | bytes 786440 | tf_op jit(solution)/shard_map/ppermute | solution.py:171
  21.8 7.6 %collective-permute-start.5 = (f32[2,32,1024]{2,1,0:T(8,128)S(1)}, f32[2,32,1024]{2,1,0:T(8,128)S(1)}, u32[]{:S(2)}, u32[]{:S(2)}) collective-permute-start(f32[2,32,1024]{2,1,0:T(8,128)S(1)} %shard_map.40), channel_id=1, source_target_pairs={{0,8},{8,0},{16,24},{24,16},{32,40},{40,32},{48,56},{56,48},{64,72... | collective-permute-start | bytes 786440 | tf_op jit(solution)/shard_map/ppermute | solution.py:171
  22.8 7.4 %collective-permute-start.15 = (f32[2,32,1024]{2,1,0:T(8,128)S(1)}, f32[2,32,1024]{2,1,0:T(8,128)S(1)}, u32[]{:S(2)}, u32[]{:S(2)}) collective-permute-start(f32[2,32,1024]{2,1,0:T(8,128)S(1)} %shard_map.42), channel_id=1, source_target_pairs={{0,8},{8,0},{16,24},{24,16},{32,40},{40,32},{48,56},{56,48},{64,72... | collective-permute-start | bytes 786440 | tf_op jit(solution)/shard_map/ppermute | solution.py:171
  23.3 6.9 %collective-permute-start.4 = (f32[2,32,1024]{2,1,0:T(8,128)S(1)}, f32[2,32,1024]{2,1,0:T(8,128)S(1)}, u32[]{:S(2)}, u32[]{:S(2)}) collective-permute-start(f32[2,32,1024]{2,1,0:T(8,128)S(1)} %shard_map.38), channel_id=1, source_target_pairs={{0,8},{8,0},{16,24},{24,16},{32,40},{40,32},{48,56},{56,48},{64,72... | collective-permute-start | bytes 786440 | tf_op jit(solution)/shard_map/ppermute | solution.py:171
  23.5 9.4 %collective-permute-start.17 = (f32[2,32,1024]{2,1,0:T(8,128)S(1)}, f32[2,32,1024]{2,1,0:T(8,128)S(1)}, u32[]{:S(2)}, u32[]{:S(2)}) collective-permute-start(f32[2,32,1024]{2,1,0:T(8,128)S(1)} %add.80), channel_id=1, source_target_pairs={{0,16},{8,120},{16,0},{24,40},{32,48},{40,24},{48,32},{56,72},{64,... | collective-permute-start | bytes 786440 | tf_op jit(solution)/shard_map/ppermute | solution.py:171
  29.5 6.5 %collective-permute-start.6 = (f32[2,32,1024]{2,1,0:T(8,128)S(1)}, f32[2,32,1024]{2,1,0:T(8,128)S(1)}, u32[]{:S(2)}, u32[]{:S(2)}) collective-permute-start(f32[2,32,1024]{2,1,0:T(8,128)S(1)} %add.71), channel_id=1, source_target_pairs={{0,16},{8,120},{16,0},{24,40},{32,48},{40,24},{48,32},{56,72},{64,... | collective-permute-start | bytes 786440 | tf_op jit(solution)/shard_map/ppermute | solution.py:171
  32.9 4.9 %collective-permute-start.18 = (f32[32,1024]{1,0:T(8,128)S(1)}, f32[32,1024]{1,0:T(8,128)S(1)}, u32[]{:S(2)}, u32[]{:S(2)}) collective-permute-start(f32[32,1024]{1,0:T(8,128)S(1)} %fusion), channel_id=1, source_target_pairs={{0,128},{8,136},{16,144},{24,152},{32,160},{40,168},{48,176},{56,1... | collective-permute-start | bytes 393224 | tf_op jit(solution)/shard_map/ppermute | solution.py:171
  36.0 3.9 %collective-permute-start.7 = (f32[32,1024]{1,0:T(8,128)S(1)}, f32[32,1024]{1,0:T(8,128)S(1)}, u32[]{:S(2)}, u32[]{:S(2)}) collective-permute-start(f32[32,1024]{1,0:T(8,128)S(1)} %fusion.3), channel_id=1, source_target_pairs={{0,128},{8,136},{16,144},{24,152},{32,160},{40,168},{48,176},{56,1... | collective-permute-start | bytes 393224 | tf_op jit(solution)/shard_map/ppermute | solution.py:171
  37.9 4.8 %collective-permute-start.19 = (f32[32,1024]{1,0:T(8,128)S(1)}, f32[32,1024]{1,0:T(8,128)S(1)}, u32[]{:S(2)}, u32[]{:S(2)}) collective-permute-start(f32[32,1024]{1,0:T(8,128)S(1)} %fusion.2), channel_id=1, source_target_pairs={{0,112},{8,24},{16,32},{24,8},{32,16},{40,56},{48,64},{56,40},{64,... | collective-permute-start | bytes 393224 | tf_op jit(solution)/shard_map/ppermute | solution.py:171
  39.9 7.5 %collective-permute-start.8 = (f32[32,1024]{1,0:T(8,128)S(1)}, f32[32,1024]{1,0:T(8,128)S(1)}, u32[]{:S(2)}, u32[]{:S(2)}) collective-permute-start(f32[32,1024]{1,0:T(8,128)S(1)} %fusion.5), channel_id=1, source_target_pairs={{0,48},{8,88},{16,96},{24,72},{32,80},{40,120},{48,0},{56,104},{64... | collective-permute-start | bytes 393224 | tf_op jit(solution)/shard_map/ppermute | solution.py:171
  42.7 10.6 %collective-permute-start.20 = (f32[32,1024]{1,0:T(8,128)S(1)}, f32[32,1024]{1,0:T(8,128)S(1)}, u32[]{:S(2)}, u32[]{:S(2)}) collective-permute-start(f32[32,1024]{1,0:T(8,128)S(1)} %add.86), channel_id=1, source_target_pairs={{0,48},{8,88},{16,96},{24,72},{32,80},{40,120},{48,0},{56,104},{64... | collective-permute-start | bytes 393224 | tf_op jit(solution)/shard_map/ppermute | solution.py:171
  47.5 9.2 %collective-permute-start.9 = (f32[32,1024]{1,0:T(8,128)S(1)}, f32[32,1024]{1,0:T(8,128)S(1)}, u32[]{:S(2)}, u32[]{:S(2)}) collective-permute-start(f32[32,1024]{1,0:T(8,128)S(1)} %add.77), channel_id=1, source_target_pairs={{0,112},{8,24},{16,32},{24,8},{32,16},{40,56},{48,64},{56,40},{64,... | collective-permute-start | bytes 393224 | tf_op jit(solution)/shard_map/ppermute | solution.py:171
  53.4 7.3 %collective-permute-start.21 = (f32[32,1024]{1,0:T(8,128)S(1)}, f32[32,1024]{1,0:T(8,128)S(1)}, u32[]{:S(2)}, u32[]{:S(2)}) collective-permute-start(f32[32,1024]{1,0:T(8,128)S(1)} %add.87), channel_id=1, source_target_pairs={{0,128},{8,136},{16,144},{24,152},{32,160},{40,168},{48,176},{56,1... | collective-permute-start | bytes 393224 | tf_op jit(solution)/shard_map/ppermute | solution.py:171
  56.7 5.7 %collective-permute-start.10 = (f32[32,1024]{1,0:T(8,128)S(1)}, f32[32,1024]{1,0:T(8,128)S(1)}, u32[]{:S(2)}, u32[]{:S(2)}) collective-permute-start(f32[32,1024]{1,0:T(8,128)S(1)} %add.78), channel_id=1, source_target_pairs={{0,128},{8,136},{16,144},{24,152},{32,160},{40,168},{48,176},{56,1... | collective-permute-start | bytes 393224 | tf_op jit(solution)/shard_map/ppermute | solution.py:171
  58.0 8.5 %collective-permute-start.22 = (f32[32,1024]{1,0:T(8,128)S(1)}, f32[32,1024]{1,0:T(8,128)S(1)}, u32[]{:S(2)}, u32[]{:S(2)}) collective-permute-start(f32[32,1024]{1,0:T(8,128)S(1)} %add.87), channel_id=1, source_target_pairs={{0,16},{8,120},{16,0},{24,40},{32,48},{40,24},{48,32},{56,72},{64,... | collective-permute-start | bytes 393224 | tf_op jit(solution)/shard_map/ppermute | solution.py:171
  58.5 8.7 %collective-permute-start.11 = (f32[32,1024]{1,0:T(8,128)S(1)}, f32[32,1024]{1,0:T(8,128)S(1)}, u32[]{:S(2)}, u32[]{:S(2)}) collective-permute-start(f32[32,1024]{1,0:T(8,128)S(1)} %add.78), channel_id=1, source_target_pairs={{0,16},{8,120},{16,0},{24,40},{32,48},{40,24},{48,32},{56,72},{64,... | collective-permute-start | bytes 393224 | tf_op jit(solution)/shard_map/ppermute | solution.py:171
  60.7 5.9 %collective-permute-start.23 = (f32[32,1024]{1,0:T(8,128)S(1)}, f32[32,1024]{1,0:T(8,128)S(1)}, u32[]{:S(2)}, u32[]{:S(2)}) collective-permute-start(f32[32,1024]{1,0:T(8,128)S(1)} %collective-permute-done.21), channel_id=1, source_target_pairs={{0,16},{8,120},{16,0},{24,40},{32,48},{40,24},{48,32},{56,72},{64,... | collective-permute-start | bytes 393224 | tf_op jit(solution)/shard_map/ppermute | solution.py:171
  61.2 7.7 %collective-permute-start.24 = (f32[2,32,1024]{2,1,0:T(8,128)S(1)}, f32[2,32,1024]{2,1,0:T(8,128)S(1)}, u32[]{:S(2)}, u32[]{:S(2)}) collective-permute-start(f32[2,32,1024]{2,1,0:T(8,128)S(1)} %pad_maximum_fusion.2.refs_4_), channel_id=1, source_target_pairs={{0,8},{8,0},{16,24},{24,16},{32,40},{40,32},{48,56},{56,48},{64,72... | collective-permute-start | bytes 786440 | tf_op jit(solution)/shard_map/ppermute | solution.py:171
  62.4 6.4 %collective-permute-start.12 = (f32[32,1024]{1,0:T(8,128)S(1)}, f32[32,1024]{1,0:T(8,128)S(1)}, u32[]{:S(2)}, u32[]{:S(2)}) collective-permute-start(f32[32,1024]{1,0:T(8,128)S(1)} %collective-permute-done.10), channel_id=1, source_target_pairs={{0,16},{8,120},{16,0},{24,40},{32,48},{40,24},{48,32},{56,72},{64,... | collective-permute-start | bytes 393224 | tf_op jit(solution)/shard_map/ppermute | solution.py:171
  66.5 2.5 %collective-permute-start.13 = (f32[2,32,1024]{2,1,0:T(8,128)S(1)}, f32[2,32,1024]{2,1,0:T(8,128)S(1)}, u32[]{:S(2)}, u32[]{:S(2)}) collective-permute-start(f32[2,32,1024]{2,1,0:T(8,128)S(1)} %pad_maximum_fusion.refs_0_), channel_id=1, source_target_pairs={{0,8},{8,0},{16,24},{24,16},{32,40},{40,32},{48,56},{56,48},{64,72... | collective-permute-start | bytes 786440 | tf_op jit(solution)/shard_map/ppermute | solution.py:171
  (3 other events, 21.6 us)

commit v5 on v4

--- a/solution.py
+++ b/solution.py
@@ -37,6 +37,7 @@
 VMEM = pl.BlockSpec(memory_space=pltpu.VMEM)
 SMEM = pl.BlockSpec(memory_space=pltpu.SMEM)
 HBM = pl.BlockSpec(memory_space=pltpu.HBM)
+ANY = pl.BlockSpec(memory_space=pl.ANY)
 
 
 def slot_columns(me, core, slot, stream, width):
@@ -110,11 +111,12 @@
     )(me, blocks, jacobian)
 
 
-def product(me, weighted, held, other_core, slots, stream):
+def product(me, weighted, held, other_core, slots, stream, *after):
     k, rows = weighted.shape
     width = held.shape[1] // (N_CORE * SLOTS * STREAMS)
 
-    def kernel(me_ref, weighted_ref, held_ref, out_ref):
+    def kernel(me_ref, weighted_ref, held_ref, *refs):
+        out_ref = refs[-1]
         core = lax.rem(me_ref[0], N_CORE)
         core = 1 - core if other_core else core
         for i, slot in enumerate(slots):
@@ -126,7 +128,7 @@
 
     return pl.pallas_call(
         kernel,
-        in_specs=[SMEM, VMEM, VMEM],
+        in_specs=[SMEM, VMEM, VMEM] + [ANY] * len(after),
         out_specs=VMEM,
         out_shape=jax.ShapeDtypeStruct((len(slots), k, width), jnp.float32),
         compiler_params=pltpu.CompilerParams(vmem_limit_bytes=24 * MIB),
@@ -135,7 +137,7 @@
             bytes_accessed=2 * rows * len(slots) * width,
             transcendentals=0,
         ),
-    )(me, weighted, held)
+    )(me, weighted, held, *after)
 
 
 def assemble(me, streams, ncols):
@@ -179,14 +181,16 @@
     weighted = weights[:, None, :] * predicted.reshape(p, k, -1)
     weighted = weighted.reshape(p * k, -1).astype(jnp.bfloat16)
 
+    highs = []
+    for stream in range(STREAMS):
+        high = swap(product(me, weighted, held, True, (2, 3), stream), CORE_SWAP)
+        highs.append(high + product(me, weighted, held, False, (2, 3), stream))
     streams = []
     for stream in range(STREAMS):
         first, second = (X_SWAP, NEAR) if X_FIRST[stream] else (NEAR, X_SWAP)
-        high = swap(product(me, weighted, held, True, (2, 3), stream), CORE_SWAP)
-        high = high + product(me, weighted, held, False, (2, 3), stream)
-        high = swap(high, first)
-        low = swap(product(me, weighted, held, True, (0, 1), stream), CORE_SWAP)
-        low = low + product(me, weighted, held, False, (0, 1), stream)
+        high = swap(highs[stream], first)
+        low = swap(product(me, weighted, held, True, (0, 1), stream, highs[-1]), CORE_SWAP)
+        low = low + product(me, weighted, held, False, (0, 1), stream, highs[-1])
         total = low[0] + high[0] + swap(low[1] + high[1], second)
         for pairs in SUMS[stream]:
             total = total + swap(total, pairs)

time: 72 us -> 71 us (0.986)
  starting transfers between devices: 39.4 us -> 38.2 us
where the time goes in v5:
time: 71 us
  starting transfers between devices  38.2 us (54%)
  waiting for transfers between devices  23.6 us (33%)
  Pallas kernels  8.64 us (12%)
    ppermute x22, starting transfers between devices, swap(): return lax.ppermute(value, 'sens', pairs)  31.1 us
    ppermute x22, waiting for transfers between devices, swap(): return lax.ppermute(value, 'sens', pairs)  18.3 us
    ppermute x4, starting transfers between devices, flip(): return lax.ppermute(value, 'cand', [(c, c ^ bits) for c in range(N_CAND)])  7.13 us
    ppermute x4, waiting for transfers between devices, flip(): return lax.ppermute(value, 'cand', [(c, c ^ bits) for c in range(N_CAND)])  5.34 us
    pallas_call x1, Pallas kernels, predict(): pl.pallas_call(predict_kernel, in_specs=[SMEM, HBM, HBM], out_specs=[VMEM...  4.87 us
    pallas_call x8, Pallas kernels, product(): pl.pallas_call(kernel, in_specs=[SMEM, VMEM, VMEM] + [ANY] * len(after),...  2.3 us
    pallas_call x1, Pallas kernels, assemble(): pl.pallas_call(kernel, in_specs=[SMEM] + [VMEM] * len(operands), out_spec...  1.47 us
  transfers between devices with their start and end apart: 26, of which 12 were waited for; matrix products, arithmetic and copies ran while one was open for 0% of the time, Pallas kernels for 3%

profile of v5, /device:TPU:1, one launch (start us, length us, event | category | flops | bytes accessed | tf_op | source)
XLA Modules:
  0.0 71.0 jit_solution(9150420111607532347)
XLA Ops:
  0.0 4.9 %shard_map.37 = (f32[32,256]{1,0:T(8,128)S(1)}, bf16[256,16384]{1,0:T(8,128)(2,1)S(1)}) custom-call(s32[1]{0:T(128)} %bitcast.me_ref, f32[32,16384]{1,0:T(8,128)} %bitcast.27, bf16[256,16384]{1,0:T(8,128)(2,1)} %jac_ref.1), custom_call_target="tpu_custom_call" | custom-call | flops 268435456 | bytes 8388608 | tf_op jit(solution)/shard_map/pallas_call | solution.py:94
  4.9 3.8 %collective-permute-start.2 = (f32[32,256]{1,0:T(8,128)S(1)}, f32[32,256]{1,0:T(8,128)S(1)}, u32[]{:S(2)}, u32[]{:S(2)}) collective-permute-start(f32[32,256]{1,0:T(8,128)S(1)} %get-tuple-element.7), channel_id=1, source_target_pairs={{0,2},{1,3},{2,0},{3,1},{4,6},{5,7},{6,4},{7,5},{8,10},{9,11},{10,... | collective-permute-start | bytes 98312 | tf_op jit(solution)/shard_map/ppermute | solution.py:177
  10.0 3.0 %collective-permute-done.1 = f32[32,256]{1,0:T(8,128)S(1)} collective-permute-done((f32[32,256]{1,0:T(8,128)S(1)}, f32[32,256]{1,0:T(8,128)S(1)}, u32[]{:S(2)}, u32[]{:S(2)}) %collective-permute-start.1) | collective-permute-done | bytes 32800 | tf_op jit(solution)/shard_map/ppermute | solution.py:177
  13.0 2.5 %collective-permute-start.3 = (f32[32,256]{1,0:T(8,128)S(1)}, f32[32,256]{1,0:T(8,128)S(1)}, u32[]{:S(2)}, u32[]{:S(2)}) collective-permute-start(f32[32,256]{1,0:T(8,128)S(1)} %add_add_fusion), channel_id=1, source_target_pairs={{0,4},{1,5},{2,6},{3,7},{4,0},{5,1},{6,2},{7,3},{8,12},{9,13},{10,... | collective-permute-start | bytes 98312 | tf_op jit(solution)/shard_map/ppermute | solution.py:177
  15.5 1.8 %collective-permute-done.3 = f32[32,256]{1,0:T(8,128)S(1)} collective-permute-done((f32[32,256]{1,0:T(8,128)S(1)}, f32[32,256]{1,0:T(8,128)S(1)}, u32[]{:S(2)}, u32[]{:S(2)}) %collective-permute-start.3) | collective-permute-done | bytes 32800 | tf_op jit(solution)/shard_map/ppermute | solution.py:177
  17.7 3.0 %collective-permute-start.4 = (f32[2,32,1024]{2,1,0:T(8,128)S(1)}, f32[2,32,1024]{2,1,0:T(8,128)S(1)}, u32[]{:S(2)}, u32[]{:S(2)}) collective-permute-start(f32[2,32,1024]{2,1,0:T(8,128)S(1)} %shard_map.38), channel_id=1, source_target_pairs={{0,8},{8,0},{16,24},{24,16},{32,40},{40,32},{48,56},{56,48},{64,72... | collective-permute-start | bytes 786440 | tf_op jit(solution)/shard_map/ppermute | solution.py:173
  22.6 5.6 %collective-permute-start.17 = (f32[2,32,1024]{2,1,0:T(8,128)S(1)}, f32[2,32,1024]{2,1,0:T(8,128)S(1)}, u32[]{:S(2)}, u32[]{:S(2)}) collective-permute-start(f32[2,32,1024]{2,1,0:T(8,128)S(1)} %add.70.refs_0_), channel_id=1, source_target_pairs={{0,16},{8,120},{16,0},{24,40},{32,48},{40,24},{48,32},{56,72},{64,... | collective-permute-start | bytes 786440 | tf_op jit(solution)/shard_map/ppermute | solution.py:173
  28.9 1.2 %collective-permute-start.7 = (f32[2,32,1024]{2,1,0:T(8,128)S(1)}, f32[2,32,1024]{2,1,0:T(8,128)S(1)}, u32[]{:S(2)}, u32[]{:S(2)}) collective-permute-start(f32[2,32,1024]{2,1,0:T(8,128)S(1)} %add.72), channel_id=1, source_target_pairs={{0,16},{8,120},{16,0},{24,40},{32,48},{40,24},{48,32},{56,72},{64,... | collective-permute-start | bytes 786440 | tf_op jit(solution)/shard_map/ppermute | solution.py:173
  30.7 1.2 %collective-permute-done.17 = f32[2,32,1024]{2,1,0:T(8,128)S(1)} collective-permute-done((f32[2,32,1024]{2,1,0:T(8,128)S(1)}, f32[2,32,1024]{2,1,0:T(8,128)S(1)}, u32[]{:S(2)}, u32[]{:S(2)}) %collective-permute-start.17) | collective-permute-done | bytes 262176 | tf_op jit(solution)/shard_map/ppermute | solution.py:173
  32.0 1.3 %collective-permute-start.18 = (f32[32,1024]{1,0:T(8,128)S(1)}, f32[32,1024]{1,0:T(8,128)S(1)}, u32[]{:S(2)}, u32[]{:S(2)}) collective-permute-start(f32[32,1024]{1,0:T(8,128)S(1)} %fusion), channel_id=1, source_target_pairs={{0,128},{8,136},{16,144},{24,152},{32,160},{40,168},{48,176},{56,1... | collective-permute-start | bytes 393224 | tf_op jit(solution)/shard_map/ppermute | solution.py:173
  33.3 2.1 %collective-permute-done.7 = f32[2,32,1024]{2,1,0:T(8,128)S(1)} collective-permute-done((f32[2,32,1024]{2,1,0:T(8,128)S(1)}, f32[2,32,1024]{2,1,0:T(8,128)S(1)}, u32[]{:S(2)}, u32[]{:S(2)}) %collective-permute-start.7) | collective-permute-done | bytes 262176 | tf_op jit(solution)/shard_map/ppermute | solution.py:173
  35.4 1.3 %collective-permute-start.8 = (f32[32,1024]{1,0:T(8,128)S(1)}, f32[32,1024]{1,0:T(8,128)S(1)}, u32[]{:S(2)}, u32[]{:S(2)}) collective-permute-start(f32[32,1024]{1,0:T(8,128)S(1)} %fusion.3), channel_id=1, source_target_pairs={{0,128},{8,136},{16,144},{24,152},{32,160},{40,168},{48,176},{56,1... | collective-permute-start | bytes 393224 | tf_op jit(solution)/shard_map/ppermute | solution.py:173
  36.9 3.3 %collective-permute-done.8 = f32[32,1024]{1,0:T(8,128)S(1)} collective-permute-done((f32[32,1024]{1,0:T(8,128)S(1)}, f32[32,1024]{1,0:T(8,128)S(1)}, u32[]{:S(2)}, u32[]{:S(2)}) %collective-permute-start.8) | collective-permute-done | bytes 131104 | tf_op jit(solution)/shard_map/ppermute | solution.py:173
  40.2 1.4 %collective-permute-start.9 = (f32[32,1024]{1,0:T(8,128)S(1)}, f32[32,1024]{1,0:T(8,128)S(1)}, u32[]{:S(2)}, u32[]{:S(2)}) collective-permute-start(f32[32,1024]{1,0:T(8,128)S(1)} %fusion.5), channel_id=1, source_target_pairs={{0,48},{8,88},{16,96},{24,72},{32,80},{40,120},{48,0},{56,104},{64... | collective-permute-start | bytes 393224 | tf_op jit(solution)/shard_map/ppermute | solution.py:173
  41.7 3.2 %collective-permute-start.20 = (f32[32,1024]{1,0:T(8,128)S(1)}, f32[32,1024]{1,0:T(8,128)S(1)}, u32[]{:S(2)}, u32[]{:S(2)}) collective-permute-start(f32[32,1024]{1,0:T(8,128)S(1)} %add.86), channel_id=1, source_target_pairs={{0,48},{8,88},{16,96},{24,72},{32,80},{40,120},{48,0},{56,104},{64... | collective-permute-start | bytes 393224 | tf_op jit(solution)/shard_map/ppermute | solution.py:173
  44.9 3.1 %collective-permute-done.9 = f32[32,1024]{1,0:T(8,128)S(1)} collective-permute-done((f32[32,1024]{1,0:T(8,128)S(1)}, f32[32,1024]{1,0:T(8,128)S(1)}, u32[]{:S(2)}, u32[]{:S(2)}) %collective-permute-start.9) | collective-permute-done | bytes 131104 | tf_op jit(solution)/shard_map/ppermute | solution.py:173
  48.4 5.0 %collective-permute-done.20 = f32[32,1024]{1,0:T(8,128)S(1)} collective-permute-done((f32[32,1024]{1,0:T(8,128)S(1)}, f32[32,1024]{1,0:T(8,128)S(1)}, u32[]{:S(2)}, u32[]{:S(2)}) %collective-permute-start.20) | collective-permute-done | bytes 131104 | tf_op jit(solution)/shard_map/ppermute | solution.py:173
  53.5 1.3 %collective-permute-start.21 = (f32[32,1024]{1,0:T(8,128)S(1)}, f32[32,1024]{1,0:T(8,128)S(1)}, u32[]{:S(2)}, u32[]{:S(2)}) collective-permute-start(f32[32,1024]{1,0:T(8,128)S(1)} %add.87), channel_id=1, source_target_pairs={{0,128},{8,136},{16,144},{24,152},{32,160},{40,168},{48,176},{56,1... | collective-permute-start | bytes 393224 | tf_op jit(solution)/shard_map/ppermute | solution.py:173
  55.9 1.3 %collective-permute-start.11 = (f32[32,1024]{1,0:T(8,128)S(1)}, f32[32,1024]{1,0:T(8,128)S(1)}, u32[]{:S(2)}, u32[]{:S(2)}) collective-permute-start(f32[32,1024]{1,0:T(8,128)S(1)} %add.79), channel_id=1, source_target_pairs={{0,128},{8,136},{16,144},{24,152},{32,160},{40,168},{48,176},{56,1... | collective-permute-start | bytes 393224 | tf_op jit(solution)/shard_map/ppermute | solution.py:173
  57.5 2.3 %collective-permute-start.12 = (f32[32,1024]{1,0:T(8,128)S(1)}, f32[32,1024]{1,0:T(8,128)S(1)}, u32[]{:S(2)}, u32[]{:S(2)}) collective-permute-start(f32[32,1024]{1,0:T(8,128)S(1)} %add.79), channel_id=1, source_target_pairs={{0,16},{8,120},{16,0},{24,40},{32,48},{40,24},{48,32},{56,72},{64,... | collective-permute-start | bytes 393224 | tf_op jit(solution)/shard_map/ppermute | solution.py:173
  60.2 1.7 %collective-permute-start.24 = (f32[2,32,1024]{2,1,0:T(8,128)S(1)}, f32[2,32,1024]{2,1,0:T(8,128)S(1)}, u32[]{:S(2)}, u32[]{:S(2)}) collective-permute-start(f32[2,32,1024]{2,1,0:T(8,128)S(1)} %pad_maximum_fusion.2.refs_4_), channel_id=1, source_target_pairs={{0,8},{8,0},{16,24},{24,16},{32,40},{40,32},{48,56},{56,48},{64,72... | collective-permute-start | bytes 786440 | tf_op jit(solution)/shard_map/ppermute | solution.py:173
  62.0 3.3 %collective-permute-start.13 = (f32[32,1024]{1,0:T(8,128)S(1)}, f32[32,1024]{1,0:T(8,128)S(1)}, u32[]{:S(2)}, u32[]{:S(2)}) collective-permute-start(f32[32,1024]{1,0:T(8,128)S(1)} %collective-permute-done.11), channel_id=1, source_target_pairs={{0,16},{8,120},{16,0},{24,40},{32,48},{40,24},{48,32},{56,72},{64,... | collective-permute-start | bytes 393224 | tf_op jit(solution)/shard_map/ppermute | solution.py:173
  65.4 1.5 %collective-permute-start.25 = (f32[2,32,1024]{2,1,0:T(8,128)S(1)}, f32[2,32,1024]{2,1,0:T(8,128)S(1)}, u32[]{:S(2)}, u32[]{:S(2)}) collective-permute-start(f32[2,32,1024]{2,1,0:T(8,128)S(1)} %pad_maximum_fusion.3.refs_5_), channel_id=1, source_target_pairs={{0,8},{8,0},{16,24},{24,16},{32,40},{40,32},{48,56},{56,48},{64,72... | collective-permute-start | bytes 786440 | tf_op jit(solution)/shard_map/ppermute | solution.py:173
  69.5 1.5 %shard_map.46 = f32[32,16384]{1,0:T(8,128)} custom-call(s32[1]{0:T(128)} %bitcast.me_ref, f32[2,32,1024]{2,1,0:T(8,128)S(1)} %pad_maximum_fusion.refs_0_, f32[2,32,1024]{2,1,0:T(8,128)S(1)} %pad_maximum_fusion.1.refs_1_, f32[2,32,1024]{2,1,0:T(8,128)S(1)} %collective-permute-done.14.refs_2_, f32[2,32,1024]{2,1,0:T(8,128)S(1)} %collective-permute-done.15.refs_3_, ...), custom_call_target="tpu_custom_call" | custom-call | tf_op jit(solution)/shard_map/pallas_call | solution.py:159
  (58 shorter events, 10.1 us)
Async XLA Ops:
  4.9 5.1 %collective-permute-start.2 = (f32[32,256]{1,0:T(8,128)S(1)}, f32[32,256]{1,0:T(8,128)S(1)}, u32[]{:S(2)}, u32[]{:S(2)}) collective-permute-start(f32[32,256]{1,0:T(8,128)S(1)} %get-tuple-element.7), channel_id=1, source_target_pairs={{0,2},{1,3},{2,0},{3,1},{4,6},{5,7},{6,4},{7,5},{8,10},{9,11},{10,... | collective-permute-start | bytes 98312 | tf_op jit(solution)/shard_map/ppermute | solution.py:177
  8.7 4.3 %collective-permute-start.1 = (f32[32,256]{1,0:T(8,128)S(1)}, f32[32,256]{1,0:T(8,128)S(1)}, u32[]{:S(2)}, u32[]{:S(2)}) collective-permute-start(f32[32,256]{1,0:T(8,128)S(1)} %get-tuple-element.7), channel_id=1, source_target_pairs={{0,3},{1,2},{2,1},{3,0},{4,7},{5,6},{6,5},{7,4},{8,11},{9,10},{10,... | collective-permute-start | bytes 98312 | tf_op jit(solution)/shard_map/ppermute | solution.py:177
  9.5 3.5 %collective-permute-start = (f32[32,256]{1,0:T(8,128)S(1)}, f32[32,256]{1,0:T(8,128)S(1)}, u32[]{:S(2)}, u32[]{:S(2)}) collective-permute-start(f32[32,256]{1,0:T(8,128)S(1)} %get-tuple-element.7), channel_id=1, source_target_pairs={{0,1},{1,0},{2,3},{3,2},{4,5},{5,4},{6,7},{7,6},{8,9},{9,8},{10,11... | collective-permute-start | bytes 98312 | tf_op jit(solution)/shard_map/ppermute | solution.py:177
  13.0 4.4 %collective-permute-start.3 = (f32[32,256]{1,0:T(8,128)S(1)}, f32[32,256]{1,0:T(8,128)S(1)}, u32[]{:S(2)}, u32[]{:S(2)}) collective-permute-start(f32[32,256]{1,0:T(8,128)S(1)} %add_add_fusion), channel_id=1, source_target_pairs={{0,4},{1,5},{2,6},{3,7},{4,0},{5,1},{6,2},{7,3},{8,12},{9,13},{10,... | collective-permute-start | bytes 98312 | tf_op jit(solution)/shard_map/ppermute | solution.py:177
  17.7 4.2 %collective-permute-start.4 = (f32[2,32,1024]{2,1,0:T(8,128)S(1)}, f32[2,32,1024]{2,1,0:T(8,128)S(1)}, u32[]{:S(2)}, u32[]{:S(2)}) collective-permute-start(f32[2,32,1024]{2,1,0:T(8,128)S(1)} %shard_map.38), channel_id=1, source_target_pairs={{0,8},{8,0},{16,24},{24,16},{32,40},{40,32},{48,56},{56,48},{64,72... | collective-permute-start | bytes 786440 | tf_op jit(solution)/shard_map/ppermute | solution.py:173
  21.0 7.9 %collective-permute-start.6 = (f32[2,32,1024]{2,1,0:T(8,128)S(1)}, f32[2,32,1024]{2,1,0:T(8,128)S(1)}, u32[]{:S(2)}, u32[]{:S(2)}) collective-permute-start(f32[2,32,1024]{2,1,0:T(8,128)S(1)} %shard_map.42), channel_id=1, source_target_pairs={{0,8},{8,0},{16,24},{24,16},{32,40},{40,32},{48,56},{56,48},{64,72... | collective-permute-start | bytes 786440 | tf_op jit(solution)/shard_map/ppermute | solution.py:173
  22.2 8.5 %collective-permute-start.16 = (f32[2,32,1024]{2,1,0:T(8,128)S(1)}, f32[2,32,1024]{2,1,0:T(8,128)S(1)}, u32[]{:S(2)}, u32[]{:S(2)}) collective-permute-start(f32[2,32,1024]{2,1,0:T(8,128)S(1)} %shard_map.44), channel_id=1, source_target_pairs={{0,8},{8,0},{16,24},{24,16},{32,40},{40,32},{48,56},{56,48},{64,72... | collective-permute-start | bytes 786440 | tf_op jit(solution)/shard_map/ppermute | solution.py:173
  22.6 9.3 %collective-permute-start.17 = (f32[2,32,1024]{2,1,0:T(8,128)S(1)}, f32[2,32,1024]{2,1,0:T(8,128)S(1)}, u32[]{:S(2)}, u32[]{:S(2)}) collective-permute-start(f32[2,32,1024]{2,1,0:T(8,128)S(1)} %add.70.refs_0_), channel_id=1, source_target_pairs={{0,16},{8,120},{16,0},{24,40},{32,48},{40,24},{48,32},{56,72},{64,... | collective-permute-start | bytes 786440 | tf_op jit(solution)/shard_map/ppermute | solution.py:173
  28.8 4.5 %collective-permute-start.5 = (f32[2,32,1024]{2,1,0:T(8,128)S(1)}, f32[2,32,1024]{2,1,0:T(8,128)S(1)}, u32[]{:S(2)}, u32[]{:S(2)}) collective-permute-start(f32[2,32,1024]{2,1,0:T(8,128)S(1)} %shard_map.40), channel_id=1, source_target_pairs={{0,8},{8,0},{16,24},{24,16},{32,40},{40,32},{48,56},{56,48},{64,72... | collective-permute-start | bytes 786440 | tf_op jit(solution)/shard_map/ppermute | solution.py:173
  28.9 6.5 %collective-permute-start.7 = (f32[2,32,1024]{2,1,0:T(8,128)S(1)}, f32[2,32,1024]{2,1,0:T(8,128)S(1)}, u32[]{:S(2)}, u32[]{:S(2)}) collective-permute-start(f32[2,32,1024]{2,1,0:T(8,128)S(1)} %add.72), channel_id=1, source_target_pairs={{0,16},{8,120},{16,0},{24,40},{32,48},{40,24},{48,32},{56,72},{64,... | collective-permute-start | bytes 786440 | tf_op jit(solution)/shard_map/ppermute | solution.py:173
  32.0 4.8 %collective-permute-start.18 = (f32[32,1024]{1,0:T(8,128)S(1)}, f32[32,1024]{1,0:T(8,128)S(1)}, u32[]{:S(2)}, u32[]{:S(2)}) collective-permute-start(f32[32,1024]{1,0:T(8,128)S(1)} %fusion), channel_id=1, source_target_pairs={{0,128},{8,136},{16,144},{24,152},{32,160},{40,168},{48,176},{56,1... | collective-permute-start | bytes 393224 | tf_op jit(solution)/shard_map/ppermute | solution.py:173
  35.4 4.7 %collective-permute-start.8 = (f32[32,1024]{1,0:T(8,128)S(1)}, f32[32,1024]{1,0:T(8,128)S(1)}, u32[]{:S(2)}, u32[]{:S(2)}) collective-permute-start(f32[32,1024]{1,0:T(8,128)S(1)} %fusion.3), channel_id=1, source_target_pairs={{0,128},{8,136},{16,144},{24,152},{32,160},{40,168},{48,176},{56,1... | collective-permute-start | bytes 393224 | tf_op jit(solution)/shard_map/ppermute | solution.py:173
  36.8 4.9 %collective-permute-start.19 = (f32[32,1024]{1,0:T(8,128)S(1)}, f32[32,1024]{1,0:T(8,128)S(1)}, u32[]{:S(2)}, u32[]{:S(2)}) collective-permute-start(f32[32,1024]{1,0:T(8,128)S(1)} %fusion.2), channel_id=1, source_target_pairs={{0,112},{8,24},{16,32},{24,8},{32,16},{40,56},{48,64},{56,40},{64,... | collective-permute-start | bytes 393224 | tf_op jit(solution)/shard_map/ppermute | solution.py:173
  40.2 7.8 %collective-permute-start.9 = (f32[32,1024]{1,0:T(8,128)S(1)}, f32[32,1024]{1,0:T(8,128)S(1)}, u32[]{:S(2)}, u32[]{:S(2)}) collective-permute-start(f32[32,1024]{1,0:T(8,128)S(1)} %fusion.5), channel_id=1, source_target_pairs={{0,48},{8,88},{16,96},{24,72},{32,80},{40,120},{48,0},{56,104},{64... | collective-permute-start | bytes 393224 | tf_op jit(solution)/shard_map/ppermute | solution.py:173
  41.7 11.8 %collective-permute-start.20 = (f32[32,1024]{1,0:T(8,128)S(1)}, f32[32,1024]{1,0:T(8,128)S(1)}, u32[]{:S(2)}, u32[]{:S(2)}) collective-permute-start(f32[32,1024]{1,0:T(8,128)S(1)} %add.86), channel_id=1, source_target_pairs={{0,48},{8,88},{16,96},{24,72},{32,80},{40,120},{48,0},{56,104},{64... | collective-permute-start | bytes 393224 | tf_op jit(solution)/shard_map/ppermute | solution.py:173
  48.0 7.9 %collective-permute-start.10 = (f32[32,1024]{1,0:T(8,128)S(1)}, f32[32,1024]{1,0:T(8,128)S(1)}, u32[]{:S(2)}, u32[]{:S(2)}) collective-permute-start(f32[32,1024]{1,0:T(8,128)S(1)} %add.78), channel_id=1, source_target_pairs={{0,112},{8,24},{16,32},{24,8},{32,16},{40,56},{48,64},{56,40},{64,... | collective-permute-start | bytes 393224 | tf_op jit(solution)/shard_map/ppermute | solution.py:173
  53.5 6.4 %collective-permute-start.21 = (f32[32,1024]{1,0:T(8,128)S(1)}, f32[32,1024]{1,0:T(8,128)S(1)}, u32[]{:S(2)}, u32[]{:S(2)}) collective-permute-start(f32[32,1024]{1,0:T(8,128)S(1)} %add.87), channel_id=1, source_target_pairs={{0,128},{8,136},{16,144},{24,152},{32,160},{40,168},{48,176},{56,1... | collective-permute-start | bytes 393224 | tf_op jit(solution)/shard_map/ppermute | solution.py:173
  55.9 6.1 %collective-permute-start.11 = (f32[32,1024]{1,0:T(8,128)S(1)}, f32[32,1024]{1,0:T(8,128)S(1)}, u32[]{:S(2)}, u32[]{:S(2)}) collective-permute-start(f32[32,1024]{1,0:T(8,128)S(1)} %add.79), channel_id=1, source_target_pairs={{0,128},{8,136},{16,144},{24,152},{32,160},{40,168},{48,176},{56,1... | collective-permute-start | bytes 393224 | tf_op jit(solution)/shard_map/ppermute | solution.py:173
  57.2 8.1 %collective-permute-start.22 = (f32[32,1024]{1,0:T(8,128)S(1)}, f32[32,1024]{1,0:T(8,128)S(1)}, u32[]{:S(2)}, u32[]{:S(2)}) collective-permute-start(f32[32,1024]{1,0:T(8,128)S(1)} %add.87), channel_id=1, source_target_pairs={{0,16},{8,120},{16,0},{24,40},{32,48},{40,24},{48,32},{56,72},{64,... | collective-permute-start | bytes 393224 | tf_op jit(solution)/shard_map/ppermute | solution.py:173
  57.5 9.4 %collective-permute-start.12 = (f32[32,1024]{1,0:T(8,128)S(1)}, f32[32,1024]{1,0:T(8,128)S(1)}, u32[]{:S(2)}, u32[]{:S(2)}) collective-permute-start(f32[32,1024]{1,0:T(8,128)S(1)} %add.79), channel_id=1, source_target_pairs={{0,16},{8,120},{16,0},{24,40},{32,48},{40,24},{48,32},{56,72},{64,... | collective-permute-start | bytes 393224 | tf_op jit(solution)/shard_map/ppermute | solution.py:173
  59.9 5.5 %collective-permute-start.23 = (f32[32,1024]{1,0:T(8,128)S(1)}, f32[32,1024]{1,0:T(8,128)S(1)}, u32[]{:S(2)}, u32[]{:S(2)}) collective-permute-start(f32[32,1024]{1,0:T(8,128)S(1)} %collective-permute-done.21), channel_id=1, source_target_pairs={{0,16},{8,120},{16,0},{24,40},{32,48},{40,24},{48,32},{56,72},{64,... | collective-permute-start | bytes 393224 | tf_op jit(solution)/shard_map/ppermute | solution.py:173
  60.2 8.1 %collective-permute-start.24 = (f32[2,32,1024]{2,1,0:T(8,128)S(1)}, f32[2,32,1024]{2,1,0:T(8,128)S(1)}, u32[]{:S(2)}, u32[]{:S(2)}) collective-permute-start(f32[2,32,1024]{2,1,0:T(8,128)S(1)} %pad_maximum_fusion.2.refs_4_), channel_id=1, source_target_pairs={{0,8},{8,0},{16,24},{24,16},{32,40},{40,32},{48,56},{56,48},{64,72... | collective-permute-start | bytes 786440 | tf_op jit(solution)/shard_map/ppermute | solution.py:173
  62.0 5.7 %collective-permute-start.13 = (f32[32,1024]{1,0:T(8,128)S(1)}, f32[32,1024]{1,0:T(8,128)S(1)}, u32[]{:S(2)}, u32[]{:S(2)}) collective-permute-start(f32[32,1024]{1,0:T(8,128)S(1)} %collective-permute-done.11), channel_id=1, source_target_pairs={{0,16},{8,120},{16,0},{24,40},{32,48},{40,24},{48,32},{56,72},{64,... | collective-permute-start | bytes 393224 | tf_op jit(solution)/shard_map/ppermute | solution.py:173
  65.3 3.0 %collective-permute-start.14 = (f32[2,32,1024]{2,1,0:T(8,128)S(1)}, f32[2,32,1024]{2,1,0:T(8,128)S(1)}, u32[]{:S(2)}, u32[]{:S(2)}) collective-permute-start(f32[2,32,1024]{2,1,0:T(8,128)S(1)} %pad_maximum_fusion.refs_0_), channel_id=1, source_target_pairs={{0,8},{8,0},{16,24},{24,16},{32,40},{40,32},{48,56},{56,48},{64,72... | collective-permute-start | bytes 786440 | tf_op jit(solution)/shard_map/ppermute | solution.py:173
  (3 other events, 22.1 us)

commit v6 on v5

--- a/solution.py
+++ b/solution.py
@@ -79,13 +79,13 @@
             copy.wait()
         cols = columns(step)
         return total + lax.dot_general(
+            held_ref[:, cols],
             blocks_buf[:, cols].astype(jnp.bfloat16),
-            held_ref[:, cols],
             (((1,), (1,)), ((), ())),
             preferred_element_type=jnp.float32,
         )
 
-    out_ref[...] = lax.fori_loop(0, STEPS, add, jnp.zeros(out_ref.shape, jnp.float32))
+    out_ref[...] = lax.fori_loop(0, STEPS, add, jnp.zeros(out_ref.shape[::-1], jnp.float32)).T
 
 
 def predict(me, blocks, jacobian):

time: 71 us -> 71.1 us (level)
  no operation moved by 1% of the time
where the time goes in v6:
time: 71.1 us; the launch traced here: 71 us
  starting transfers between devices  38 us (53%)
  waiting for transfers between devices  23.7 us (33%)
  Pallas kernels  8.67 us (12%)
    ppermute x22, starting transfers between devices, swap(): return lax.ppermute(value, 'sens', pairs)  30.9 us
    ppermute x22, waiting for transfers between devices, swap(): return lax.ppermute(value, 'sens', pairs)  18.4 us
    ppermute x4, starting transfers between devices, flip(): return lax.ppermute(value, 'cand', [(c, c ^ bits) for c in range(N_CAND)])  7.14 us
    ppermute x4, waiting for transfers between devices, flip(): return lax.ppermute(value, 'cand', [(c, c ^ bits) for c in range(N_CAND)])  5.33 us
    pallas_call x1, Pallas kernels, predict(): pl.pallas_call(predict_kernel, in_specs=[SMEM, HBM, HBM], out_specs=[VMEM...  4.9 us
    pallas_call x8, Pallas kernels, product(): pl.pallas_call(kernel, in_specs=[SMEM, VMEM, VMEM] + [ANY] * len(after),...  2.3 us
    pallas_call x1, Pallas kernels, assemble(): pl.pallas_call(kernel, in_specs=[SMEM] + [VMEM] * len(operands), out_spec...  1.47 us
  transfers between devices with their start and end apart: 26, of which 12 were waited for; matrix products, arithmetic and copies ran while one was open for 0% of the time, Pallas kernels for 3%

profile of v6, /device:TPU:1, one launch (start us, length us, event | category | flops | bytes accessed | tf_op | source)
XLA Modules:
  0.0 71.0 jit_solution(103704000110765264)
XLA Ops:
  0.0 4.9 %shard_map.37 = (f32[32,256]{1,0:T(8,128)S(1)}, bf16[256,16384]{1,0:T(8,128)(2,1)S(1)}) custom-call(s32[1]{0:T(128)} %bitcast.me_ref, f32[32,16384]{1,0:T(8,128)} %bitcast.27, bf16[256,16384]{1,0:T(8,128)(2,1)} %jac_ref.1), custom_call_target="tpu_custom_call" | custom-call | flops 268435456 | bytes 8388608 | tf_op jit(solution)/shard_map/pallas_call | solution.py:94
  4.9 3.8 %collective-permute-start.2 = (f32[32,256]{1,0:T(8,128)S(1)}, f32[32,256]{1,0:T(8,128)S(1)}, u32[]{:S(2)}, u32[]{:S(2)}) collective-permute-start(f32[32,256]{1,0:T(8,128)S(1)} %get-tuple-element.7), channel_id=1, source_target_pairs={{0,2},{1,3},{2,0},{3,1},{4,6},{5,7},{6,4},{7,5},{8,10},{9,11},{10,... | collective-permute-start | bytes 98312 | tf_op jit(solution)/shard_map/ppermute | solution.py:177
  10.0 3.0 %collective-permute-done.1 = f32[32,256]{1,0:T(8,128)S(1)} collective-permute-done((f32[32,256]{1,0:T(8,128)S(1)}, f32[32,256]{1,0:T(8,128)S(1)}, u32[]{:S(2)}, u32[]{:S(2)}) %collective-permute-start.1) | collective-permute-done | bytes 32800 | tf_op jit(solution)/shard_map/ppermute | solution.py:177
  13.0 2.5 %collective-permute-start.3 = (f32[32,256]{1,0:T(8,128)S(1)}, f32[32,256]{1,0:T(8,128)S(1)}, u32[]{:S(2)}, u32[]{:S(2)}) collective-permute-start(f32[32,256]{1,0:T(8,128)S(1)} %add_add_fusion), channel_id=1, source_target_pairs={{0,4},{1,5},{2,6},{3,7},{4,0},{5,1},{6,2},{7,3},{8,12},{9,13},{10,... | collective-permute-start | bytes 98312 | tf_op jit(solution)/shard_map/ppermute | solution.py:177
  15.6 1.8 %collective-permute-done.3 = f32[32,256]{1,0:T(8,128)S(1)} collective-permute-done((f32[32,256]{1,0:T(8,128)S(1)}, f32[32,256]{1,0:T(8,128)S(1)}, u32[]{:S(2)}, u32[]{:S(2)}) %collective-permute-start.3) | collective-permute-done | bytes 32800 | tf_op jit(solution)/shard_map/ppermute | solution.py:177
  17.7 3.0 %collective-permute-start.4 = (f32[2,32,1024]{2,1,0:T(8,128)S(1)}, f32[2,32,1024]{2,1,0:T(8,128)S(1)}, u32[]{:S(2)}, u32[]{:S(2)}) collective-permute-start(f32[2,32,1024]{2,1,0:T(8,128)S(1)} %shard_map.38), channel_id=1, source_target_pairs={{0,8},{8,0},{16,24},{24,16},{32,40},{40,32},{48,56},{56,48},{64,72... | collective-permute-start | bytes 786440 | tf_op jit(solution)/shard_map/ppermute | solution.py:173
  22.6 5.6 %collective-permute-start.17 = (f32[2,32,1024]{2,1,0:T(8,128)S(1)}, f32[2,32,1024]{2,1,0:T(8,128)S(1)}, u32[]{:S(2)}, u32[]{:S(2)}) collective-permute-start(f32[2,32,1024]{2,1,0:T(8,128)S(1)} %add.70.refs_0_), channel_id=1, source_target_pairs={{0,16},{8,120},{16,0},{24,40},{32,48},{40,24},{48,32},{56,72},{64,... | collective-permute-start | bytes 786440 | tf_op jit(solution)/shard_map/ppermute | solution.py:173
  28.9 1.2 %collective-permute-start.7 = (f32[2,32,1024]{2,1,0:T(8,128)S(1)}, f32[2,32,1024]{2,1,0:T(8,128)S(1)}, u32[]{:S(2)}, u32[]{:S(2)}) collective-permute-start(f32[2,32,1024]{2,1,0:T(8,128)S(1)} %add.72), channel_id=1, source_target_pairs={{0,16},{8,120},{16,0},{24,40},{32,48},{40,24},{48,32},{56,72},{64,... | collective-permute-start | bytes 786440 | tf_op jit(solution)/shard_map/ppermute | solution.py:173
  30.7 1.2 %collective-permute-done.17 = f32[2,32,1024]{2,1,0:T(8,128)S(1)} collective-permute-done((f32[2,32,1024]{2,1,0:T(8,128)S(1)}, f32[2,32,1024]{2,1,0:T(8,128)S(1)}, u32[]{:S(2)}, u32[]{:S(2)}) %collective-permute-start.17) | collective-permute-done | bytes 262176 | tf_op jit(solution)/shard_map/ppermute | solution.py:173
  32.0 1.3 %collective-permute-start.18 = (f32[32,1024]{1,0:T(8,128)S(1)}, f32[32,1024]{1,0:T(8,128)S(1)}, u32[]{:S(2)}, u32[]{:S(2)}) collective-permute-start(f32[32,1024]{1,0:T(8,128)S(1)} %fusion), channel_id=1, source_target_pairs={{0,128},{8,136},{16,144},{24,152},{32,160},{40,168},{48,176},{56,1... | collective-permute-start | bytes 393224 | tf_op jit(solution)/shard_map/ppermute | solution.py:173
  33.3 2.1 %collective-permute-done.7 = f32[2,32,1024]{2,1,0:T(8,128)S(1)} collective-permute-done((f32[2,32,1024]{2,1,0:T(8,128)S(1)}, f32[2,32,1024]{2,1,0:T(8,128)S(1)}, u32[]{:S(2)}, u32[]{:S(2)}) %collective-permute-start.7) | collective-permute-done | bytes 262176 | tf_op jit(solution)/shard_map/ppermute | solution.py:173
  35.5 1.3 %collective-permute-start.8 = (f32[32,1024]{1,0:T(8,128)S(1)}, f32[32,1024]{1,0:T(8,128)S(1)}, u32[]{:S(2)}, u32[]{:S(2)}) collective-permute-start(f32[32,1024]{1,0:T(8,128)S(1)} %fusion.3), channel_id=1, source_target_pairs={{0,128},{8,136},{16,144},{24,152},{32,160},{40,168},{48,176},{56,1... | collective-permute-start | bytes 393224 | tf_op jit(solution)/shard_map/ppermute | solution.py:173
  36.9 3.3 %collective-permute-done.8 = f32[32,1024]{1,0:T(8,128)S(1)} collective-permute-done((f32[32,1024]{1,0:T(8,128)S(1)}, f32[32,1024]{1,0:T(8,128)S(1)}, u32[]{:S(2)}, u32[]{:S(2)}) %collective-permute-start.8) | collective-permute-done | bytes 131104 | tf_op jit(solution)/shard_map/ppermute | solution.py:173
  40.2 1.4 %collective-permute-start.9 = (f32[32,1024]{1,0:T(8,128)S(1)}, f32[32,1024]{1,0:T(8,128)S(1)}, u32[]{:S(2)}, u32[]{:S(2)}) collective-permute-start(f32[32,1024]{1,0:T(8,128)S(1)} %fusion.5), channel_id=1, source_target_pairs={{0,48},{8,88},{16,96},{24,72},{32,80},{40,120},{48,0},{56,104},{64... | collective-permute-start | bytes 393224 | tf_op jit(solution)/shard_map/ppermute | solution.py:173
  41.7 3.2 %collective-permute-start.20 = (f32[32,1024]{1,0:T(8,128)S(1)}, f32[32,1024]{1,0:T(8,128)S(1)}, u32[]{:S(2)}, u32[]{:S(2)}) collective-permute-start(f32[32,1024]{1,0:T(8,128)S(1)} %add.86), channel_id=1, source_target_pairs={{0,48},{8,88},{16,96},{24,72},{32,80},{40,120},{48,0},{56,104},{64... | collective-permute-start | bytes 393224 | tf_op jit(solution)/shard_map/ppermute | solution.py:173
  44.9 4.3 %collective-permute-done.9 = f32[32,1024]{1,0:T(8,128)S(1)} collective-permute-done((f32[32,1024]{1,0:T(8,128)S(1)}, f32[32,1024]{1,0:T(8,128)S(1)}, u32[]{:S(2)}, u32[]{:S(2)}) %collective-permute-start.9) | collective-permute-done | bytes 131104 | tf_op jit(solution)/shard_map/ppermute | solution.py:173
  49.3 4.1 %collective-permute-done.20 = f32[32,1024]{1,0:T(8,128)S(1)} collective-permute-done((f32[32,1024]{1,0:T(8,128)S(1)}, f32[32,1024]{1,0:T(8,128)S(1)}, u32[]{:S(2)}, u32[]{:S(2)}) %collective-permute-start.20) | collective-permute-done | bytes 131104 | tf_op jit(solution)/shard_map/ppermute | solution.py:173
  53.5 1.3 %collective-permute-start.21 = (f32[32,1024]{1,0:T(8,128)S(1)}, f32[32,1024]{1,0:T(8,128)S(1)}, u32[]{:S(2)}, u32[]{:S(2)}) collective-permute-start(f32[32,1024]{1,0:T(8,128)S(1)} %add.87), channel_id=1, source_target_pairs={{0,128},{8,136},{16,144},{24,152},{32,160},{40,168},{48,176},{56,1... | collective-permute-start | bytes 393224 | tf_op jit(solution)/shard_map/ppermute | solution.py:173
  55.9 1.3 %collective-permute-start.11 = (f32[32,1024]{1,0:T(8,128)S(1)}, f32[32,1024]{1,0:T(8,128)S(1)}, u32[]{:S(2)}, u32[]{:S(2)}) collective-permute-start(f32[32,1024]{1,0:T(8,128)S(1)} %add.79), channel_id=1, source_target_pairs={{0,128},{8,136},{16,144},{24,152},{32,160},{40,168},{48,176},{56,1... | collective-permute-start | bytes 393224 | tf_op jit(solution)/shard_map/ppermute | solution.py:173
  57.6 2.3 %collective-permute-start.12 = (f32[32,1024]{1,0:T(8,128)S(1)}, f32[32,1024]{1,0:T(8,128)S(1)}, u32[]{:S(2)}, u32[]{:S(2)}) collective-permute-start(f32[32,1024]{1,0:T(8,128)S(1)} %add.79), channel_id=1, source_target_pairs={{0,16},{8,120},{16,0},{24,40},{32,48},{40,24},{48,32},{56,72},{64,... | collective-permute-start | bytes 393224 | tf_op jit(solution)/shard_map/ppermute | solution.py:173
  60.3 1.7 %collective-permute-start.24 = (f32[2,32,1024]{2,1,0:T(8,128)S(1)}, f32[2,32,1024]{2,1,0:T(8,128)S(1)}, u32[]{:S(2)}, u32[]{:S(2)}) collective-permute-start(f32[2,32,1024]{2,1,0:T(8,128)S(1)} %pad_maximum_fusion.2.refs_4_), channel_id=1, source_target_pairs={{0,8},{8,0},{16,24},{24,16},{32,40},{40,32},{48,56},{56,48},{64,72... | collective-permute-start | bytes 786440 | tf_op jit(solution)/shard_map/ppermute | solution.py:173
  62.0 3.1 %collective-permute-start.13 = (f32[32,1024]{1,0:T(8,128)S(1)}, f32[32,1024]{1,0:T(8,128)S(1)}, u32[]{:S(2)}, u32[]{:S(2)}) collective-permute-start(f32[32,1024]{1,0:T(8,128)S(1)} %collective-permute-done.11), channel_id=1, source_target_pairs={{0,16},{8,120},{16,0},{24,40},{32,48},{40,24},{48,32},{56,72},{64,... | collective-permute-start | bytes 393224 | tf_op jit(solution)/shard_map/ppermute | solution.py:173
  65.2 1.7 %collective-permute-start.25 = (f32[2,32,1024]{2,1,0:T(8,128)S(1)}, f32[2,32,1024]{2,1,0:T(8,128)S(1)}, u32[]{:S(2)}, u32[]{:S(2)}) collective-permute-start(f32[2,32,1024]{2,1,0:T(8,128)S(1)} %pad_maximum_fusion.3.refs_5_), channel_id=1, source_target_pairs={{0,8},{8,0},{16,24},{24,16},{32,40},{40,32},{48,56},{56,48},{64,72... | collective-permute-start | bytes 786440 | tf_op jit(solution)/shard_map/ppermute | solution.py:173
  69.5 1.5 %shard_map.46 = f32[32,16384]{1,0:T(8,128)} custom-call(s32[1]{0:T(128)} %bitcast.me_ref, f32[2,32,1024]{2,1,0:T(8,128)S(1)} %pad_maximum_fusion.refs_0_, f32[2,32,1024]{2,1,0:T(8,128)S(1)} %pad_maximum_fusion.1.refs_1_, f32[2,32,1024]{2,1,0:T(8,128)S(1)} %collective-permute-done.14.refs_2_, f32[2,32,1024]{2,1,0:T(8,128)S(1)} %collective-permute-done.15.refs_3_, ...), custom_call_target="tpu_custom_call" | custom-call | tf_op jit(solution)/shard_map/pallas_call | solution.py:159
  (58 shorter events, 9.8 us)
Async XLA Ops:
  4.9 5.1 %collective-permute-start.2 = (f32[32,256]{1,0:T(8,128)S(1)}, f32[32,256]{1,0:T(8,128)S(1)}, u32[]{:S(2)}, u32[]{:S(2)}) collective-permute-start(f32[32,256]{1,0:T(8,128)S(1)} %get-tuple-element.7), channel_id=1, source_target_pairs={{0,2},{1,3},{2,0},{3,1},{4,6},{5,7},{6,4},{7,5},{8,10},{9,11},{10,... | collective-permute-start | bytes 98312 | tf_op jit(solution)/shard_map/ppermute | solution.py:177
  8.7 4.3 %collective-permute-start.1 = (f32[32,256]{1,0:T(8,128)S(1)}, f32[32,256]{1,0:T(8,128)S(1)}, u32[]{:S(2)}, u32[]{:S(2)}) collective-permute-start(f32[32,256]{1,0:T(8,128)S(1)} %get-tuple-element.7), channel_id=1, source_target_pairs={{0,3},{1,2},{2,1},{3,0},{4,7},{5,6},{6,5},{7,4},{8,11},{9,10},{10,... | collective-permute-start | bytes 98312 | tf_op jit(solution)/shard_map/ppermute | solution.py:177
  9.5 3.5 %collective-permute-start = (f32[32,256]{1,0:T(8,128)S(1)}, f32[32,256]{1,0:T(8,128)S(1)}, u32[]{:S(2)}, u32[]{:S(2)}) collective-permute-start(f32[32,256]{1,0:T(8,128)S(1)} %get-tuple-element.7), channel_id=1, source_target_pairs={{0,1},{1,0},{2,3},{3,2},{4,5},{5,4},{6,7},{7,6},{8,9},{9,8},{10,11... | collective-permute-start | bytes 98312 | tf_op jit(solution)/shard_map/ppermute | solution.py:177
  13.0 4.4 %collective-permute-start.3 = (f32[32,256]{1,0:T(8,128)S(1)}, f32[32,256]{1,0:T(8,128)S(1)}, u32[]{:S(2)}, u32[]{:S(2)}) collective-permute-start(f32[32,256]{1,0:T(8,128)S(1)} %add_add_fusion), channel_id=1, source_target_pairs={{0,4},{1,5},{2,6},{3,7},{4,0},{5,1},{6,2},{7,3},{8,12},{9,13},{10,... | collective-permute-start | bytes 98312 | tf_op jit(solution)/shard_map/ppermute | solution.py:177
  17.7 4.2 %collective-permute-start.4 = (f32[2,32,1024]{2,1,0:T(8,128)S(1)}, f32[2,32,1024]{2,1,0:T(8,128)S(1)}, u32[]{:S(2)}, u32[]{:S(2)}) collective-permute-start(f32[2,32,1024]{2,1,0:T(8,128)S(1)} %shard_map.38), channel_id=1, source_target_pairs={{0,8},{8,0},{16,24},{24,16},{32,40},{40,32},{48,56},{56,48},{64,72... | collective-permute-start | bytes 786440 | tf_op jit(solution)/shard_map/ppermute | solution.py:173
  21.0 7.9 %collective-permute-start.6 = (f32[2,32,1024]{2,1,0:T(8,128)S(1)}, f32[2,32,1024]{2,1,0:T(8,128)S(1)}, u32[]{:S(2)}, u32[]{:S(2)}) collective-permute-start(f32[2,32,1024]{2,1,0:T(8,128)S(1)} %shard_map.42), channel_id=1, source_target_pairs={{0,8},{8,0},{16,24},{24,16},{32,40},{40,32},{48,56},{56,48},{64,72... | collective-permute-start | bytes 786440 | tf_op jit(solution)/shard_map/ppermute | solution.py:173
  22.2 8.5 %collective-permute-start.16 = (f32[2,32,1024]{2,1,0:T(8,128)S(1)}, f32[2,32,1024]{2,1,0:T(8,128)S(1)}, u32[]{:S(2)}, u32[]{:S(2)}) collective-permute-start(f32[2,32,1024]{2,1,0:T(8,128)S(1)} %shard_map.44), channel_id=1, source_target_pairs={{0,8},{8,0},{16,24},{24,16},{32,40},{40,32},{48,56},{56,48},{64,72... | collective-permute-start | bytes 786440 | tf_op jit(solution)/shard_map/ppermute | solution.py:173
  22.6 9.3 %collective-permute-start.17 = (f32[2,32,1024]{2,1,0:T(8,128)S(1)}, f32[2,32,1024]{2,1,0:T(8,128)S(1)}, u32[]{:S(2)}, u32[]{:S(2)}) collective-permute-start(f32[2,32,1024]{2,1,0:T(8,128)S(1)} %add.70.refs_0_), channel_id=1, source_target_pairs={{0,16},{8,120},{16,0},{24,40},{32,48},{40,24},{48,32},{56,72},{64,... | collective-permute-start | bytes 786440 | tf_op jit(solution)/shard_map/ppermute | solution.py:173
  28.8 4.5 %collective-permute-start.5 = (f32[2,32,1024]{2,1,0:T(8,128)S(1)}, f32[2,32,1024]{2,1,0:T(8,128)S(1)}, u32[]{:S(2)}, u32[]{:S(2)}) collective-permute-start(f32[2,32,1024]{2,1,0:T(8,128)S(1)} %shard_map.40), channel_id=1, source_target_pairs={{0,8},{8,0},{16,24},{24,16},{32,40},{40,32},{48,56},{56,48},{64,72... | collective-permute-start | bytes 786440 | tf_op jit(solution)/shard_map/ppermute | solution.py:173
  28.9 6.5 %collective-permute-start.7 = (f32[2,32,1024]{2,1,0:T(8,128)S(1)}, f32[2,32,1024]{2,1,0:T(8,128)S(1)}, u32[]{:S(2)}, u32[]{:S(2)}) collective-permute-start(f32[2,32,1024]{2,1,0:T(8,128)S(1)} %add.72), channel_id=1, source_target_pairs={{0,16},{8,120},{16,0},{24,40},{32,48},{40,24},{48,32},{56,72},{64,... | collective-permute-start | bytes 786440 | tf_op jit(solution)/shard_map/ppermute | solution.py:173
  32.0 4.8 %collective-permute-start.18 = (f32[32,1024]{1,0:T(8,128)S(1)}, f32[32,1024]{1,0:T(8,128)S(1)}, u32[]{:S(2)}, u32[]{:S(2)}) collective-permute-start(f32[32,1024]{1,0:T(8,128)S(1)} %fusion), channel_id=1, source_target_pairs={{0,128},{8,136},{16,144},{24,152},{32,160},{40,168},{48,176},{56,1... | collective-permute-start | bytes 393224 | tf_op jit(solution)/shard_map/ppermute | solution.py:173
  35.5 4.7 %collective-permute-start.8 = (f32[32,1024]{1,0:T(8,128)S(1)}, f32[32,1024]{1,0:T(8,128)S(1)}, u32[]{:S(2)}, u32[]{:S(2)}) collective-permute-start(f32[32,1024]{1,0:T(8,128)S(1)} %fusion.3), channel_id=1, source_target_pairs={{0,128},{8,136},{16,144},{24,152},{32,160},{40,168},{48,176},{56,1... | collective-permute-start | bytes 393224 | tf_op jit(solution)/shard_map/ppermute | solution.py:173
  36.8 4.9 %collective-permute-start.19 = (f32[32,1024]{1,0:T(8,128)S(1)}, f32[32,1024]{1,0:T(8,128)S(1)}, u32[]{:S(2)}, u32[]{:S(2)}) collective-permute-start(f32[32,1024]{1,0:T(8,128)S(1)} %fusion.2), channel_id=1, source_target_pairs={{0,112},{8,24},{16,32},{24,8},{32,16},{40,56},{48,64},{56,40},{64,... | collective-permute-start | bytes 393224 | tf_op jit(solution)/shard_map/ppermute | solution.py:173
  40.2 9.0 %collective-permute-start.9 = (f32[32,1024]{1,0:T(8,128)S(1)}, f32[32,1024]{1,0:T(8,128)S(1)}, u32[]{:S(2)}, u32[]{:S(2)}) collective-permute-start(f32[32,1024]{1,0:T(8,128)S(1)} %fusion.5), channel_id=1, source_target_pairs={{0,48},{8,88},{16,96},{24,72},{32,80},{40,120},{48,0},{56,104},{64... | collective-permute-start | bytes 393224 | tf_op jit(solution)/shard_map/ppermute | solution.py:173
  41.7 11.8 %collective-permute-start.20 = (f32[32,1024]{1,0:T(8,128)S(1)}, f32[32,1024]{1,0:T(8,128)S(1)}, u32[]{:S(2)}, u32[]{:S(2)}) collective-permute-start(f32[32,1024]{1,0:T(8,128)S(1)} %add.86), channel_id=1, source_target_pairs={{0,48},{8,88},{16,96},{24,72},{32,80},{40,120},{48,0},{56,104},{64... | collective-permute-start | bytes 393224 | tf_op jit(solution)/shard_map/ppermute | solution.py:173
  49.2 6.6 %collective-permute-start.10 = (f32[32,1024]{1,0:T(8,128)S(1)}, f32[32,1024]{1,0:T(8,128)S(1)}, u32[]{:S(2)}, u32[]{:S(2)}) collective-permute-start(f32[32,1024]{1,0:T(8,128)S(1)} %add.78), channel_id=1, source_target_pairs={{0,112},{8,24},{16,32},{24,8},{32,16},{40,56},{48,64},{56,40},{64,... | collective-permute-start | bytes 393224 | tf_op jit(solution)/shard_map/ppermute | solution.py:173
  53.5 6.4 %collective-permute-start.21 = (f32[32,1024]{1,0:T(8,128)S(1)}, f32[32,1024]{1,0:T(8,128)S(1)}, u32[]{:S(2)}, u32[]{:S(2)}) collective-permute-start(f32[32,1024]{1,0:T(8,128)S(1)} %add.87), channel_id=1, source_target_pairs={{0,128},{8,136},{16,144},{24,152},{32,160},{40,168},{48,176},{56,1... | collective-permute-start | bytes 393224 | tf_op jit(solution)/shard_map/ppermute | solution.py:173
  55.9 6.1 %collective-permute-start.11 = (f32[32,1024]{1,0:T(8,128)S(1)}, f32[32,1024]{1,0:T(8,128)S(1)}, u32[]{:S(2)}, u32[]{:S(2)}) collective-permute-start(f32[32,1024]{1,0:T(8,128)S(1)} %add.79), channel_id=1, source_target_pairs={{0,128},{8,136},{16,144},{24,152},{32,160},{40,168},{48,176},{56,1... | collective-permute-start | bytes 393224 | tf_op jit(solution)/shard_map/ppermute | solution.py:173
  57.2 7.9 %collective-permute-start.22 = (f32[32,1024]{1,0:T(8,128)S(1)}, f32[32,1024]{1,0:T(8,128)S(1)}, u32[]{:S(2)}, u32[]{:S(2)}) collective-permute-start(f32[32,1024]{1,0:T(8,128)S(1)} %add.87), channel_id=1, source_target_pairs={{0,16},{8,120},{16,0},{24,40},{32,48},{40,24},{48,32},{56,72},{64,... | collective-permute-start | bytes 393224 | tf_op jit(solution)/shard_map/ppermute | solution.py:173
  57.6 9.3 %collective-permute-start.12 = (f32[32,1024]{1,0:T(8,128)S(1)}, f32[32,1024]{1,0:T(8,128)S(1)}, u32[]{:S(2)}, u32[]{:S(2)}) collective-permute-start(f32[32,1024]{1,0:T(8,128)S(1)} %add.79), channel_id=1, source_target_pairs={{0,16},{8,120},{16,0},{24,40},{32,48},{40,24},{48,32},{56,72},{64,... | collective-permute-start | bytes 393224 | tf_op jit(solution)/shard_map/ppermute | solution.py:173
  59.9 5.3 %collective-permute-start.23 = (f32[32,1024]{1,0:T(8,128)S(1)}, f32[32,1024]{1,0:T(8,128)S(1)}, u32[]{:S(2)}, u32[]{:S(2)}) collective-permute-start(f32[32,1024]{1,0:T(8,128)S(1)} %collective-permute-done.21), channel_id=1, source_target_pairs={{0,16},{8,120},{16,0},{24,40},{32,48},{40,24},{48,32},{56,72},{64,... | collective-permute-start | bytes 393224 | tf_op jit(solution)/shard_map/ppermute | solution.py:173
  60.3 8.1 %collective-permute-start.24 = (f32[2,32,1024]{2,1,0:T(8,128)S(1)}, f32[2,32,1024]{2,1,0:T(8,128)S(1)}, u32[]{:S(2)}, u32[]{:S(2)}) collective-permute-start(f32[2,32,1024]{2,1,0:T(8,128)S(1)} %pad_maximum_fusion.2.refs_4_), channel_id=1, source_target_pairs={{0,8},{8,0},{16,24},{24,16},{32,40},{40,32},{48,56},{56,48},{64,72... | collective-permute-start | bytes 786440 | tf_op jit(solution)/shard_map/ppermute | solution.py:173
  62.0 5.5 %collective-permute-start.13 = (f32[32,1024]{1,0:T(8,128)S(1)}, f32[32,1024]{1,0:T(8,128)S(1)}, u32[]{:S(2)}, u32[]{:S(2)}) collective-permute-start(f32[32,1024]{1,0:T(8,128)S(1)} %collective-permute-done.11), channel_id=1, source_target_pairs={{0,16},{8,120},{16,0},{24,40},{32,48},{40,24},{48,32},{56,72},{64,... | collective-permute-start | bytes 393224 | tf_op jit(solution)/shard_map/ppermute | solution.py:173
  65.1 3.3 %collective-permute-start.14 = (f32[2,32,1024]{2,1,0:T(8,128)S(1)}, f32[2,32,1024]{2,1,0:T(8,128)S(1)}, u32[]{:S(2)}, u32[]{:S(2)}) collective-permute-start(f32[2,32,1024]{2,1,0:T(8,128)S(1)} %pad_maximum_fusion.refs_0_), channel_id=1, source_target_pairs={{0,8},{8,0},{16,24},{24,16},{32,40},{40,32},{48,56},{56,48},{64,72... | collective-permute-start | bytes 786440 | tf_op jit(solution)/shard_map/ppermute | solution.py:173
  (3 other events, 22.6 us)
